TPU v7x, 256 devices: a whole 4x4x8 slice. The times are simulated.
256 devices in a mesh: layer: 32 (over x_hi, z, core), row: 8 (over x_lo, y).
Axes of the slice: x: 4 (x_hi: 2, x_lo: 2; x = x_hi * 2 + x_lo), y: 4, z: 8, core: 2. Of those that a mesh axis runs over, the one named last changes fastest.
Arguments:
- waves: bfloat16 [32, 3072, 512], P('layer', 'row'), may hold values from -6 to 6
- operators: bfloat16 [32, 4, 3072, 3072], P('layer', None, 'row'), may hold values from -0.0546875 to 0.0546875
- sources: bfloat16 [3072, 512], P('row'), may hold values from -6 to 6
- source_layer: int32 [128], replicated, may hold values from 0 to 31
Outputs:
- traces: bfloat16 [32, 3072, 512], P('layer', 'row')
All inputs are finite; a program needn't handle non-finite values.
Results may differ from a plain program's by a relative error of at most 0.0057.
Values may be sent and summed in bfloat16 or wider, within the bound.
No kernel may reach another device: no remote copies, remote signals or barrier semaphores. Data moves between devices by JAX's collectives and lax.ppermute only.
A program may use at most 64 MiB of HBM per device.

v0:
```python
import jax
import jax.numpy as jnp
from jax import lax
from jax.sharding import PartitionSpec as P

TICKS = 3


def shifted(array, axis, by):
    peers = lax.axis_size(axis)
    pairs = [(i, i + by) for i in range(peers) if 0 <= i + by < peers]
    return lax.ppermute(array, axis, pairs)


def combine(real_prod, imag_prod, shot_count):
    real_part = real_prod[:, :shot_count] - imag_prod[:, shot_count:]
    imag_part = real_prod[:, shot_count:] + imag_prod[:, :shot_count]
    return jnp.concatenate([real_part, imag_part], axis=1)


def per_device(waves, operators, sources, source_layer):
    tile_rows = operators.shape[2]
    full_rows = operators.shape[3]
    column_count = waves.shape[2]
    shot_count = column_count // 4
    half = 2 * shot_count
    stacked = operators[0].reshape(4 * tile_rows, full_rows)
    layer_id = lax.axis_index("layer")
    shot_mask = jnp.tile((source_layer == layer_id).astype(jnp.float32), 4)
    source_term = sources.astype(jnp.float32) * shot_mask[None, :]
    current = waves[0]
    for sweep_tick in range(TICKS):
        products = jnp.dot(
            stacked,
            lax.all_gather(current, "row", axis=0, tiled=True),
            preferred_element_type=jnp.float32,
        )
        products = products.reshape(4, tile_rows, column_count)
        down_out = combine(products[0][:, :half], products[1][:, :half], shot_count) + combine(
            products[2][:, half:], products[3][:, half:], shot_count
        )
        up_out = combine(products[0][:, half:], products[1][:, half:], shot_count) + combine(
            products[2][:, :half], products[3][:, :half], shot_count
        )
        down_out = (down_out + source_term[:, :half]).astype(jnp.bfloat16)
        up_out = (up_out + source_term[:, half:]).astype(jnp.bfloat16)
        down_next = shifted(down_out, "layer", 1)
        up_next = shifted(up_out, "layer", -1)
        current = jnp.concatenate([down_next, up_next], axis=1)
    return current[None]


def solution(mesh):
    return jax.shard_map(
        per_device,
        mesh=mesh,
        in_specs=(P("layer", "row", None), P("layer", None, "row", None), P("row", None), P()),
        out_specs=P("layer", "row", None),
        check_vma=False,
    )
```

profile of v0, /device:TPU:6, one launch (start us, length us, event | category | flops | bytes accessed | tf_op | source)
XLA Modules:
  0.0 220.6 jit_solution(12235580169698713619)
XLA Ops:
  6.5 0.7 all-gather.9.cloned.1.call-update
  7.3 1.2 copy.5
  8.5 0.7 compare_convert_fusion
  9.2 0.1 convert_multiply_fusion
  9.3 48.8 %all-gather.9.cloned.1.call-done = bf16[1,3072,512]{2,1,0:T(8,128)(2,1)} async-done(((bf16[1,384,512]{2,1,0:T(8,128)(2,1)}), bf16[1,3072,512]{2,1,0:T(8,128)(2,1)}) %all-gather.9.cloned.1.call-update) | async-done | bytes 3145744 | tf_op jit(solution)/shard_map/all_gather | solution.py:35
  58.2 8.7 %fusion = f32[1536,512]{0,1:T(8,128)S(1)} fusion(bf16[1536,3072]{1,0:T(8,128)(2,1)} %bitcast.17, bf16[1,3072,512]{2,1,0:T(8,128)(2,1)} %all-gather.9.cloned.1.call-done), kind=kOutput, calls=%fused_computation.2 | convolution fusion | flops 4831838208 | bytes 15728640 | tf_op jit(solution)/shard_map/dot_general | solution.py:33
  66.9 0.2 slice_subtract_fusion.10
  67.0 0.1 fusion.3
  67.2 1.9 collective-permute-start
  69.1 7.3 %collective-permute-start.1 = (bf16[384,256]{0,1:T(8,128)(2,1)S(1)}, bf16[384,256]{0,1:T(8,128)(2,1)S(1)}, u32[]{:S(2)}, u32[]{:S(2)}) collective-permute-start(bf16[384,256]{0,1:T(8,128)(2,1)S(1)} %get-tuple-element.34), channel_id=1, source_target_pairs={{8,0},{16,8},{24,16},{32,24},{40,32},{48,40},{56,48},{64,56},{72,6... | collective-permute-start | bytes 589832 | tf_op jit(solution)/shard_map/ppermute | solution.py:12
  76.4 1.4 collective-permute-done
  77.8 1.8 collective-permute-done.1
  79.6 0.8 pad_maximum_fusion
  80.4 0.0 all-gather.7.cloned.1.call-start
  80.4 44.7 %all-gather.5.cloned.1.call-done = bf16[3072,512]{0,1:T(8,128)(2,1)} async-done(((bf16[384,512]{0,1:T(8,128)(2,1)}), bf16[3072,512]{0,1:T(8,128)(2,1)}) %all-gather.5.cloned.1.call-update) | async-done | bytes 3145744 | tf_op jit(solution)/shard_map/all_gather | solution.py:35
  125.2 8.6 %convolution_bitcast_fusion.1 = f32[1536,512]{0,1:T(8,128)S(1)} fusion(bf16[3072,512]{0,1:T(8,128)(2,1)} %all-gather.5.cloned.1.call-done, bf16[1536,3072]{1,0:T(8,128)(2,1)} %bitcast.18), kind=kOutput, calls=%fused_computation.1 | convolution fusion | flops 4831838208 | bytes 15728640 | tf_op jit(solution)/shard_map/dot_general | solution.py:33
  133.8 0.2 slice_subtract_fusion.6
  134.0 0.1 fusion.7
  134.1 1.9 collective-permute-start.2
  136.0 7.3 %collective-permute-start.3 = (bf16[384,256]{0,1:T(8,128)(2,1)S(1)}, bf16[384,256]{0,1:T(8,128)(2,1)S(1)}, u32[]{:S(2)}, u32[]{:S(2)}) collective-permute-start(bf16[384,256]{0,1:T(8,128)(2,1)S(1)} %get-tuple-element.32), channel_id=1, source_target_pairs={{8,0},{16,8},{24,16},{32,24},{40,32},{48,40},{56,48},{64,56},{72,6... | collective-permute-start | bytes 589832 | tf_op jit(solution)/shard_map/ppermute | solution.py:12
  143.3 1.4 collective-permute-done.2
  144.7 1.8 collective-permute-done.3
  146.5 0.8 pad_maximum_fusion.1
  147.3 44.4 %all-gather.7.cloned.1.call-done = bf16[3072,512]{0,1:T(8,128)(2,1)} async-done(((bf16[384,512]{0,1:T(8,128)(2,1)}), bf16[3072,512]{0,1:T(8,128)(2,1)}) %all-gather.7.cloned.1.call-update) | async-done | bytes 3145744 | tf_op jit(solution)/shard_map/all_gather | solution.py:35
  191.7 8.6 %convolution_bitcast_fusion = f32[1536,512]{0,1:T(8,128)S(1)} fusion(bf16[3072,512]{0,1:T(8,128)(2,1)} %all-gather.7.cloned.1.call-done, bf16[1536,3072]{1,0:T(8,128)(2,1)} %bitcast.19), kind=kOutput, calls=%fused_computation | convolution fusion | flops 4831838208 | bytes 15728640 | tf_op jit(solution)/shard_map/dot_general | solution.py:33
  200.4 0.2 slice_subtract_fusion.2
  200.6 0.1 fusion.11
  200.7 1.9 collective-permute-start.4
  202.6 7.3 %collective-permute-start.5 = (bf16[384,256]{0,1:T(8,128)(2,1)S(1)}, bf16[384,256]{0,1:T(8,128)(2,1)S(1)}, u32[]{:S(2)}, u32[]{:S(2)}) collective-permute-start(bf16[384,256]{0,1:T(8,128)(2,1)S(1)} %get-tuple-element.30), channel_id=1, source_target_pairs={{8,0},{16,8},{24,16},{32,24},{40,32},{48,40},{56,48},{64,56},{72,6... | collective-permute-start | bytes 589832 | tf_op jit(solution)/shard_map/ppermute | solution.py:12
  209.9 1.4 collective-permute-done.4
  211.3 1.8 collective-permute-done.5
  213.1 0.9 copy.6
  (6 shorter events, 0.1 us)
Async XLA Ops:
  6.5 51.6 %all-gather.9.cloned.1.call-start = ((), (), s32[]{:S(2)}) async-start(), calls=%async_computation.2 | async-start | bytes 3538944 | tf_op jit(solution)/shard_map/all_gather | solution.py:35
  7.3 117.9 %all-gather.5.cloned.1.call-start = ((), (), s32[]{:S(2)}) async-start(), calls=%async_computation | async-start | bytes 3538944 | tf_op jit(solution)/shard_map/all_gather | solution.py:35
  67.2 10.6 %collective-permute-start = (bf16[384,256]{0,1:T(8,128)(2,1)S(1)}, bf16[384,256]{0,1:T(8,128)(2,1)S(1)}, u32[]{:S(2)}, u32[]{:S(2)}) collective-permute-start(bf16[384,256]{0,1:T(8,128)(2,1)S(1)} %get-tuple-element.33), channel_id=1, source_target_pairs={{0,8},{8,16},{16,24},{24,32},{32,40},{40,48},{48,56},{56,64},{64,7... | collective-permute-start | bytes 589832 | tf_op jit(solution)/shard_map/ppermute | solution.py:12
  69.1 10.4 %collective-permute-start.1 = (bf16[384,256]{0,1:T(8,128)(2,1)S(1)}, bf16[384,256]{0,1:T(8,128)(2,1)S(1)}, u32[]{:S(2)}, u32[]{:S(2)}) collective-permute-start(bf16[384,256]{0,1:T(8,128)(2,1)S(1)} %get-tuple-element.34), channel_id=1, source_target_pairs={{8,0},{16,8},{24,16},{32,24},{40,32},{48,40},{56,48},{64,56},{72,6... | collective-permute-start | bytes 589832 | tf_op jit(solution)/shard_map/ppermute | solution.py:12
  80.4 111.4 %all-gather.7.cloned.1.call-start = ((), (), s32[]{:S(2)}) async-start(), calls=%async_computation.1 | async-start | bytes 3538944 | tf_op jit(solution)/shard_map/all_gather | solution.py:35
  134.1 10.6 %collective-permute-start.2 = (bf16[384,256]{0,1:T(8,128)(2,1)S(1)}, bf16[384,256]{0,1:T(8,128)(2,1)S(1)}, u32[]{:S(2)}, u32[]{:S(2)}) collective-permute-start(bf16[384,256]{0,1:T(8,128)(2,1)S(1)} %get-tuple-element.31), channel_id=1, source_target_pairs={{0,8},{8,16},{16,24},{24,32},{32,40},{40,48},{48,56},{56,64},{64,7... | collective-permute-start | bytes 589832 | tf_op jit(solution)/shard_map/ppermute | solution.py:12
  136.0 10.4 %collective-permute-start.3 = (bf16[384,256]{0,1:T(8,128)(2,1)S(1)}, bf16[384,256]{0,1:T(8,128)(2,1)S(1)}, u32[]{:S(2)}, u32[]{:S(2)}) collective-permute-start(bf16[384,256]{0,1:T(8,128)(2,1)S(1)} %get-tuple-element.32), channel_id=1, source_target_pairs={{8,0},{16,8},{24,16},{32,24},{40,32},{48,40},{56,48},{64,56},{72,6... | collective-permute-start | bytes 589832 | tf_op jit(solution)/shard_map/ppermute | solution.py:12
  200.7 10.6 %collective-permute-start.4 = (bf16[384,256]{0,1:T(8,128)(2,1)S(1)}, bf16[384,256]{0,1:T(8,128)(2,1)S(1)}, u32[]{:S(2)}, u32[]{:S(2)}) collective-permute-start(bf16[384,256]{0,1:T(8,128)(2,1)S(1)} %get-tuple-element.29), channel_id=1, source_target_pairs={{0,8},{8,16},{16,24},{24,32},{32,40},{40,48},{48,56},{56,64},{64,7... | collective-permute-start | bytes 589832 | tf_op jit(solution)/shard_map/ppermute | solution.py:12
  202.6 10.4 %collective-permute-start.5 = (bf16[384,256]{0,1:T(8,128)(2,1)S(1)}, bf16[384,256]{0,1:T(8,128)(2,1)S(1)}, u32[]{:S(2)}, u32[]{:S(2)}) collective-permute-start(bf16[384,256]{0,1:T(8,128)(2,1)S(1)} %get-tuple-element.30), channel_id=1, source_target_pairs={{8,0},{16,8},{24,16},{32,24},{40,32},{48,40},{56,48},{64,56},{72,6... | collective-permute-start | bytes 589832 | tf_op jit(solution)/shard_map/ppermute | solution.py:12
Sparse Core Ops, SparseCore 0:
  9.1 48.9 all-gather.8
  80.5 44.6 all-gather.4
  147.4 44.2 all-gather.6
where the time goes:
time: 221 us
  waiting for transfers between devices  148 us (67%)
  starting transfers between devices  27.6 us (12%)
  matrix products  26 us (12%)
  between operations  13.2 us (6%)
  other arithmetic  3.33 us (2%)
    all_gather x3, waiting for transfers between devices, per_device(): lax.all_gather(current, 'row', axis=0, tiled=True)  138 us
    ppermute x6, starting transfers between devices, shifted(): return lax.ppermute(array, axis, pairs)  27.5 us
    dot_general x3, matrix products, per_device(): jnp.dot(stacked, lax.all_gather(current, 'row', axis=0, tiled=True), pref...  26 us
    ppermute x6, waiting for transfers between devices, shifted(): return lax.ppermute(array, axis, pairs)  9.5 us
  transfers between devices with their start and end apart: 9, of which 9 were waited for; matrix products, arithmetic and copies ran while one was open for 1% of the time, Pallas kernels for 0%

commit v1 on v0

v1 whole, which is shorter than its diff:
```python
import functools

import jax
import jax.numpy as jnp
from jax import lax
from jax.experimental import pallas as pl
from jax.experimental.pallas import tpu as pltpu
from jax.sharding import PartitionSpec as P

TICKS = 3
AXES = ("layer", "row")


def at_row(row, dx, dy):
    return ((row // 4 + dx) % 2) * 4 + (row % 4 + dy) % 4


def near_layer(layer):
    return layer ^ 1


def far_layer(layer):
    return layer - 1 if layer % 2 == 0 else layer + 1


def permute(array, layers, rows, layer_to, dx, dy):
    pairs = [
        (layer * rows + row, layer_to(layer) * rows + at_row(row, dx, dy))
        for layer in range(layers)
        for row in range(rows)
        if 0 <= layer_to(layer) < layers
    ]
    return lax.ppermute(array, AXES, pairs)


def block_product(op_buf, block, half):
    count = half // 2
    near_re, near_im = block[:, :count], block[:, count:half]
    far_re, far_im = block[:, half : half + count], block[:, half + count :]
    lhs = jnp.concatenate([op_buf[part] for part in range(4)], axis=1)
    rhs = jnp.concatenate(
        [
            jnp.concatenate([far_re, far_im, near_re, near_im], axis=1),
            jnp.concatenate([-far_im, far_re, -near_im, near_re], axis=1),
            jnp.concatenate([near_re, near_im, far_re, far_im], axis=1),
            jnp.concatenate([-near_im, near_re, -far_im, far_re], axis=1),
        ],
        axis=0,
    )
    return jnp.dot(lhs, rhs, preferred_element_type=jnp.float32)


def stage_kernel(layout, first, last, places, ops, *refs):
    refs = list(refs)
    count = sum(len(cols) for block in layout for cols in block)
    pieces, refs = refs[:count], refs[count:]
    extra = None
    if not first:
        before, refs = refs[0], refs[1:]
    if last:
        extra, refs = refs[0], refs[1:]
        near_out, far_out, op_buf, sems = refs
    else:
        total_out, op_buf, sems = refs
    rows = ops.shape[2]
    copies = []
    for j in range(len(layout)):
        copy = pltpu.make_async_copy(
            ops.at[0, :, :, pl.ds(pl.multiple_of(places[j] * rows, rows), rows)],
            op_buf.at[j],
            sems.at[j],
        )
        copy.start()
        copies.append(copy)
    total = None if first else before[...]
    at = 0
    for j, block in enumerate(layout):
        parts = []
        for cols in block:
            group = [pieces[at + c][...] for c in range(len(cols))]
            at += len(cols)
            parts.append(group[0] if len(group) == 1 else jnp.concatenate(group, axis=1))
        whole = parts[0] if len(parts) == 1 else jnp.concatenate(parts, axis=0)
        copies[j].wait()
        term = block_product(op_buf.at[j], whole, whole.shape[1] // 2)
        total = term if total is None else total + term
    if last:
        total = total + extra[...].astype(jnp.float32)
        half = total.shape[1] // 2
        near_out[...] = total[:, :half].astype(jnp.bfloat16)
        far_out[...] = total[:, half:].astype(jnp.bfloat16)
    else:
        total_out[...] = total


def stage(operators, places, blocks, before=None, extra=None):
    rows = operators.shape[2]
    layout = [[[0] * len(cols) for cols in block] for block in blocks]
    flat = [piece for block in blocks for cols in block for piece in cols]
    width = sum(piece.shape[1] for piece in blocks[0][0])
    operands = [places, operators] + flat
    if before is not None:
        operands.append(before)
    if extra is not None:
        operands.append(extra)
    vmem = pl.BlockSpec(memory_space=pltpu.VMEM)
    if extra is not None:
        out_shape = [jax.ShapeDtypeStruct((rows, width // 2), jnp.bfloat16)] * 2
        out_specs = [vmem, vmem]
    else:
        out_shape = jax.ShapeDtypeStruct((rows, width), jnp.float32)
        out_specs = vmem
    n = len(blocks)
    return pl.pallas_call(
        functools.partial(stage_kernel, layout, before is None, extra is not None),
        out_shape=out_shape,
        in_specs=[pl.BlockSpec(memory_space=pltpu.SMEM), pl.BlockSpec(memory_space=pl.ANY)]
        + [vmem] * (len(operands) - 2),
        out_specs=out_specs,
        scratch_shapes=[
            pltpu.VMEM((n, 4, rows, rows), jnp.bfloat16),
            pltpu.SemaphoreType.DMA((n,)),
        ],
        compiler_params=pltpu.CompilerParams(vmem_limit_bytes=24 * 2**20),
        cost_estimate=pl.CostEstimate(
            flops=2 * n * 4 * rows * rows * width,
            bytes_accessed=n * (4 * rows * rows + rows * width) * 2,
            transcendentals=0,
        ),
    )(*operands)


def per_device(layers, waves, operators, sources, source_layer):
    rows = 8
    tile_rows = operators.shape[2]
    half = waves.shape[2] // 2
    third = tile_rows // 3
    layer_id = lax.axis_index("layer")
    row_id = lax.axis_index("row")
    even = layer_id % 2 == 0

    def place(dx, dy):
        return at_row(row_id, dx, dy)

    def places(*shifts):
        return jnp.stack([place(dx, dy) for dx, dy in shifts]).astype(jnp.int32)

    def swap_if_even(array):
        swapped = jnp.concatenate([array[:, half:], array[:, :half]], axis=1)
        return jnp.where(even, swapped, array)

    def stay(layer):
        return layer

    def move(array, dx, dy):
        return permute(array, layers, rows, stay, dx, dy)

    mask = jnp.tile((source_layer == layer_id).astype(jnp.bfloat16), 4)
    masked = sources * mask[None, :]
    swapped = jnp.concatenate([masked[:, half:], masked[:, :half]], axis=1)
    source_term = jnp.where(even, masked, swapped)
    own = swap_if_even(waves[0])
    for tick in range(TICKS):
        below = move(own, 0, -1)
        above = move(own, 0, 1)
        across = move(own, 1, 0)
        far_y = move(below, 0, -1)
        across_above = move(across, 0, 1)
        across_below = move(below, 1, 0)
        part0 = move(far_y[:third], 1, 0)
        part1 = move(across_above[third : 2 * third], 0, 1)
        part2 = move(across_below[2 * third :], 0, -1)
        total = stage(
            operators, places((0, 0), (0, 1), (0, -1), (1, 0)), [[[own]], [[below]], [[above]], [[across]]]
        )
        total = stage(
            operators,
            places((0, 2), (1, -1), (1, 1)),
            [[[far_y]], [[across_above]], [[across_below]]],
            before=total,
        )
        near, far = stage(
            operators, places((1, 2)), [[[part0], [part1], [part2]]], before=total, extra=source_term
        )
        near_in = permute(near, layers, rows, near_layer, 0, 0)
        far_in = permute(far, layers, rows, far_layer, 0, 0)
        own = jnp.concatenate([near_in, far_in], axis=1)
    return swap_if_even(own)[None]


def solution(mesh):
    return jax.shard_map(
        functools.partial(per_device, mesh.shape["layer"]),
        mesh=mesh,
        in_specs=(P("layer", "row", None), P("layer", None, "row", None), P("row", None), P()),
        out_specs=P("layer", "row", None),
        check_vma=False,
    )
```

time: 221 us -> 133 us (0.60)
  waiting for transfers between devices: 148 us -> 43.3 us
  starting transfers between devices: 27.6 us -> 53.8 us
  matrix products: 26 us -> 0 us
  Pallas kernels: 0 us -> 25.6 us
  between operations: 13.2 us -> 0.37 us
  local copies, waits for them, and re-layouts: 2.15 us -> 4.91 us
    all_gather x3 -> x0, waiting for transfers between devices: 138 us -> none  [per_device(): lax.all_gather(current, 'row', axis=0, tiled=True)]
    ppermute x6 -> x33, waiting for transfers between devices: 9.5 us -> 43.3 us  [permute(): return lax.ppermute(array, AXES, pairs)]
    ppermute x6 -> x33, starting transfers between devices: 27.5 us -> 53.8 us  [permute(): return lax.ppermute(array, AXES, pairs)]
    dot_general x3 -> x0, matrix products: 26 us -> none  [per_device(): jnp.dot(stacked, lax.all_gather(current, 'row', axis=0, tiled=True), pref...]
    pallas_call x0 -> x9, Pallas kernels: none -> 25.6 us  [stage(): pl.pallas_call(functools.partial(stage_kernel, layout, before is None, ex...]
    select_n x0 -> x3, other arithmetic: none -> 3.05 us  [the longest x2 1.93 us: swap_if_even(): return jnp.where(even, swapped, array)]
    unnamed x1 -> x6, local copies, waits for them, and re-layouts: 1.21 us -> 3.72 us
  transfers between devices with their start and end apart: 9 -> 33, of which waited for: 9 -> 11; matrix products, arithmetic and copies ran while one was open for 1% -> 2% of each run, Pallas kernels for 0% -> 17%
where the time goes in v1:
time: 133 us
  starting transfers between devices  53.8 us (40%)
  waiting for transfers between devices  43.3 us (33%)
  Pallas kernels  25.6 us (19%)
  local copies, waits for them, and re-layouts  4.91 us (4%)
  other arithmetic  4.88 us (4%)
    ppermute x33, starting transfers between devices, permute(): return lax.ppermute(array, AXES, pairs)  53.8 us
    ppermute x33, waiting for transfers between devices, permute(): return lax.ppermute(array, AXES, pairs)  43.3 us
    pallas_call x9, Pallas kernels, stage(): pl.pallas_call(functools.partial(stage_kernel, layout, before is None, ex...  25.6 us
    unnamed x6, local copies, waits for them, and re-layouts  3.72 us
  transfers between devices with their start and end apart: 33, of which 11 were waited for; matrix products, arithmetic and copies ran while one was open for 2% of the time, Pallas kernels for 17%

profile of v1, /device:TPU:6, one launch (start us, length us, event | category | flops | bytes accessed | tf_op | source)
XLA Modules:
  0.0 132.9 jit_solution(18066768862120908561)
XLA Ops:
  2.1 3.1 %collective-permute-start = (bf16[384,512]{1,0:T(8,128)(2,1)S(1)}, bf16[384,512]{1,0:T(8,128)(2,1)S(1)}, u32[]{:S(2)}, u32[]{:S(2)}) collective-permute-start(bf16[384,512]{1,0:T(8,128)(2,1)S(1)} %maximum_select_fusion.refs_0_), channel_id=1, source_target_pairs={{0,3},{1,0},{2,1},{3,2},{4,7},{5,4},{6,5},{7,6},{8,11},{9,8},{10,9... | collective-permute-start | bytes 1179656 | tf_op jit(solution)/shard_map/ppermute | solution.py:33
  7.8 1.1 maximum_select_fusion.1.refs_4_
  8.9 4.7 %collective-permute-done.refs_1_ = bf16[384,512]{1,0:T(8,128)(2,1)S(1)} collective-permute-done((bf16[384,512]{1,0:T(8,128)(2,1)S(1)}, bf16[384,512]{1,0:T(8,128)(2,1)S(1)}, u32[]{:S(2)}, u32[]{:S(2)}) %collective-permute-start) | collective-permute-done | bytes 393248 | tf_op jit(solution)/shard_map/ppermute | solution.py:33
  13.6 3.7 %collective-permute-start.1 = (bf16[384,512]{1,0:T(8,128)(2,1)S(1)}, bf16[384,512]{1,0:T(8,128)(2,1)S(1)}, u32[]{:S(2)}, u32[]{:S(2)}) collective-permute-start(bf16[384,512]{1,0:T(8,128)(2,1)S(1)} %collective-permute-done.refs_1_), channel_id=1, source_target_pairs={{0,3},{1,0},{2,1},{3,2},{4,7},{5,4},{6,5},{7,6},{8,11},{9,8},{10,9... | collective-permute-start | bytes 1179656 | tf_op jit(solution)/shard_map/ppermute | solution.py:33
  18.3 3.7 %copy-done = bf16[1,4,384,3072]{3,2,1,0:T(8,128)(2,1)S(1)} copy-done((bf16[1,4,384,3072]{3,2,1,0:T(8,128)(2,1)S(1)}, bf16[1,4,384,3072]{3,2,1,0:T(8,128)(2,1)}, u32[]{:S(2)}) %copy-start) | copy-done | bytes 9437208
  22.0 4.2 %shard_map.46.refs_3_ = f32[384,512]{1,0:T(8,128)S(1)} custom-call(s32[4]{0:T(128)S(1)} %pad_add_fusion.1.places, bf16[1,4,384,3072]{3,2,1,0:T(8,128)(2,1)S(1)} %copy-done, bf16[384,512]{1,0:T(8,128)(2,1)S(1)} %maximum_select_fusion.refs_0_, bf16[384,512]{1,0:T(8,128)(2,1)S(1)} %collective-permute-done.refs_1_, ...), custom_call_target="tpu_custom_call" | custom-call | flops 2415919104 | bytes 6291456 | tf_op jit(solution)/shard_map/pallas_call | solution.py:114
  26.2 1.3 collective-permute-start.2
  27.5 3.3 %collective-permute-start.7 = (bf16[128,512]{1,0:T(8,128)(2,1)S(1)}, bf16[128,512]{1,0:T(8,128)(2,1)S(1)}, u32[]{:S(2)}, u32[]{:S(2)}) collective-permute-start(bf16[128,512]{1,0:T(8,128)(2,1)S(1)} %slice.56), channel_id=1, source_target_pairs={{0,3},{1,0},{2,1},{3,2},{4,7},{5,4},{6,5},{7,6},{8,11},{9,8},{10,9... | collective-permute-start | bytes 393224 | tf_op jit(solution)/shard_map/ppermute | solution.py:33
  31.0 3.3 %shard_map.47.refs_3_ = f32[384,512]{1,0:T(8,128)S(1)} custom-call(s32[3]{0:T(128)S(1)} %pad_add_fusion.places, bf16[1,4,384,3072]{3,2,1,0:T(8,128)(2,1)S(1)} %copy-done.1, bf16[384,512]{1,0:T(8,128)(2,1)S(1)} %collective-permute-done.1.refs_0_, bf16[384,512]{1,0:T(8,128)(2,1)S(1)} %collective-permute-done.4.refs_1_, ...), custom_call_target="tpu_custom_call" | custom-call | flops 1811939328 | bytes 4718592 | tf_op jit(solution)/shard_map/pallas_call | solution.py:114
  34.3 2.8 %collective-permute-done.5.refs_1_ = bf16[128,512]{1,0:T(8,128)(2,1)S(1)} collective-permute-done((bf16[128,512]{1,0:T(8,128)(2,1)S(1)}, bf16[128,512]{1,0:T(8,128)(2,1)S(1)}, u32[]{:S(2)}, u32[]{:S(2)}) %collective-permute-start.5) | collective-permute-done | bytes 131104 | tf_op jit(solution)/shard_map/ppermute | solution.py:33
  38.4 8.7 %collective-permute-start.10 = (bf16[384,256]{1,0:T(8,128)(2,1)S(1)}, bf16[384,256]{1,0:T(8,128)(2,1)S(1)}, u32[]{:S(2)}, u32[]{:S(2)}) collective-permute-start(bf16[384,256]{1,0:T(8,128)(2,1)S(1)} %get-tuple-element.12), channel_id=1, source_target_pairs={{8,16},{9,17},{10,18},{11,19},{12,20},{13,21},{14,22},{15,23},{16,... | collective-permute-start | bytes 589832 | tf_op jit(solution)/shard_map/ppermute | solution.py:33
  47.2 3.4 %collective-permute-done.10 = bf16[384,256]{1,0:T(8,128)(2,1)S(1)} collective-permute-done((bf16[384,256]{1,0:T(8,128)(2,1)S(1)}, bf16[384,256]{1,0:T(8,128)(2,1)S(1)}, u32[]{:S(2)}, u32[]{:S(2)}) %collective-permute-start.10) | collective-permute-done | bytes 196640 | tf_op jit(solution)/shard_map/ppermute | solution.py:33
  51.1 1.6 %collective-permute-start.19 = (bf16[384,512]{1,0:T(8,128)(2,1)S(1)}, bf16[384,512]{1,0:T(8,128)(2,1)S(1)}, u32[]{:S(2)}, u32[]{:S(2)}) collective-permute-start(bf16[384,512]{1,0:T(8,128)(2,1)S(1)} %constant_dynamic-update-slice_fusion.refs_0_), channel_id=1, source_target_pairs={{0,1},{1,2},{2,3},{3,0},{4,5},{5,6},{6,7},{7,4},{8,9},{9,10},{10,1... | collective-permute-start | bytes 1179656 | tf_op jit(solution)/shard_map/ppermute | solution.py:33
  52.7 9.0 %collective-permute-done.11.refs_1_ = bf16[384,512]{1,0:T(8,128)(2,1)S(1)} collective-permute-done((bf16[384,512]{1,0:T(8,128)(2,1)S(1)}, bf16[384,512]{1,0:T(8,128)(2,1)S(1)}, u32[]{:S(2)}, u32[]{:S(2)}) %collective-permute-start.11) | collective-permute-done | bytes 393248 | tf_op jit(solution)/shard_map/ppermute | solution.py:33
  62.0 1.7 %collective-permute-start.15 = (bf16[384,512]{1,0:T(8,128)(2,1)S(1)}, bf16[384,512]{1,0:T(8,128)(2,1)S(1)}, u32[]{:S(2)}, u32[]{:S(2)}) collective-permute-start(bf16[384,512]{1,0:T(8,128)(2,1)S(1)} %collective-permute-done.14.refs_3_), channel_id=1, source_target_pairs={{0,1},{1,2},{2,3},{3,0},{4,5},{5,6},{6,7},{7,4},{8,9},{9,10},{10,1... | collective-permute-start | bytes 1179656 | tf_op jit(solution)/shard_map/ppermute | solution.py:33
  63.7 4.2 %shard_map.49.refs_3_ = f32[384,512]{1,0:T(8,128)S(1)} custom-call(s32[4]{0:T(128)S(1)} %pad_add_fusion.1.places, bf16[1,4,384,3072]{3,2,1,0:T(8,128)(2,1)S(1)} %copy-done.1, bf16[384,512]{1,0:T(8,128)(2,1)S(1)} %constant_dynamic-update-slice_fusion.refs_0_, bf16[384,512]{1,0:T(8,128)(2,1)S(1)} %collective-permute-done.11.refs_1_, ...), custom_call_target="tpu_custom_call" | custom-call | flops 2415919104 | bytes 6291456 | tf_op jit(solution)/shard_map/pallas_call | solution.py:114
  67.9 2.9 %collective-permute-done.12.refs_0_ = bf16[384,512]{1,0:T(8,128)(2,1)S(1)} collective-permute-done((bf16[384,512]{1,0:T(8,128)(2,1)S(1)}, bf16[384,512]{1,0:T(8,128)(2,1)S(1)}, u32[]{:S(2)}, u32[]{:S(2)}) %collective-permute-start.12) | collective-permute-done | bytes 393248 | tf_op jit(solution)/shard_map/ppermute | solution.py:33
  71.0 1.4 %collective-permute-done.15.refs_1_ = bf16[384,512]{1,0:T(8,128)(2,1)S(1)} collective-permute-done((bf16[384,512]{1,0:T(8,128)(2,1)S(1)}, bf16[384,512]{1,0:T(8,128)(2,1)S(1)}, u32[]{:S(2)}, u32[]{:S(2)}) %collective-permute-start.15) | collective-permute-done | bytes 393248 | tf_op jit(solution)/shard_map/ppermute | solution.py:33
  72.9 2.9 %collective-permute-start.18 = (bf16[128,512]{1,0:T(8,128)(2,1)S(1)}, bf16[128,512]{1,0:T(8,128)(2,1)S(1)}, u32[]{:S(2)}, u32[]{:S(2)}) collective-permute-start(bf16[128,512]{1,0:T(8,128)(2,1)S(1)} %slice.61), channel_id=1, source_target_pairs={{0,3},{1,0},{2,1},{3,2},{4,7},{5,4},{6,5},{7,6},{8,11},{9,8},{10,9... | collective-permute-start | bytes 393224 | tf_op jit(solution)/shard_map/ppermute | solution.py:33
  75.8 3.3 %shard_map.50.refs_3_ = f32[384,512]{1,0:T(8,128)S(1)} custom-call(s32[3]{0:T(128)S(1)} %pad_add_fusion.places, bf16[1,4,384,3072]{3,2,1,0:T(8,128)(2,1)S(1)} %copy-done.1, bf16[384,512]{1,0:T(8,128)(2,1)S(1)} %collective-permute-done.12.refs_0_, bf16[384,512]{1,0:T(8,128)(2,1)S(1)} %collective-permute-done.15.refs_1_, ...), custom_call_target="tpu_custom_call" | custom-call | flops 1811939328 | bytes 4718592 | tf_op jit(solution)/shard_map/pallas_call | solution.py:114
  80.3 4.1 %collective-permute-start.21 = (bf16[384,256]{1,0:T(8,128)(2,1)S(1)}, bf16[384,256]{1,0:T(8,128)(2,1)S(1)}, u32[]{:S(2)}, u32[]{:S(2)}) collective-permute-start(bf16[384,256]{1,0:T(8,128)(2,1)S(1)} %get-tuple-element.14), channel_id=1, source_target_pairs={{8,16},{9,17},{10,18},{11,19},{12,20},{13,21},{14,22},{15,23},{16,... | collective-permute-start | bytes 589832 | tf_op jit(solution)/shard_map/ppermute | solution.py:33
  84.4 6.6 %collective-permute-done.21 = bf16[384,256]{1,0:T(8,128)(2,1)S(1)} collective-permute-done((bf16[384,256]{1,0:T(8,128)(2,1)S(1)}, bf16[384,256]{1,0:T(8,128)(2,1)S(1)}, u32[]{:S(2)}, u32[]{:S(2)}) %collective-permute-start.21) | collective-permute-done | bytes 196640 | tf_op jit(solution)/shard_map/ppermute | solution.py:33
  91.0 3.1 %collective-permute-start.22 = (bf16[384,512]{1,0:T(8,128)(2,1)S(1)}, bf16[384,512]{1,0:T(8,128)(2,1)S(1)}, u32[]{:S(2)}, u32[]{:S(2)}) collective-permute-start(bf16[384,512]{1,0:T(8,128)(2,1)S(1)} %constant_dynamic-update-slice_fusion.2.refs_0_), channel_id=1, source_target_pairs={{0,3},{1,0},{2,1},{3,2},{4,7},{5,4},{6,5},{7,6},{8,11},{9,8},{10,9... | collective-permute-start | bytes 1179656 | tf_op jit(solution)/shard_map/ppermute | solution.py:33
  94.8 5.5 %collective-permute-done.22.refs_1_ = bf16[384,512]{1,0:T(8,128)(2,1)S(1)} collective-permute-done((bf16[384,512]{1,0:T(8,128)(2,1)S(1)}, bf16[384,512]{1,0:T(8,128)(2,1)S(1)}, u32[]{:S(2)}, u32[]{:S(2)}) %collective-permute-start.22) | collective-permute-done | bytes 393248 | tf_op jit(solution)/shard_map/ppermute | solution.py:33
  100.2 3.5 %collective-permute-start.23 = (bf16[384,512]{1,0:T(8,128)(2,1)S(1)}, bf16[384,512]{1,0:T(8,128)(2,1)S(1)}, u32[]{:S(2)}, u32[]{:S(2)}) collective-permute-start(bf16[384,512]{1,0:T(8,128)(2,1)S(1)} %collective-permute-done.22.refs_1_), channel_id=1, source_target_pairs={{0,3},{1,0},{2,1},{3,2},{4,7},{5,4},{6,5},{7,6},{8,11},{9,8},{10,9... | collective-permute-start | bytes 1179656 | tf_op jit(solution)/shard_map/ppermute | solution.py:33
  105.1 4.2 %shard_map.52.refs_3_ = f32[384,512]{1,0:T(8,128)S(1)} custom-call(s32[4]{0:T(128)S(1)} %pad_add_fusion.1.places, bf16[1,4,384,3072]{3,2,1,0:T(8,128)(2,1)S(1)} %copy-done.1, bf16[384,512]{1,0:T(8,128)(2,1)S(1)} %constant_dynamic-update-slice_fusion.2.refs_0_, bf16[384,512]{1,0:T(8,128)(2,1)S(1)} %collective-permute-done.22.refs_1_, ...), custom_call_target="tpu_custom_call" | custom-call | flops 2415919104 | bytes 6291456 | tf_op jit(solution)/shard_map/pallas_call | solution.py:114
  109.4 2.4 %collective-permute-start.24 = (bf16[128,512]{1,0:T(8,128)(2,1)S(1)}, bf16[128,512]{1,0:T(8,128)(2,1)S(1)}, u32[]{:S(2)}, u32[]{:S(2)}) collective-permute-start(bf16[128,512]{1,0:T(8,128)(2,1)S(1)} %slice.62), channel_id=1, source_target_pairs={{0,4},{1,5},{2,6},{3,7},{4,0},{5,1},{6,2},{7,3},{8,12},{9,13},{10,... | collective-permute-start | bytes 393224 | tf_op jit(solution)/shard_map/ppermute | solution.py:33
  111.8 1.9 %collective-permute-done.26.refs_1_ = bf16[384,512]{1,0:T(8,128)(2,1)S(1)} collective-permute-done((bf16[384,512]{1,0:T(8,128)(2,1)S(1)}, bf16[384,512]{1,0:T(8,128)(2,1)S(1)}, u32[]{:S(2)}, u32[]{:S(2)}) %collective-permute-start.26) | collective-permute-done | bytes 393248 | tf_op jit(solution)/shard_map/ppermute | solution.py:33
  113.8 3.3 %collective-permute-start.29 = (bf16[128,512]{1,0:T(8,128)(2,1)S(1)}, bf16[128,512]{1,0:T(8,128)(2,1)S(1)}, u32[]{:S(2)}, u32[]{:S(2)}) collective-permute-start(bf16[128,512]{1,0:T(8,128)(2,1)S(1)} %slice.64), channel_id=1, source_target_pairs={{0,3},{1,0},{2,1},{3,2},{4,7},{5,4},{6,5},{7,6},{8,11},{9,8},{10,9... | collective-permute-start | bytes 393224 | tf_op jit(solution)/shard_map/ppermute | solution.py:33
  117.1 3.3 %shard_map.53.refs_3_ = f32[384,512]{1,0:T(8,128)S(1)} custom-call(s32[3]{0:T(128)S(1)} %pad_add_fusion.places, bf16[1,4,384,3072]{3,2,1,0:T(8,128)(2,1)S(1)} %copy-done.1, bf16[384,512]{1,0:T(8,128)(2,1)S(1)} %collective-permute-done.23.refs_0_, bf16[384,512]{1,0:T(8,128)(2,1)S(1)} %collective-permute-done.26.refs_1_, ...), custom_call_target="tpu_custom_call" | custom-call | flops 1811939328 | bytes 4718592 | tf_op jit(solution)/shard_map/pallas_call | solution.py:114
  121.4 6.3 %collective-permute-start.31 = (bf16[384,256]{1,0:T(8,128)(2,1)S(1)}, bf16[384,256]{1,0:T(8,128)(2,1)S(1)}, u32[]{:S(2)}, u32[]{:S(2)}) collective-permute-start(bf16[384,256]{1,0:T(8,128)(2,1)S(1)} %get-tuple-element.15), channel_id=1, source_target_pairs={{8,16},{9,17},{10,18},{11,19},{12,20},{13,21},{14,22},{15,23},{16,... | collective-permute-start | bytes 589832 | tf_op jit(solution)/shard_map/ppermute | solution.py:33
  127.8 4.2 %collective-permute-done.31 = bf16[384,256]{1,0:T(8,128)(2,1)S(1)} collective-permute-done((bf16[384,256]{1,0:T(8,128)(2,1)S(1)}, bf16[384,256]{1,0:T(8,128)(2,1)S(1)}, u32[]{:S(2)}, u32[]{:S(2)}) %collective-permute-start.31) | collective-permute-done | bytes 196640 | tf_op jit(solution)/shard_map/ppermute | solution.py:33
  (70 shorter events, 13.8 us)
Async XLA Ops:
  2.1 11.5 %collective-permute-start = (bf16[384,512]{1,0:T(8,128)(2,1)S(1)}, bf16[384,512]{1,0:T(8,128)(2,1)S(1)}, u32[]{:S(2)}, u32[]{:S(2)}) collective-permute-start(bf16[384,512]{1,0:T(8,128)(2,1)S(1)} %maximum_select_fusion.refs_0_), channel_id=1, source_target_pairs={{0,3},{1,0},{2,1},{3,2},{4,7},{5,4},{6,5},{7,6},{8,11},{9,8},{10,9... | collective-permute-start | bytes 1179656 | tf_op jit(solution)/shard_map/ppermute | solution.py:33
  5.2 12.9 %collective-permute-start.3 = (bf16[384,512]{1,0:T(8,128)(2,1)S(1)}, bf16[384,512]{1,0:T(8,128)(2,1)S(1)}, u32[]{:S(2)}, u32[]{:S(2)}) collective-permute-start(bf16[384,512]{1,0:T(8,128)(2,1)S(1)} %maximum_select_fusion.refs_0_), channel_id=1, source_target_pairs={{0,4},{1,5},{2,6},{3,7},{4,0},{5,1},{6,2},{7,3},{8,12},{9,13},{10,... | collective-permute-start | bytes 1179656 | tf_op jit(solution)/shard_map/ppermute | solution.py:33
  6.1 12.2 %collective-permute-start.8 = (bf16[384,512]{1,0:T(8,128)(2,1)S(1)}, bf16[384,512]{1,0:T(8,128)(2,1)S(1)}, u32[]{:S(2)}, u32[]{:S(2)}) collective-permute-start(bf16[384,512]{1,0:T(8,128)(2,1)S(1)} %maximum_select_fusion.refs_0_), channel_id=1, source_target_pairs={{0,1},{1,2},{2,3},{3,0},{4,5},{5,6},{6,7},{7,4},{8,9},{9,10},{10,1... | collective-permute-start | bytes 1179656 | tf_op jit(solution)/shard_map/ppermute | solution.py:33
  13.6 12.6 %collective-permute-start.1 = (bf16[384,512]{1,0:T(8,128)(2,1)S(1)}, bf16[384,512]{1,0:T(8,128)(2,1)S(1)}, u32[]{:S(2)}, u32[]{:S(2)}) collective-permute-start(bf16[384,512]{1,0:T(8,128)(2,1)S(1)} %collective-permute-done.refs_1_), channel_id=1, source_target_pairs={{0,3},{1,0},{2,1},{3,2},{4,7},{5,4},{6,5},{7,6},{8,11},{9,8},{10,9... | collective-permute-start | bytes 1179656 | tf_op jit(solution)/shard_map/ppermute | solution.py:33
  17.3 10.2 %collective-permute-start.6 = (bf16[384,512]{1,0:T(8,128)(2,1)S(1)}, bf16[384,512]{1,0:T(8,128)(2,1)S(1)}, u32[]{:S(2)}, u32[]{:S(2)}) collective-permute-start(bf16[384,512]{1,0:T(8,128)(2,1)S(1)} %collective-permute-done.refs_1_), channel_id=1, source_target_pairs={{0,4},{1,5},{2,6},{3,7},{4,0},{5,1},{6,2},{7,3},{8,12},{9,13},{10,... | collective-permute-start | bytes 1179656 | tf_op jit(solution)/shard_map/ppermute | solution.py:33
  18.1 12.7 %collective-permute-start.4 = (bf16[384,512]{1,0:T(8,128)(2,1)S(1)}, bf16[384,512]{1,0:T(8,128)(2,1)S(1)}, u32[]{:S(2)}, u32[]{:S(2)}) collective-permute-start(bf16[384,512]{1,0:T(8,128)(2,1)S(1)} %collective-permute-done.3.refs_3_), channel_id=1, source_target_pairs={{0,1},{1,2},{2,3},{3,0},{4,5},{5,6},{6,7},{7,4},{8,9},{9,10},{10,1... | collective-permute-start | bytes 1179656 | tf_op jit(solution)/shard_map/ppermute | solution.py:33
  26.2 8.0 %collective-permute-start.2 = (bf16[128,512]{1,0:T(8,128)(2,1)S(1)}, bf16[128,512]{1,0:T(8,128)(2,1)S(1)}, u32[]{:S(2)}, u32[]{:S(2)}) collective-permute-start(bf16[128,512]{1,0:T(8,128)(2,1)S(1)} %slice.54), channel_id=1, source_target_pairs={{0,4},{1,5},{2,6},{3,7},{4,0},{5,1},{6,2},{7,3},{8,12},{9,13},{10,... | collective-permute-start | bytes 393224 | tf_op jit(solution)/shard_map/ppermute | solution.py:33
  27.5 6.7 %collective-permute-start.7 = (bf16[128,512]{1,0:T(8,128)(2,1)S(1)}, bf16[128,512]{1,0:T(8,128)(2,1)S(1)}, u32[]{:S(2)}, u32[]{:S(2)}) collective-permute-start(bf16[128,512]{1,0:T(8,128)(2,1)S(1)} %slice.56), channel_id=1, source_target_pairs={{0,3},{1,0},{2,1},{3,2},{4,7},{5,4},{6,5},{7,6},{8,11},{9,8},{10,9... | collective-permute-start | bytes 393224 | tf_op jit(solution)/shard_map/ppermute | solution.py:33
  30.9 6.3 %collective-permute-start.5 = (bf16[128,512]{1,0:T(8,128)(2,1)S(1)}, bf16[128,512]{1,0:T(8,128)(2,1)S(1)}, u32[]{:S(2)}, u32[]{:S(2)}) collective-permute-start(bf16[128,512]{1,0:T(8,128)(2,1)S(1)} %slice.55), channel_id=1, source_target_pairs={{0,1},{1,2},{2,3},{3,0},{4,5},{5,6},{6,7},{7,4},{8,9},{9,10},{10,1... | collective-permute-start | bytes 393224 | tf_op jit(solution)/shard_map/ppermute | solution.py:33
  38.2 9.0 %collective-permute-start.9 = (bf16[384,256]{1,0:T(8,128)(2,1)S(1)}, bf16[384,256]{1,0:T(8,128)(2,1)S(1)}, u32[]{:S(2)}, u32[]{:S(2)}) collective-permute-start(bf16[384,256]{1,0:T(8,128)(2,1)S(1)} %get-tuple-element.11), channel_id=1, source_target_pairs={{0,8},{1,9},{2,10},{3,11},{4,12},{5,13},{6,14},{7,15},{8,0},{9,1},... | collective-permute-start | bytes 589832 | tf_op jit(solution)/shard_map/ppermute | solution.py:33
  38.4 12.1 %collective-permute-start.10 = (bf16[384,256]{1,0:T(8,128)(2,1)S(1)}, bf16[384,256]{1,0:T(8,128)(2,1)S(1)}, u32[]{:S(2)}, u32[]{:S(2)}) collective-permute-start(bf16[384,256]{1,0:T(8,128)(2,1)S(1)} %get-tuple-element.12), channel_id=1, source_target_pairs={{8,16},{9,17},{10,18},{11,19},{12,20},{13,21},{14,22},{15,23},{16,... | collective-permute-start | bytes 589832 | tf_op jit(solution)/shard_map/ppermute | solution.py:33
  50.6 11.1 %collective-permute-start.11 = (bf16[384,512]{1,0:T(8,128)(2,1)S(1)}, bf16[384,512]{1,0:T(8,128)(2,1)S(1)}, u32[]{:S(2)}, u32[]{:S(2)}) collective-permute-start(bf16[384,512]{1,0:T(8,128)(2,1)S(1)} %constant_dynamic-update-slice_fusion.refs_0_), channel_id=1, source_target_pairs={{0,3},{1,0},{2,1},{3,2},{4,7},{5,4},{6,5},{7,6},{8,11},{9,8},{10,9... | collective-permute-start | bytes 1179656 | tf_op jit(solution)/shard_map/ppermute | solution.py:33
  51.1 10.9 %collective-permute-start.14 = (bf16[384,512]{1,0:T(8,128)(2,1)S(1)}, bf16[384,512]{1,0:T(8,128)(2,1)S(1)}, u32[]{:S(2)}, u32[]{:S(2)}) collective-permute-start(bf16[384,512]{1,0:T(8,128)(2,1)S(1)} %constant_dynamic-update-slice_fusion.refs_0_), channel_id=1, source_target_pairs={{0,4},{1,5},{2,6},{3,7},{4,0},{5,1},{6,2},{7,3},{8,12},{9,13},{10,... | collective-permute-start | bytes 1179656 | tf_op jit(solution)/shard_map/ppermute | solution.py:33
  51.1 12.6 %collective-permute-start.19 = (bf16[384,512]{1,0:T(8,128)(2,1)S(1)}, bf16[384,512]{1,0:T(8,128)(2,1)S(1)}, u32[]{:S(2)}, u32[]{:S(2)}) collective-permute-start(bf16[384,512]{1,0:T(8,128)(2,1)S(1)} %constant_dynamic-update-slice_fusion.refs_0_), channel_id=1, source_target_pairs={{0,1},{1,2},{2,3},{3,0},{4,5},{5,6},{6,7},{7,4},{8,9},{9,10},{10,1... | collective-permute-start | bytes 1179656 | tf_op jit(solution)/shard_map/ppermute | solution.py:33
  61.7 9.2 %collective-permute-start.12 = (bf16[384,512]{1,0:T(8,128)(2,1)S(1)}, bf16[384,512]{1,0:T(8,128)(2,1)S(1)}, u32[]{:S(2)}, u32[]{:S(2)}) collective-permute-start(bf16[384,512]{1,0:T(8,128)(2,1)S(1)} %collective-permute-done.11.refs_1_), channel_id=1, source_target_pairs={{0,3},{1,0},{2,1},{3,2},{4,7},{5,4},{6,5},{7,6},{8,11},{9,8},{10,9... | collective-permute-start | bytes 1179656 | tf_op jit(solution)/shard_map/ppermute | solution.py:33
  62.0 10.4 %collective-permute-start.15 = (bf16[384,512]{1,0:T(8,128)(2,1)S(1)}, bf16[384,512]{1,0:T(8,128)(2,1)S(1)}, u32[]{:S(2)}, u32[]{:S(2)}) collective-permute-start(bf16[384,512]{1,0:T(8,128)(2,1)S(1)} %collective-permute-done.14.refs_3_), channel_id=1, source_target_pairs={{0,1},{1,2},{2,3},{3,0},{4,5},{5,6},{6,7},{7,4},{8,9},{9,10},{10,1... | collective-permute-start | bytes 1179656 | tf_op jit(solution)/shard_map/ppermute | solution.py:33
  63.7 9.2 %collective-permute-start.17 = (bf16[384,512]{1,0:T(8,128)(2,1)S(1)}, bf16[384,512]{1,0:T(8,128)(2,1)S(1)}, u32[]{:S(2)}, u32[]{:S(2)}) collective-permute-start(bf16[384,512]{1,0:T(8,128)(2,1)S(1)} %collective-permute-done.11.refs_1_), channel_id=1, source_target_pairs={{0,4},{1,5},{2,6},{3,7},{4,0},{5,1},{6,2},{7,3},{8,12},{9,13},{10,... | collective-permute-start | bytes 1179656 | tf_op jit(solution)/shard_map/ppermute | solution.py:33
  70.9 8.3 %collective-permute-start.13 = (bf16[128,512]{1,0:T(8,128)(2,1)S(1)}, bf16[128,512]{1,0:T(8,128)(2,1)S(1)}, u32[]{:S(2)}, u32[]{:S(2)}) collective-permute-start(bf16[128,512]{1,0:T(8,128)(2,1)S(1)} %slice.59), channel_id=1, source_target_pairs={{0,4},{1,5},{2,6},{3,7},{4,0},{5,1},{6,2},{7,3},{8,12},{9,13},{10,... | collective-permute-start | bytes 393224 | tf_op jit(solution)/shard_map/ppermute | solution.py:33
  72.4 6.7 %collective-permute-start.16 = (bf16[128,512]{1,0:T(8,128)(2,1)S(1)}, bf16[128,512]{1,0:T(8,128)(2,1)S(1)}, u32[]{:S(2)}, u32[]{:S(2)}) collective-permute-start(bf16[128,512]{1,0:T(8,128)(2,1)S(1)} %slice.60), channel_id=1, source_target_pairs={{0,1},{1,2},{2,3},{3,0},{4,5},{5,6},{6,7},{7,4},{8,9},{9,10},{10,1... | collective-permute-start | bytes 393224 | tf_op jit(solution)/shard_map/ppermute | solution.py:33
  72.9 6.2 %collective-permute-start.18 = (bf16[128,512]{1,0:T(8,128)(2,1)S(1)}, bf16[128,512]{1,0:T(8,128)(2,1)S(1)}, u32[]{:S(2)}, u32[]{:S(2)}) collective-permute-start(bf16[128,512]{1,0:T(8,128)(2,1)S(1)} %slice.61), channel_id=1, source_target_pairs={{0,3},{1,0},{2,1},{3,2},{4,7},{5,4},{6,5},{7,6},{8,11},{9,8},{10,9... | collective-permute-start | bytes 393224 | tf_op jit(solution)/shard_map/ppermute | solution.py:33
  80.3 10.7 %collective-permute-start.21 = (bf16[384,256]{1,0:T(8,128)(2,1)S(1)}, bf16[384,256]{1,0:T(8,128)(2,1)S(1)}, u32[]{:S(2)}, u32[]{:S(2)}) collective-permute-start(bf16[384,256]{1,0:T(8,128)(2,1)S(1)} %get-tuple-element.14), channel_id=1, source_target_pairs={{8,16},{9,17},{10,18},{11,19},{12,20},{13,21},{14,22},{15,23},{16,... | collective-permute-start | bytes 589832 | tf_op jit(solution)/shard_map/ppermute | solution.py:33
  91.0 9.2 %collective-permute-start.22 = (bf16[384,512]{1,0:T(8,128)(2,1)S(1)}, bf16[384,512]{1,0:T(8,128)(2,1)S(1)}, u32[]{:S(2)}, u32[]{:S(2)}) collective-permute-start(bf16[384,512]{1,0:T(8,128)(2,1)S(1)} %constant_dynamic-update-slice_fusion.2.refs_0_), channel_id=1, source_target_pairs={{0,3},{1,0},{2,1},{3,2},{4,7},{5,4},{6,5},{7,6},{8,11},{9,8},{10,9... | collective-permute-start | bytes 1179656 | tf_op jit(solution)/shard_map/ppermute | solution.py:33
  94.2 9.5 %collective-permute-start.25 = (bf16[384,512]{1,0:T(8,128)(2,1)S(1)}, bf16[384,512]{1,0:T(8,128)(2,1)S(1)}, u32[]{:S(2)}, u32[]{:S(2)}) collective-permute-start(bf16[384,512]{1,0:T(8,128)(2,1)S(1)} %constant_dynamic-update-slice_fusion.2.refs_0_), channel_id=1, source_target_pairs={{0,4},{1,5},{2,6},{3,7},{4,0},{5,1},{6,2},{7,3},{8,12},{9,13},{10,... | collective-permute-start | bytes 1179656 | tf_op jit(solution)/shard_map/ppermute | solution.py:33
  94.8 10.4 %collective-permute-start.30 = (bf16[384,512]{1,0:T(8,128)(2,1)S(1)}, bf16[384,512]{1,0:T(8,128)(2,1)S(1)}, u32[]{:S(2)}, u32[]{:S(2)}) collective-permute-start(bf16[384,512]{1,0:T(8,128)(2,1)S(1)} %constant_dynamic-update-slice_fusion.2.refs_0_), channel_id=1, source_target_pairs={{0,1},{1,2},{2,3},{3,0},{4,5},{5,6},{6,7},{7,4},{8,9},{9,10},{10,1... | collective-permute-start | bytes 1179656 | tf_op jit(solution)/shard_map/ppermute | solution.py:33
  100.2 9.1 %collective-permute-start.23 = (bf16[384,512]{1,0:T(8,128)(2,1)S(1)}, bf16[384,512]{1,0:T(8,128)(2,1)S(1)}, u32[]{:S(2)}, u32[]{:S(2)}) collective-permute-start(bf16[384,512]{1,0:T(8,128)(2,1)S(1)} %collective-permute-done.22.refs_1_), channel_id=1, source_target_pairs={{0,3},{1,0},{2,1},{3,2},{4,7},{5,4},{6,5},{7,6},{8,11},{9,8},{10,9... | collective-permute-start | bytes 1179656 | tf_op jit(solution)/shard_map/ppermute | solution.py:33
  103.7 9.9 %collective-permute-start.26 = (bf16[384,512]{1,0:T(8,128)(2,1)S(1)}, bf16[384,512]{1,0:T(8,128)(2,1)S(1)}, u32[]{:S(2)}, u32[]{:S(2)}) collective-permute-start(bf16[384,512]{1,0:T(8,128)(2,1)S(1)} %collective-permute-done.25.refs_3_), channel_id=1, source_target_pairs={{0,1},{1,2},{2,3},{3,0},{4,5},{5,6},{6,7},{7,4},{8,9},{9,10},{10,1... | collective-permute-start | bytes 1179656 | tf_op jit(solution)/shard_map/ppermute | solution.py:33
  103.7 10.0 %collective-permute-start.28 = (bf16[384,512]{1,0:T(8,128)(2,1)S(1)}, bf16[384,512]{1,0:T(8,128)(2,1)S(1)}, u32[]{:S(2)}, u32[]{:S(2)}) collective-permute-start(bf16[384,512]{1,0:T(8,128)(2,1)S(1)} %collective-permute-done.22.refs_1_), channel_id=1, source_target_pairs={{0,4},{1,5},{2,6},{3,7},{4,0},{5,1},{6,2},{7,3},{8,12},{9,13},{10,... | collective-permute-start | bytes 1179656 | tf_op jit(solution)/shard_map/ppermute | solution.py:33
  109.4 11.0 %collective-permute-start.24 = (bf16[128,512]{1,0:T(8,128)(2,1)S(1)}, bf16[128,512]{1,0:T(8,128)(2,1)S(1)}, u32[]{:S(2)}, u32[]{:S(2)}) collective-permute-start(bf16[128,512]{1,0:T(8,128)(2,1)S(1)} %slice.62), channel_id=1, source_target_pairs={{0,4},{1,5},{2,6},{3,7},{4,0},{5,1},{6,2},{7,3},{8,12},{9,13},{10,... | collective-permute-start | bytes 393224 | tf_op jit(solution)/shard_map/ppermute | solution.py:33
  113.6 6.7 %collective-permute-start.27 = (bf16[128,512]{1,0:T(8,128)(2,1)S(1)}, bf16[128,512]{1,0:T(8,128)(2,1)S(1)}, u32[]{:S(2)}, u32[]{:S(2)}) collective-permute-start(bf16[128,512]{1,0:T(8,128)(2,1)S(1)} %slice.63), channel_id=1, source_target_pairs={{0,1},{1,2},{2,3},{3,0},{4,5},{5,6},{6,7},{7,4},{8,9},{9,10},{10,1... | collective-permute-start | bytes 393224 | tf_op jit(solution)/shard_map/ppermute | solution.py:33
  113.8 6.6 %collective-permute-start.29 = (bf16[128,512]{1,0:T(8,128)(2,1)S(1)}, bf16[128,512]{1,0:T(8,128)(2,1)S(1)}, u32[]{:S(2)}, u32[]{:S(2)}) collective-permute-start(bf16[128,512]{1,0:T(8,128)(2,1)S(1)} %slice.64), channel_id=1, source_target_pairs={{0,3},{1,0},{2,1},{3,2},{4,7},{5,4},{6,5},{7,6},{8,11},{9,8},{10,9... | collective-permute-start | bytes 393224 | tf_op jit(solution)/shard_map/ppermute | solution.py:33
  121.4 10.6 %collective-permute-start.31 = (bf16[384,256]{1,0:T(8,128)(2,1)S(1)}, bf16[384,256]{1,0:T(8,128)(2,1)S(1)}, u32[]{:S(2)}, u32[]{:S(2)}) collective-permute-start(bf16[384,256]{1,0:T(8,128)(2,1)S(1)} %get-tuple-element.15), channel_id=1, source_target_pairs={{8,16},{9,17},{10,18},{11,19},{12,20},{13,21},{14,22},{15,23},{16,... | collective-permute-start | bytes 589832 | tf_op jit(solution)/shard_map/ppermute | solution.py:33
  127.7 4.3 %collective-permute-start.32 = (bf16[384,256]{1,0:T(8,128)(2,1)S(1)}, bf16[384,256]{1,0:T(8,128)(2,1)S(1)}, u32[]{:S(2)}, u32[]{:S(2)}) collective-permute-start(bf16[384,256]{1,0:T(8,128)(2,1)S(1)} %get-tuple-element.16), channel_id=1, source_target_pairs={{0,8},{1,9},{2,10},{3,11},{4,12},{5,13},{6,14},{7,15},{8,0},{9,1},... | collective-permute-start | bytes 589832 | tf_op jit(solution)/shard_map/ppermute | solution.py:33
  (3 other events, 16.9 us)

commit v2 on v1

v2 whole, which is shorter than its diff:
```python
import functools

import jax
import jax.numpy as jnp
from jax import lax
from jax.experimental import pallas as pl
from jax.experimental.pallas import tpu as pltpu
from jax.sharding import PartitionSpec as P

TICKS = 3
AXES = ("layer", "row")
VMEM = pl.BlockSpec(memory_space=pltpu.VMEM)
SMEM = pl.BlockSpec(memory_space=pltpu.SMEM)
HBM = pl.BlockSpec(memory_space=pltpu.HBM)


def at_row(row, dx, dy):
    return (row ^ (4 * dx)) & 4 | (row + dy) & 3


def stay(layer):
    return layer


def near_layer(layer):
    return layer ^ 1


def far_layer(layer):
    return layer - 1 if layer % 2 == 0 else layer + 1


def permute(array, layers, rows, layer_to, dx, dy):
    pairs = [
        (layer * rows + row, layer_to(layer) * rows + at_row(row, dx, dy))
        for layer in range(layers)
        for row in range(rows)
        if 0 <= layer_to(layer) < layers
    ]
    return lax.ppermute(array, AXES, pairs)


def block_product(ops, near, far):
    count = near.shape[1] // 2
    near_re, near_im, far_re, far_im = near[:, :count], near[:, count:], far[:, :count], far[:, count:]
    lhs = jnp.concatenate([ops[part] for part in range(4)], axis=1)
    rhs = jnp.concatenate(
        [
            jnp.concatenate([far_re, far_im, near_re, near_im], axis=1),
            jnp.concatenate([-far_im, far_re, -near_im, near_re], axis=1),
            jnp.concatenate([near_re, near_im, far_re, far_im], axis=1),
            jnp.concatenate([-near_im, near_re, -far_im, far_re], axis=1),
        ],
        axis=0,
    )
    return jnp.dot(lhs, rhs, preferred_element_type=jnp.float32)


def halves_of(refs, swap):
    if len(refs) == 2:
        return refs[0][...], refs[1][...]
    half = refs[0].shape[1] // 2
    first, second = refs[0][:, :half], refs[0][:, half:]
    if swap is None:
        return first, second
    return jnp.where(swap, second, first), jnp.where(swap, first, second)


def stage_kernel(shifts, layout, parity, first, last, where, ops, *refs):
    refs = list(refs)
    blocks = []
    for parts in layout:
        blocks.append([])
        for count in parts:
            blocks[-1].append(refs[:count])
            refs = refs[count:]
    if not first:
        before, refs = refs[0], refs[1:]
    if last:
        sources, source_layer, near_out, far_out, op_buf, sems = refs
    else:
        total_out, op_buf, sems = refs
    rows = ops.shape[2]
    even = where[1] % 2 == 0
    copies = []
    for j, shift in enumerate(shifts):
        place = at_row(where[0], *shift)
        copy = pltpu.make_async_copy(
            ops.at[0, :, :, pl.ds(pl.multiple_of(place * rows, rows), rows)], op_buf.at[j], sems.at[j]
        )
        copy.start()
        copies.append(copy)
    total = None if first else before[...]
    for j, parts in enumerate(blocks):
        halves = [halves_of(part, even if parity else None) for part in parts]
        near, far = (jnp.concatenate(half, axis=0) for half in zip(*halves))
        copies[j].wait()
        term = block_product(op_buf.at[j], near, far)
        total = term if total is None else total + term
    if last:
        half = total.shape[1] // 2
        mask = (source_layer[...] == where[1]).astype(jnp.float32)
        mask = jnp.concatenate([mask, mask], axis=1)
        down, up = sources[:, :half].astype(jnp.float32) * mask, sources[:, half:].astype(jnp.float32) * mask
        near_out[...] = (total[:, :half] + jnp.where(even, down, up)).astype(jnp.bfloat16)
        far_out[...] = (total[:, half:] + jnp.where(even, up, down)).astype(jnp.bfloat16)
    else:
        total_out[...] = total


def stage(operators, where, blocks, parity=False, before=None, extra=None):
    rows = operators.shape[2]
    shifts = [shift for shift, _ in blocks]
    layout = [[len(part) for part in parts] for _, parts in blocks]
    flat = [array for _, parts in blocks for part in parts for array in part]
    width = sum(array.shape[1] for array in blocks[0][1][0])
    operands = [where, operators] + flat
    if before is not None:
        operands.append(before)
    if extra is not None:
        operands.extend(extra)
        out_shape = [jax.ShapeDtypeStruct((rows, width // 2), jnp.bfloat16)] * 2
        out_specs = [VMEM, VMEM]
    else:
        out_shape = jax.ShapeDtypeStruct((rows, width), jnp.float32)
        out_specs = VMEM
    n = len(blocks)
    return pl.pallas_call(
        functools.partial(stage_kernel, shifts, layout, parity, before is None, extra is not None),
        out_shape=out_shape,
        in_specs=[SMEM, HBM] + [VMEM] * (len(operands) - 2),
        out_specs=out_specs,
        scratch_shapes=[
            pltpu.VMEM((n, 4, rows, rows), jnp.bfloat16),
            pltpu.SemaphoreType.DMA((n,)),
        ],
        compiler_params=pltpu.CompilerParams(vmem_limit_bytes=48 * 2**20),
        cost_estimate=pl.CostEstimate(
            flops=2 * n * 4 * rows * rows * width,
            bytes_accessed=n * (4 * rows * rows + rows * width) * 2,
            transcendentals=0,
        ),
    )(*operands)


def join_kernel(near, far, out):
    half = near.shape[1]
    out[:, :half] = near[...]
    out[:, half:] = far[...]


def join(near, far):
    return pl.pallas_call(
        join_kernel,
        out_shape=jax.ShapeDtypeStruct((near.shape[0], 2 * near.shape[1]), near.dtype),
        in_specs=[VMEM, VMEM],
        out_specs=VMEM,
        compiler_params=pltpu.CompilerParams(vmem_limit_bytes=2 * 2**20),
    )(near, far)


def finish_kernel(where, near, far, out):
    half = near.shape[1]
    even = where[1] % 2 == 0
    out[0, :, :half] = jnp.where(even, far[...], near[...])
    out[0, :, half:] = jnp.where(even, near[...], far[...])


def finish(where, near, far):
    return pl.pallas_call(
        finish_kernel,
        out_shape=jax.ShapeDtypeStruct((1, near.shape[0], 2 * near.shape[1]), near.dtype),
        in_specs=[SMEM, VMEM, VMEM],
        out_specs=VMEM,
        compiler_params=pltpu.CompilerParams(vmem_limit_bytes=2 * 2**20),
    )(where, near, far)


def per_device(layers, rows, waves, operators, sources, source_layer):
    third = operators.shape[2] // 3
    where = jnp.stack([lax.axis_index("row"), lax.axis_index("layer")]).astype(jnp.int32)
    source_layer = source_layer.reshape(1, -1)

    def move(array, dx, dy):
        return permute(array, layers, rows, stay, dx, dy)

    outs = None
    for tick in range(TICKS):
        if outs is None:
            own = [waves[0]]
            below, across, above = [move(own[0], 0, -1)], [move(own[0], 1, 0)], [move(own[0], 0, 1)]
            below_whole, across_whole = below[0], across[0]
        else:
            targets = ((0, -1), (1, 0), (0, 1), (0, 0))
            below, across, above, own = (
                [permute(out, layers, rows, to, *shift) for out, to in zip(outs, (near_layer, far_layer))]
                for shift in targets
            )
            below_whole, across_whole = join(*below), join(*across)
        far_y = move(below_whole, 0, -1)
        across_below = move(below_whole, 1, 0)
        across_above = move(across_whole, 0, 1)
        part0 = move(far_y[:third], 1, 0)
        part1 = move(across_above[third : 2 * third], 0, 1)
        part2 = move(across_below[2 * third :], 0, -1)
        total = stage(
            operators,
            where,
            [((0, 0), [own]), ((0, 1), [below]), ((1, 0), [across]), ((0, -1), [above])],
            parity=tick == 0,
        )
        total = stage(
            operators,
            where,
            [((0, 2), [[far_y]]), ((1, 1), [[across_below]]), ((1, -1), [[across_above]])],
            parity=tick == 0,
            before=total,
        )
        outs = stage(
            operators,
            where,
            [((1, 2), [[part0], [part1], [part2]])],
            parity=tick == 0,
            before=total,
            extra=(sources, source_layer),
        )
    near_in = permute(outs[0], layers, rows, near_layer, 0, 0)
    far_in = permute(outs[1], layers, rows, far_layer, 0, 0)
    return finish(where, near_in, far_in)


def solution(mesh):
    return jax.shard_map(
        functools.partial(per_device, mesh.shape["layer"], mesh.shape["row"]),
        mesh=mesh,
        in_specs=(P("layer", "row", None), P("layer", None, "row", None), P("row", None), P()),
        out_specs=P("layer", "row", None),
        check_vma=False,
    )
```

time: 133 us -> 146 us (1.098)
  starting transfers between devices: 53.8 us -> 80 us
  waiting for transfers between devices: 43.3 us -> 27.2 us
  Pallas kernels: 25.6 us -> 36.1 us
  other arithmetic: 4.88 us -> 0.07 us
  local copies, waits for them, and re-layouts: 4.91 us -> 1.1 us
    ppermute x33 -> x39, starting transfers between devices: 53.8 us -> 80 us  [permute(): return lax.ppermute(array, AXES, pairs)]
    ppermute x33 -> x39, waiting for transfers between devices: 43.3 us -> 27.2 us  [permute(): return lax.ppermute(array, AXES, pairs)]
    pallas_call x9 -> x14, Pallas kernels: 25.6 us -> 36.1 us  [the longest x9 34.7 us: stage(): pl.pallas_call(functools.partial(stage_kernel, shifts, layout, parity, be...]
    select_n x3 -> x0, other arithmetic: 3.05 us -> none  [the longest x2 1.93 us: swap_if_even(): return jnp.where(even, swapped, array)]
    unnamed x6, local copies, waits for them, and re-layouts: 3.72 us -> 1.01 us
  transfers between devices with their start and end apart: 33 -> 39, of which waited for: 11 -> 10; matrix products, arithmetic and copies ran while one was open for 2% -> 0% of each run, Pallas kernels for 17% -> 19%
where the time goes in v2:
time: 146 us; the launch traced here: 145 us
  starting transfers between devices  80 us (55%)
  Pallas kernels  36.1 us (25%)
  waiting for transfers between devices  27.2 us (19%)
    ppermute x39, starting transfers between devices, permute(): return lax.ppermute(array, AXES, pairs)  80 us
    pallas_call x9, Pallas kernels, stage(): pl.pallas_call(functools.partial(stage_kernel, shifts, layout, parity, be...  34.7 us
    ppermute x39, waiting for transfers between devices, permute(): return lax.ppermute(array, AXES, pairs)  27.2 us
  transfers between devices with their start and end apart: 39, of which 10 were waited for; matrix products, arithmetic and copies ran while one was open for 0% of the time, Pallas kernels for 19%

profile of v2, /device:TPU:6, one launch (start us, length us, event | category | flops | bytes accessed | tf_op | source)
XLA Modules:
  0.0 144.9 jit_solution(9376940196440132012)
XLA Ops:
  0.0 3.0 %collective-permute-start = (bf16[384,512]{1,0:T(8,128)(2,1)}, bf16[384,512]{1,0:T(8,128)(2,1)S(1)}, u32[]{:S(2)}, u32[]{:S(2)}) collective-permute-start(bf16[384,512]{1,0:T(8,128)(2,1)} %bitcast.4), channel_id=1, source_target_pairs={{0,3},{1,0},{2,1},{3,2},{4,7},{5,4},{6,5},{7,6},{8,11},{9,8},{10,9... | collective-permute-start | bytes 1179656 | tf_op jit(solution)/shard_map/ppermute | solution.py:40
  3.8 7.9 %collective-permute-done.refs_1_ = bf16[384,512]{1,0:T(8,128)(2,1)S(1)} collective-permute-done((bf16[384,512]{1,0:T(8,128)(2,1)}, bf16[384,512]{1,0:T(8,128)(2,1)S(1)}, u32[]{:S(2)}, u32[]{:S(2)}) %collective-permute-start) | collective-permute-done | bytes 393248 | tf_op jit(solution)/shard_map/ppermute | solution.py:40
  11.7 3.6 %collective-permute-start.1 = (bf16[384,512]{1,0:T(8,128)(2,1)S(1)}, bf16[384,512]{1,0:T(8,128)(2,1)S(1)}, u32[]{:S(2)}, u32[]{:S(2)}) collective-permute-start(bf16[384,512]{1,0:T(8,128)(2,1)S(1)} %collective-permute-done.refs_1_), channel_id=1, source_target_pairs={{0,3},{1,0},{2,1},{3,2},{4,7},{5,4},{6,5},{7,6},{8,11},{9,8},{10,9... | collective-permute-start | bytes 1179656 | tf_op jit(solution)/shard_map/ppermute | solution.py:40
  17.2 5.0 %shard_map.46.refs_3_ = f32[384,512]{1,0:T(8,128)S(1)} custom-call(s32[2]{0:T(128)S(1)} %pad_add_fusion.where, bf16[1,4,384,3072]{3,2,1,0:T(8,128)(2,1)} %ops.17, bf16[384,512]{1,0:T(8,128)(2,1)S(1)} %bitcast.7, bf16[384,512]{1,0:T(8,128)(2,1)S(1)} %collective-permute-done.refs_1_, bf16[384,512]{1,0:T(8,128)(2,1)S(1)} %collective-permute-done.3.refs_2_, ...), custom_call_target="tpu_custom_call" | custom-call | flops 2415919104 | bytes 6291456 | tf_op jit(solution)/shard_map/pallas_call | solution.py:128
  23.7 2.7 %collective-permute-done.6.refs_1_ = bf16[384,512]{1,0:T(8,128)(2,1)S(1)} collective-permute-done((bf16[384,512]{1,0:T(8,128)(2,1)S(1)}, bf16[384,512]{1,0:T(8,128)(2,1)S(1)}, u32[]{:S(2)}, u32[]{:S(2)}) %collective-permute-start.6) | collective-permute-done | bytes 393248 | tf_op jit(solution)/shard_map/ppermute | solution.py:40
  28.6 4.0 %shard_map.47.refs_3_ = f32[384,512]{1,0:T(8,128)S(1)} custom-call(s32[2]{0:T(128)S(1)} %pad_add_fusion.where, bf16[1,4,384,3072]{3,2,1,0:T(8,128)(2,1)} %ops.17, bf16[384,512]{1,0:T(8,128)(2,1)S(1)} %collective-permute-done.1.refs_0_, bf16[384,512]{1,0:T(8,128)(2,1)S(1)} %collective-permute-done.6.refs_1_, ...), custom_call_target="tpu_custom_call" | custom-call | flops 1811939328 | bytes 4718592 | tf_op jit(solution)/shard_map/pallas_call | solution.py:128
  33.8 2.6 %shard_map.48 = (bf16[384,256]{1,0:T(8,128)(2,1)S(1)}, bf16[384,256]{1,0:T(8,128)(2,1)S(1)}) custom-call(s32[2]{0:T(128)S(1)} %pad_add_fusion.where, bf16[1,4,384,3072]{3,2,1,0:T(8,128)(2,1)} %ops.17, bf16[128,512]{1,0:T(8,128)(2,1)S(1)} %collective-permute-done.2.refs_0_, bf16[128,512]{1,0:T(8,128)(2,1)S(1)} %collective-permute-done.5.refs_1_, ...), custom_call_target="tpu_custom_call" | custom-call | flops 603979776 | bytes 1572864 | tf_op jit(solution)/shard_map/pallas_call | solution.py:128
  36.4 5.7 %collective-permute-start.10 = (bf16[384,256]{1,0:T(8,128)(2,1)S(1)}, bf16[384,256]{1,0:T(8,128)(2,1)S(1)}, u32[]{:S(2)}, u32[]{:S(2)}) collective-permute-start(bf16[384,256]{1,0:T(8,128)(2,1)S(1)} %get-tuple-element.12), channel_id=1, source_target_pairs={{8,19},{9,16},{10,17},{11,18},{12,23},{13,20},{14,21},{15,22},{16,... | collective-permute-start | bytes 589832 | tf_op jit(solution)/shard_map/ppermute | solution.py:40
  42.2 4.8 %collective-permute-start.14 = (bf16[384,256]{1,0:T(8,128)(2,1)S(1)}, bf16[384,256]{1,0:T(8,128)(2,1)S(1)}, u32[]{:S(2)}, u32[]{:S(2)}) collective-permute-start(bf16[384,256]{1,0:T(8,128)(2,1)S(1)} %get-tuple-element.12), channel_id=1, source_target_pairs={{8,20},{9,21},{10,22},{11,23},{12,16},{13,17},{14,18},{15,19},{16,... | collective-permute-start | bytes 589832 | tf_op jit(solution)/shard_map/ppermute | solution.py:40
  48.3 5.7 %collective-permute-start.20 = (bf16[384,256]{1,0:T(8,128)(2,1)S(1)}, bf16[384,256]{1,0:T(8,128)(2,1)S(1)}, u32[]{:S(2)}, u32[]{:S(2)}) collective-permute-start(bf16[384,256]{1,0:T(8,128)(2,1)S(1)} %get-tuple-element.12), channel_id=1, source_target_pairs={{8,16},{9,17},{10,18},{11,19},{12,20},{13,21},{14,22},{15,23},{16,... | collective-permute-start | bytes 589832 | tf_op jit(solution)/shard_map/ppermute | solution.py:40
  54.3 3.8 %collective-permute-start.22 = (bf16[384,256]{1,0:T(8,128)(2,1)S(1)}, bf16[384,256]{1,0:T(8,128)(2,1)S(1)}, u32[]{:S(2)}, u32[]{:S(2)}) collective-permute-start(bf16[384,256]{1,0:T(8,128)(2,1)S(1)} %get-tuple-element.12), channel_id=1, source_target_pairs={{8,17},{9,18},{10,19},{11,16},{12,21},{13,22},{14,23},{15,20},{16,... | collective-permute-start | bytes 589832 | tf_op jit(solution)/shard_map/ppermute | solution.py:40
  59.0 2.7 %collective-permute-start.11 = (bf16[384,512]{1,0:T(8,128)(2,1)S(1)}, bf16[384,512]{1,0:T(8,128)(2,1)S(1)}, u32[]{:S(2)}, u32[]{:S(2)}) collective-permute-start(bf16[384,512]{1,0:T(8,128)(2,1)S(1)} %shard_map.49), channel_id=1, source_target_pairs={{0,3},{1,0},{2,1},{3,2},{4,7},{5,4},{6,5},{7,6},{8,11},{9,8},{10,9... | collective-permute-start | bytes 1179656 | tf_op jit(solution)/shard_map/ppermute | solution.py:40
  62.5 2.3 %collective-permute-done.21.refs_6_ = bf16[384,256]{1,0:T(8,128)(2,1)S(1)} collective-permute-done((bf16[384,256]{1,0:T(8,128)(2,1)S(1)}, bf16[384,256]{1,0:T(8,128)(2,1)S(1)}, u32[]{:S(2)}, u32[]{:S(2)}) %collective-permute-start.21) | collective-permute-done | bytes 196640 | tf_op jit(solution)/shard_map/ppermute | solution.py:40
  64.8 2.4 %collective-permute-done.22.refs_7_ = bf16[384,256]{1,0:T(8,128)(2,1)S(1)} collective-permute-done((bf16[384,256]{1,0:T(8,128)(2,1)S(1)}, bf16[384,256]{1,0:T(8,128)(2,1)S(1)}, u32[]{:S(2)}, u32[]{:S(2)}) %collective-permute-start.22) | collective-permute-done | bytes 196640 | tf_op jit(solution)/shard_map/ppermute | solution.py:40
  67.2 5.0 %shard_map.51.refs_3_ = f32[384,512]{1,0:T(8,128)S(1)} custom-call(s32[2]{0:T(128)S(1)} %pad_add_fusion.where, bf16[1,4,384,3072]{3,2,1,0:T(8,128)(2,1)} %ops.17, bf16[384,256]{1,0:T(8,128)(2,1)S(1)} %collective-permute-done.19.refs_0_, bf16[384,256]{1,0:T(8,128)(2,1)S(1)} %collective-permute-done.20.refs_1_, ...), custom_call_target="tpu_custom_call" | custom-call | flops 2415919104 | bytes 6291456 | tf_op jit(solution)/shard_map/pallas_call | solution.py:128
  72.2 2.9 %collective-permute-done.15.refs_2_ = bf16[384,512]{1,0:T(8,128)(2,1)S(1)} collective-permute-done((bf16[384,512]{1,0:T(8,128)(2,1)S(1)}, bf16[384,512]{1,0:T(8,128)(2,1)S(1)}, u32[]{:S(2)}, u32[]{:S(2)}) %collective-permute-start.15) | collective-permute-done | bytes 393248 | tf_op jit(solution)/shard_map/ppermute | solution.py:40
  76.3 3.3 %collective-permute-start.18 = (bf16[128,512]{1,0:T(8,128)(2,1)S(1)}, bf16[128,512]{1,0:T(8,128)(2,1)S(1)}, u32[]{:S(2)}, u32[]{:S(2)}) collective-permute-start(bf16[128,512]{1,0:T(8,128)(2,1)S(1)} %slice.41), channel_id=1, source_target_pairs={{0,3},{1,0},{2,1},{3,2},{4,7},{5,4},{6,5},{7,6},{8,11},{9,8},{10,9... | collective-permute-start | bytes 393224 | tf_op jit(solution)/shard_map/ppermute | solution.py:40
  79.6 4.0 %shard_map.52.refs_3_ = f32[384,512]{1,0:T(8,128)S(1)} custom-call(s32[2]{0:T(128)S(1)} %pad_add_fusion.where, bf16[1,4,384,3072]{3,2,1,0:T(8,128)(2,1)} %ops.17, bf16[384,512]{1,0:T(8,128)(2,1)S(1)} %collective-permute-done.11.refs_0_, bf16[384,512]{1,0:T(8,128)(2,1)S(1)} %collective-permute-done.17.refs_1_, ...), custom_call_target="tpu_custom_call" | custom-call | flops 1811939328 | bytes 4718592 | tf_op jit(solution)/shard_map/pallas_call | solution.py:128
  83.6 2.6 %shard_map.53 = (bf16[384,256]{1,0:T(8,128)(2,1)S(1)}, bf16[384,256]{1,0:T(8,128)(2,1)S(1)}) custom-call(s32[2]{0:T(128)S(1)} %pad_add_fusion.where, bf16[1,4,384,3072]{3,2,1,0:T(8,128)(2,1)} %ops.17, bf16[128,512]{1,0:T(8,128)(2,1)S(1)} %collective-permute-done.12.refs_0_, bf16[128,512]{1,0:T(8,128)(2,1)S(1)} %collective-permute-done.16.refs_1_, ...), custom_call_target="tpu_custom_call" | custom-call | flops 603979776 | bytes 1572864 | tf_op jit(solution)/shard_map/pallas_call | solution.py:128
  86.4 2.9 %collective-permute-start.27 = (bf16[384,256]{1,0:T(8,128)(2,1)S(1)}, bf16[384,256]{1,0:T(8,128)(2,1)S(1)}, u32[]{:S(2)}, u32[]{:S(2)}) collective-permute-start(bf16[384,256]{1,0:T(8,128)(2,1)S(1)} %get-tuple-element.13), channel_id=1, source_target_pairs={{0,12},{1,13},{2,14},{3,15},{4,8},{5,9},{6,10},{7,11},{8,4},{9,5},... | collective-permute-start | bytes 589832 | tf_op jit(solution)/shard_map/ppermute | solution.py:40
  89.2 2.0 %collective-permute-start.28 = (bf16[384,256]{1,0:T(8,128)(2,1)S(1)}, bf16[384,256]{1,0:T(8,128)(2,1)S(1)}, u32[]{:S(2)}, u32[]{:S(2)}) collective-permute-start(bf16[384,256]{1,0:T(8,128)(2,1)S(1)} %get-tuple-element.14), channel_id=1, source_target_pairs={{8,20},{9,21},{10,22},{11,23},{12,16},{13,17},{14,18},{15,19},{16,... | collective-permute-start | bytes 589832 | tf_op jit(solution)/shard_map/ppermute | solution.py:40
  91.2 5.6 %collective-permute-start.24 = (bf16[384,256]{1,0:T(8,128)(2,1)S(1)}, bf16[384,256]{1,0:T(8,128)(2,1)S(1)}, u32[]{:S(2)}, u32[]{:S(2)}) collective-permute-start(bf16[384,256]{1,0:T(8,128)(2,1)S(1)} %get-tuple-element.14), channel_id=1, source_target_pairs={{8,19},{9,16},{10,17},{11,18},{12,23},{13,20},{14,21},{15,22},{16,... | collective-permute-start | bytes 589832 | tf_op jit(solution)/shard_map/ppermute | solution.py:40
  96.9 5.2 %collective-permute-start.34 = (bf16[384,256]{1,0:T(8,128)(2,1)S(1)}, bf16[384,256]{1,0:T(8,128)(2,1)S(1)}, u32[]{:S(2)}, u32[]{:S(2)}) collective-permute-start(bf16[384,256]{1,0:T(8,128)(2,1)S(1)} %get-tuple-element.14), channel_id=1, source_target_pairs={{8,16},{9,17},{10,18},{11,19},{12,20},{13,21},{14,22},{15,23},{16,... | collective-permute-start | bytes 589832 | tf_op jit(solution)/shard_map/ppermute | solution.py:40
  102.2 6.0 %collective-permute-start.36 = (bf16[384,256]{1,0:T(8,128)(2,1)S(1)}, bf16[384,256]{1,0:T(8,128)(2,1)S(1)}, u32[]{:S(2)}, u32[]{:S(2)}) collective-permute-start(bf16[384,256]{1,0:T(8,128)(2,1)S(1)} %get-tuple-element.14), channel_id=1, source_target_pairs={{8,17},{9,18},{10,19},{11,16},{12,21},{13,22},{14,23},{15,20},{16,... | collective-permute-start | bytes 589832 | tf_op jit(solution)/shard_map/ppermute | solution.py:40
  108.4 3.5 %collective-permute-start.25 = (bf16[384,512]{1,0:T(8,128)(2,1)S(1)}, bf16[384,512]{1,0:T(8,128)(2,1)S(1)}, u32[]{:S(2)}, u32[]{:S(2)}) collective-permute-start(bf16[384,512]{1,0:T(8,128)(2,1)S(1)} %shard_map.54), channel_id=1, source_target_pairs={{0,3},{1,0},{2,1},{3,2},{4,7},{5,4},{6,5},{7,6},{8,11},{9,8},{10,9... | collective-permute-start | bytes 1179656 | tf_op jit(solution)/shard_map/ppermute | solution.py:40
  113.0 2.0 %collective-permute-done.36.refs_7_ = bf16[384,256]{1,0:T(8,128)(2,1)S(1)} collective-permute-done((bf16[384,256]{1,0:T(8,128)(2,1)S(1)}, bf16[384,256]{1,0:T(8,128)(2,1)S(1)}, u32[]{:S(2)}, u32[]{:S(2)}) %collective-permute-start.36) | collective-permute-done | bytes 196640 | tf_op jit(solution)/shard_map/ppermute | solution.py:40
  115.0 5.0 %shard_map.56.refs_3_ = f32[384,512]{1,0:T(8,128)S(1)} custom-call(s32[2]{0:T(128)S(1)} %pad_add_fusion.where, bf16[1,4,384,3072]{3,2,1,0:T(8,128)(2,1)} %ops.17, bf16[384,256]{1,0:T(8,128)(2,1)S(1)} %collective-permute-done.33.refs_0_, bf16[384,256]{1,0:T(8,128)(2,1)S(1)} %collective-permute-done.34.refs_1_, ...), custom_call_target="tpu_custom_call" | custom-call | flops 2415919104 | bytes 6291456 | tf_op jit(solution)/shard_map/pallas_call | solution.py:128
  123.3 3.0 %collective-permute-start.32 = (bf16[128,512]{1,0:T(8,128)(2,1)S(1)}, bf16[128,512]{1,0:T(8,128)(2,1)S(1)}, u32[]{:S(2)}, u32[]{:S(2)}) collective-permute-start(bf16[128,512]{1,0:T(8,128)(2,1)S(1)} %slice.44), channel_id=1, source_target_pairs={{0,3},{1,0},{2,1},{3,2},{4,7},{5,4},{6,5},{7,6},{8,11},{9,8},{10,9... | collective-permute-start | bytes 393224 | tf_op jit(solution)/shard_map/ppermute | solution.py:40
  126.2 4.0 %shard_map.57.refs_3_ = f32[384,512]{1,0:T(8,128)S(1)} custom-call(s32[2]{0:T(128)S(1)} %pad_add_fusion.where, bf16[1,4,384,3072]{3,2,1,0:T(8,128)(2,1)} %ops.17, bf16[384,512]{1,0:T(8,128)(2,1)S(1)} %collective-permute-done.25.refs_0_, bf16[384,512]{1,0:T(8,128)(2,1)S(1)} %collective-permute-done.31.refs_1_, ...), custom_call_target="tpu_custom_call" | custom-call | flops 1811939328 | bytes 4718592 | tf_op jit(solution)/shard_map/pallas_call | solution.py:128
  130.3 2.6 %shard_map.58 = (bf16[384,256]{1,0:T(8,128)(2,1)S(1)}, bf16[384,256]{1,0:T(8,128)(2,1)S(1)}) custom-call(s32[2]{0:T(128)S(1)} %pad_add_fusion.where, bf16[1,4,384,3072]{3,2,1,0:T(8,128)(2,1)} %ops.17, bf16[128,512]{1,0:T(8,128)(2,1)S(1)} %collective-permute-done.26.refs_0_, bf16[128,512]{1,0:T(8,128)(2,1)S(1)} %collective-permute-done.30.refs_1_, ...), custom_call_target="tpu_custom_call" | custom-call | flops 603979776 | bytes 1572864 | tf_op jit(solution)/shard_map/pallas_call | solution.py:128
  133.0 7.1 %collective-permute-start.38 = (bf16[384,256]{1,0:T(8,128)(2,1)S(1)}, bf16[384,256]{1,0:T(8,128)(2,1)S(1)}, u32[]{:S(2)}, u32[]{:S(2)}) collective-permute-start(bf16[384,256]{1,0:T(8,128)(2,1)S(1)} %get-tuple-element.16), channel_id=1, source_target_pairs={{8,16},{9,17},{10,18},{11,19},{12,20},{13,21},{14,22},{15,23},{16,... | collective-permute-start | bytes 589832 | tf_op jit(solution)/shard_map/ppermute | solution.py:40
  140.1 3.5 %collective-permute-done.38.far = bf16[384,256]{1,0:T(8,128)(2,1)S(1)} collective-permute-done((bf16[384,256]{1,0:T(8,128)(2,1)S(1)}, bf16[384,256]{1,0:T(8,128)(2,1)S(1)}, u32[]{:S(2)}, u32[]{:S(2)}) %collective-permute-start.38) | collective-permute-done | bytes 196640 | tf_op jit(solution)/shard_map/ppermute | solution.py:40
  (76 shorter events, 18.4 us)
Async XLA Ops:
  0.0 11.7 %collective-permute-start = (bf16[384,512]{1,0:T(8,128)(2,1)}, bf16[384,512]{1,0:T(8,128)(2,1)S(1)}, u32[]{:S(2)}, u32[]{:S(2)}) collective-permute-start(bf16[384,512]{1,0:T(8,128)(2,1)} %bitcast.4), channel_id=1, source_target_pairs={{0,3},{1,0},{2,1},{3,2},{4,7},{5,4},{6,5},{7,6},{8,11},{9,8},{10,9... | collective-permute-start | bytes 1179656 | tf_op jit(solution)/shard_map/ppermute | solution.py:40
  3.0 13.1 %collective-permute-start.3 = (bf16[384,512]{1,0:T(8,128)(2,1)}, bf16[384,512]{1,0:T(8,128)(2,1)S(1)}, u32[]{:S(2)}, u32[]{:S(2)}) collective-permute-start(bf16[384,512]{1,0:T(8,128)(2,1)} %bitcast.5), channel_id=1, source_target_pairs={{0,4},{1,5},{2,6},{3,7},{4,0},{5,1},{6,2},{7,3},{8,12},{9,13},{10,... | collective-permute-start | bytes 1179656 | tf_op jit(solution)/shard_map/ppermute | solution.py:40
  3.8 12.4 %collective-permute-start.8 = (bf16[384,512]{1,0:T(8,128)(2,1)}, bf16[384,512]{1,0:T(8,128)(2,1)S(1)}, u32[]{:S(2)}, u32[]{:S(2)}) collective-permute-start(bf16[384,512]{1,0:T(8,128)(2,1)} %bitcast.6), channel_id=1, source_target_pairs={{0,1},{1,2},{2,3},{3,0},{4,5},{5,6},{6,7},{7,4},{8,9},{9,10},{10,1... | collective-permute-start | bytes 1179656 | tf_op jit(solution)/shard_map/ppermute | solution.py:40
  11.7 11.1 %collective-permute-start.1 = (bf16[384,512]{1,0:T(8,128)(2,1)S(1)}, bf16[384,512]{1,0:T(8,128)(2,1)S(1)}, u32[]{:S(2)}, u32[]{:S(2)}) collective-permute-start(bf16[384,512]{1,0:T(8,128)(2,1)S(1)} %collective-permute-done.refs_1_), channel_id=1, source_target_pairs={{0,3},{1,0},{2,1},{3,2},{4,7},{5,4},{6,5},{7,6},{8,11},{9,8},{10,9... | collective-permute-start | bytes 1179656 | tf_op jit(solution)/shard_map/ppermute | solution.py:40
  15.3 11.1 %collective-permute-start.6 = (bf16[384,512]{1,0:T(8,128)(2,1)S(1)}, bf16[384,512]{1,0:T(8,128)(2,1)S(1)}, u32[]{:S(2)}, u32[]{:S(2)}) collective-permute-start(bf16[384,512]{1,0:T(8,128)(2,1)S(1)} %collective-permute-done.refs_1_), channel_id=1, source_target_pairs={{0,4},{1,5},{2,6},{3,7},{4,0},{5,1},{6,2},{7,3},{8,12},{9,13},{10,... | collective-permute-start | bytes 1179656 | tf_op jit(solution)/shard_map/ppermute | solution.py:40
  16.1 11.4 %collective-permute-start.4 = (bf16[384,512]{1,0:T(8,128)(2,1)S(1)}, bf16[384,512]{1,0:T(8,128)(2,1)S(1)}, u32[]{:S(2)}, u32[]{:S(2)}) collective-permute-start(bf16[384,512]{1,0:T(8,128)(2,1)S(1)} %collective-permute-done.3.refs_2_), channel_id=1, source_target_pairs={{0,1},{1,2},{2,3},{3,0},{4,5},{5,6},{6,7},{7,4},{8,9},{9,10},{10,1... | collective-permute-start | bytes 1179656 | tf_op jit(solution)/shard_map/ppermute | solution.py:40
  22.8 9.8 %collective-permute-start.2 = (bf16[128,512]{1,0:T(8,128)(2,1)S(1)}, bf16[128,512]{1,0:T(8,128)(2,1)S(1)}, u32[]{:S(2)}, u32[]{:S(2)}) collective-permute-start(bf16[128,512]{1,0:T(8,128)(2,1)S(1)} %slice.36), channel_id=1, source_target_pairs={{0,4},{1,5},{2,6},{3,7},{4,0},{5,1},{6,2},{7,3},{8,12},{9,13},{10,... | collective-permute-start | bytes 393224 | tf_op jit(solution)/shard_map/ppermute | solution.py:40
  36.4 11.9 %collective-permute-start.10 = (bf16[384,256]{1,0:T(8,128)(2,1)S(1)}, bf16[384,256]{1,0:T(8,128)(2,1)S(1)}, u32[]{:S(2)}, u32[]{:S(2)}) collective-permute-start(bf16[384,256]{1,0:T(8,128)(2,1)S(1)} %get-tuple-element.12), channel_id=1, source_target_pairs={{8,19},{9,16},{10,17},{11,18},{12,23},{13,20},{14,21},{15,22},{16,... | collective-permute-start | bytes 589832 | tf_op jit(solution)/shard_map/ppermute | solution.py:40
  42.1 12.0 %collective-permute-start.13 = (bf16[384,256]{1,0:T(8,128)(2,1)S(1)}, bf16[384,256]{1,0:T(8,128)(2,1)S(1)}, u32[]{:S(2)}, u32[]{:S(2)}) collective-permute-start(bf16[384,256]{1,0:T(8,128)(2,1)S(1)} %get-tuple-element.11), channel_id=1, source_target_pairs={{0,12},{1,13},{2,14},{3,15},{4,8},{5,9},{6,10},{7,11},{8,4},{9,5},... | collective-permute-start | bytes 589832 | tf_op jit(solution)/shard_map/ppermute | solution.py:40
  42.2 12.1 %collective-permute-start.14 = (bf16[384,256]{1,0:T(8,128)(2,1)S(1)}, bf16[384,256]{1,0:T(8,128)(2,1)S(1)}, u32[]{:S(2)}, u32[]{:S(2)}) collective-permute-start(bf16[384,256]{1,0:T(8,128)(2,1)S(1)} %get-tuple-element.12), channel_id=1, source_target_pairs={{8,20},{9,21},{10,22},{11,23},{12,16},{13,17},{14,18},{15,19},{16,... | collective-permute-start | bytes 589832 | tf_op jit(solution)/shard_map/ppermute | solution.py:40
  47.0 11.2 %collective-permute-start.9 = (bf16[384,256]{1,0:T(8,128)(2,1)S(1)}, bf16[384,256]{1,0:T(8,128)(2,1)S(1)}, u32[]{:S(2)}, u32[]{:S(2)}) collective-permute-start(bf16[384,256]{1,0:T(8,128)(2,1)S(1)} %get-tuple-element.11), channel_id=1, source_target_pairs={{0,11},{1,8},{2,9},{3,10},{4,15},{5,12},{6,13},{7,14},{8,3},{9,0},... | collective-permute-start | bytes 589832 | tf_op jit(solution)/shard_map/ppermute | solution.py:40
  47.1 11.8 %collective-permute-start.19 = (bf16[384,256]{1,0:T(8,128)(2,1)S(1)}, bf16[384,256]{1,0:T(8,128)(2,1)S(1)}, u32[]{:S(2)}, u32[]{:S(2)}) collective-permute-start(bf16[384,256]{1,0:T(8,128)(2,1)S(1)} %get-tuple-element.11), channel_id=1, source_target_pairs={{0,8},{1,9},{2,10},{3,11},{4,12},{5,13},{6,14},{7,15},{8,0},{9,1},... | collective-permute-start | bytes 589832 | tf_op jit(solution)/shard_map/ppermute | solution.py:40
  48.3 13.3 %collective-permute-start.20 = (bf16[384,256]{1,0:T(8,128)(2,1)S(1)}, bf16[384,256]{1,0:T(8,128)(2,1)S(1)}, u32[]{:S(2)}, u32[]{:S(2)}) collective-permute-start(bf16[384,256]{1,0:T(8,128)(2,1)S(1)} %get-tuple-element.12), channel_id=1, source_target_pairs={{8,16},{9,17},{10,18},{11,19},{12,20},{13,21},{14,22},{15,23},{16,... | collective-permute-start | bytes 589832 | tf_op jit(solution)/shard_map/ppermute | solution.py:40
  54.1 10.8 %collective-permute-start.21 = (bf16[384,256]{1,0:T(8,128)(2,1)S(1)}, bf16[384,256]{1,0:T(8,128)(2,1)S(1)}, u32[]{:S(2)}, u32[]{:S(2)}) collective-permute-start(bf16[384,256]{1,0:T(8,128)(2,1)S(1)} %get-tuple-element.11), channel_id=1, source_target_pairs={{0,9},{1,10},{2,11},{3,8},{4,13},{5,14},{6,15},{7,12},{8,1},{9,2},... | collective-permute-start | bytes 589832 | tf_op jit(solution)/shard_map/ppermute | solution.py:40
  54.3 12.9 %collective-permute-start.22 = (bf16[384,256]{1,0:T(8,128)(2,1)S(1)}, bf16[384,256]{1,0:T(8,128)(2,1)S(1)}, u32[]{:S(2)}, u32[]{:S(2)}) collective-permute-start(bf16[384,256]{1,0:T(8,128)(2,1)S(1)} %get-tuple-element.12), channel_id=1, source_target_pairs={{8,17},{9,18},{10,19},{11,16},{12,21},{13,22},{14,23},{15,20},{16,... | collective-permute-start | bytes 589832 | tf_op jit(solution)/shard_map/ppermute | solution.py:40
  58.2 16.8 %collective-permute-start.15 = (bf16[384,512]{1,0:T(8,128)(2,1)S(1)}, bf16[384,512]{1,0:T(8,128)(2,1)S(1)}, u32[]{:S(2)}, u32[]{:S(2)}) collective-permute-start(bf16[384,512]{1,0:T(8,128)(2,1)S(1)} %shard_map.50), channel_id=1, source_target_pairs={{0,1},{1,2},{2,3},{3,0},{4,5},{5,6},{6,7},{7,4},{8,9},{9,10},{10,1... | collective-permute-start | bytes 1179656 | tf_op jit(solution)/shard_map/ppermute | solution.py:40
  59.0 16.2 %collective-permute-start.11 = (bf16[384,512]{1,0:T(8,128)(2,1)S(1)}, bf16[384,512]{1,0:T(8,128)(2,1)S(1)}, u32[]{:S(2)}, u32[]{:S(2)}) collective-permute-start(bf16[384,512]{1,0:T(8,128)(2,1)S(1)} %shard_map.49), channel_id=1, source_target_pairs={{0,3},{1,0},{2,1},{3,2},{4,7},{5,4},{6,5},{7,6},{8,11},{9,8},{10,9... | collective-permute-start | bytes 1179656 | tf_op jit(solution)/shard_map/ppermute | solution.py:40
  61.6 14.6 %collective-permute-start.17 = (bf16[384,512]{1,0:T(8,128)(2,1)S(1)}, bf16[384,512]{1,0:T(8,128)(2,1)S(1)}, u32[]{:S(2)}, u32[]{:S(2)}) collective-permute-start(bf16[384,512]{1,0:T(8,128)(2,1)S(1)} %shard_map.49), channel_id=1, source_target_pairs={{0,4},{1,5},{2,6},{3,7},{4,0},{5,1},{6,2},{7,3},{8,12},{9,13},{10,... | collective-permute-start | bytes 1179656 | tf_op jit(solution)/shard_map/ppermute | solution.py:40
  75.1 8.5 %collective-permute-start.16 = (bf16[128,512]{1,0:T(8,128)(2,1)S(1)}, bf16[128,512]{1,0:T(8,128)(2,1)S(1)}, u32[]{:S(2)}, u32[]{:S(2)}) collective-permute-start(bf16[128,512]{1,0:T(8,128)(2,1)S(1)} %slice.40), channel_id=1, source_target_pairs={{0,1},{1,2},{2,3},{3,0},{4,5},{5,6},{6,7},{7,4},{8,9},{9,10},{10,1... | collective-permute-start | bytes 393224 | tf_op jit(solution)/shard_map/ppermute | solution.py:40
  86.2 10.7 %collective-permute-start.23 = (bf16[384,256]{1,0:T(8,128)(2,1)S(1)}, bf16[384,256]{1,0:T(8,128)(2,1)S(1)}, u32[]{:S(2)}, u32[]{:S(2)}) collective-permute-start(bf16[384,256]{1,0:T(8,128)(2,1)S(1)} %get-tuple-element.13), channel_id=1, source_target_pairs={{0,11},{1,8},{2,9},{3,10},{4,15},{5,12},{6,13},{7,14},{8,3},{9,0},... | collective-permute-start | bytes 589832 | tf_op jit(solution)/shard_map/ppermute | solution.py:40
  86.4 15.7 %collective-permute-start.27 = (bf16[384,256]{1,0:T(8,128)(2,1)S(1)}, bf16[384,256]{1,0:T(8,128)(2,1)S(1)}, u32[]{:S(2)}, u32[]{:S(2)}) collective-permute-start(bf16[384,256]{1,0:T(8,128)(2,1)S(1)} %get-tuple-element.13), channel_id=1, source_target_pairs={{0,12},{1,13},{2,14},{3,15},{4,8},{5,9},{6,10},{7,11},{8,4},{9,5},... | collective-permute-start | bytes 589832 | tf_op jit(solution)/shard_map/ppermute | solution.py:40
  89.2 12.9 %collective-permute-start.28 = (bf16[384,256]{1,0:T(8,128)(2,1)S(1)}, bf16[384,256]{1,0:T(8,128)(2,1)S(1)}, u32[]{:S(2)}, u32[]{:S(2)}) collective-permute-start(bf16[384,256]{1,0:T(8,128)(2,1)S(1)} %get-tuple-element.14), channel_id=1, source_target_pairs={{8,20},{9,21},{10,22},{11,23},{12,16},{13,17},{14,18},{15,19},{16,... | collective-permute-start | bytes 589832 | tf_op jit(solution)/shard_map/ppermute | solution.py:40
  91.2 17.0 %collective-permute-start.24 = (bf16[384,256]{1,0:T(8,128)(2,1)S(1)}, bf16[384,256]{1,0:T(8,128)(2,1)S(1)}, u32[]{:S(2)}, u32[]{:S(2)}) collective-permute-start(bf16[384,256]{1,0:T(8,128)(2,1)S(1)} %get-tuple-element.14), channel_id=1, source_target_pairs={{8,19},{9,16},{10,17},{11,18},{12,23},{13,20},{14,21},{15,22},{16,... | collective-permute-start | bytes 589832 | tf_op jit(solution)/shard_map/ppermute | solution.py:40
  96.8 11.6 %collective-permute-start.33 = (bf16[384,256]{1,0:T(8,128)(2,1)S(1)}, bf16[384,256]{1,0:T(8,128)(2,1)S(1)}, u32[]{:S(2)}, u32[]{:S(2)}) collective-permute-start(bf16[384,256]{1,0:T(8,128)(2,1)S(1)} %get-tuple-element.13), channel_id=1, source_target_pairs={{0,8},{1,9},{2,10},{3,11},{4,12},{5,13},{6,14},{7,15},{8,0},{9,1},... | collective-permute-start | bytes 589832 | tf_op jit(solution)/shard_map/ppermute | solution.py:40
  96.9 15.0 %collective-permute-start.34 = (bf16[384,256]{1,0:T(8,128)(2,1)S(1)}, bf16[384,256]{1,0:T(8,128)(2,1)S(1)}, u32[]{:S(2)}, u32[]{:S(2)}) collective-permute-start(bf16[384,256]{1,0:T(8,128)(2,1)S(1)} %get-tuple-element.14), channel_id=1, source_target_pairs={{8,16},{9,17},{10,18},{11,19},{12,20},{13,21},{14,22},{15,23},{16,... | collective-permute-start | bytes 589832 | tf_op jit(solution)/shard_map/ppermute | solution.py:40
  102.1 10.9 %collective-permute-start.35 = (bf16[384,256]{1,0:T(8,128)(2,1)S(1)}, bf16[384,256]{1,0:T(8,128)(2,1)S(1)}, u32[]{:S(2)}, u32[]{:S(2)}) collective-permute-start(bf16[384,256]{1,0:T(8,128)(2,1)S(1)} %get-tuple-element.13), channel_id=1, source_target_pairs={{0,9},{1,10},{2,11},{3,8},{4,13},{5,14},{6,15},{7,12},{8,1},{9,2},... | collective-permute-start | bytes 589832 | tf_op jit(solution)/shard_map/ppermute | solution.py:40
  102.2 12.9 %collective-permute-start.36 = (bf16[384,256]{1,0:T(8,128)(2,1)S(1)}, bf16[384,256]{1,0:T(8,128)(2,1)S(1)}, u32[]{:S(2)}, u32[]{:S(2)}) collective-permute-start(bf16[384,256]{1,0:T(8,128)(2,1)S(1)} %get-tuple-element.14), channel_id=1, source_target_pairs={{8,17},{9,18},{10,19},{11,16},{12,21},{13,22},{14,23},{15,20},{16,... | collective-permute-start | bytes 589832 | tf_op jit(solution)/shard_map/ppermute | solution.py:40
  108.3 13.4 %collective-permute-start.29 = (bf16[384,512]{1,0:T(8,128)(2,1)S(1)}, bf16[384,512]{1,0:T(8,128)(2,1)S(1)}, u32[]{:S(2)}, u32[]{:S(2)}) collective-permute-start(bf16[384,512]{1,0:T(8,128)(2,1)S(1)} %shard_map.55), channel_id=1, source_target_pairs={{0,1},{1,2},{2,3},{3,0},{4,5},{5,6},{6,7},{7,4},{8,9},{9,10},{10,1... | collective-permute-start | bytes 1179656 | tf_op jit(solution)/shard_map/ppermute | solution.py:40
  108.4 13.6 %collective-permute-start.25 = (bf16[384,512]{1,0:T(8,128)(2,1)S(1)}, bf16[384,512]{1,0:T(8,128)(2,1)S(1)}, u32[]{:S(2)}, u32[]{:S(2)}) collective-permute-start(bf16[384,512]{1,0:T(8,128)(2,1)S(1)} %shard_map.54), channel_id=1, source_target_pairs={{0,3},{1,0},{2,1},{3,2},{4,7},{5,4},{6,5},{7,6},{8,11},{9,8},{10,9... | collective-permute-start | bytes 1179656 | tf_op jit(solution)/shard_map/ppermute | solution.py:40
  111.9 11.3 %collective-permute-start.31 = (bf16[384,512]{1,0:T(8,128)(2,1)S(1)}, bf16[384,512]{1,0:T(8,128)(2,1)S(1)}, u32[]{:S(2)}, u32[]{:S(2)}) collective-permute-start(bf16[384,512]{1,0:T(8,128)(2,1)S(1)} %shard_map.54), channel_id=1, source_target_pairs={{0,4},{1,5},{2,6},{3,7},{4,0},{5,1},{6,2},{7,3},{8,12},{9,13},{10,... | collective-permute-start | bytes 1179656 | tf_op jit(solution)/shard_map/ppermute | solution.py:40
  121.7 8.6 %collective-permute-start.30 = (bf16[128,512]{1,0:T(8,128)(2,1)S(1)}, bf16[128,512]{1,0:T(8,128)(2,1)S(1)}, u32[]{:S(2)}, u32[]{:S(2)}) collective-permute-start(bf16[128,512]{1,0:T(8,128)(2,1)S(1)} %slice.43), channel_id=1, source_target_pairs={{0,1},{1,2},{2,3},{3,0},{4,5},{5,6},{6,7},{7,4},{8,9},{9,10},{10,1... | collective-permute-start | bytes 393224 | tf_op jit(solution)/shard_map/ppermute | solution.py:40
  133.0 10.6 %collective-permute-start.38 = (bf16[384,256]{1,0:T(8,128)(2,1)S(1)}, bf16[384,256]{1,0:T(8,128)(2,1)S(1)}, u32[]{:S(2)}, u32[]{:S(2)}) collective-permute-start(bf16[384,256]{1,0:T(8,128)(2,1)S(1)} %get-tuple-element.16), channel_id=1, source_target_pairs={{8,16},{9,17},{10,18},{11,19},{12,20},{13,21},{14,22},{15,23},{16,... | collective-permute-start | bytes 589832 | tf_op jit(solution)/shard_map/ppermute | solution.py:40
  (10 other events, 74.6 us)

commit v3 on v2

v3 whole, which is shorter than its diff:
```python
import functools

import jax
import jax.numpy as jnp
from jax import lax
from jax.experimental import pallas as pl
from jax.experimental.pallas import tpu as pltpu
from jax.sharding import PartitionSpec as P

TICKS = 3
AXES = ("layer", "row")
VMEM = pl.BlockSpec(memory_space=pltpu.VMEM)
SMEM = pl.BlockSpec(memory_space=pltpu.SMEM)


def at_row(row, dx, dy):
    return (row ^ (4 * dx)) & 4 | (row + dy) & 3


def stay(layer):
    return layer


def near_layer(layer):
    return layer ^ 1


def far_layer(layer):
    return layer - 1 if layer % 2 == 0 else layer + 1


def permute(array, layers, rows, layer_to, dx, dy):
    pairs = [
        (layer * rows + row, layer_to(layer) * rows + at_row(row, dx, dy))
        for layer in range(layers)
        for row in range(rows)
        if 0 <= layer_to(layer) < layers
    ]
    return lax.ppermute(array, AXES, pairs)


def block_product(ops, block):
    count = block.shape[1] // 4
    re1, im1, re2, im2 = (block[:, j * count : (j + 1) * count] for j in range(4))
    lhs = jnp.concatenate(ops, axis=1)
    rhs = jnp.concatenate(
        [
            block,
            jnp.concatenate([-im1, re1, -im2, re2], axis=1),
            jnp.concatenate([re2, im2, re1, im1], axis=1),
            jnp.concatenate([-im2, re2, -im1, re1], axis=1),
        ],
        axis=0,
    )
    return jnp.dot(lhs, rhs, preferred_element_type=jnp.float32)


def stage_kernel(shifts, layout, parity, first, last, where, ops, *refs):
    refs = list(refs)
    blocks = []
    for parts in layout:
        blocks.append([])
        for count in parts:
            blocks[-1].append(refs[:count])
            refs = refs[count:]
    if not first:
        before, refs = refs[0], refs[1:]
    if last:
        extra, near_out, far_out = refs
    else:
        (total_out,) = refs
    rows = ops.shape[2]
    total = None if first else before[...]
    for j, parts in enumerate(blocks):
        whole = [jnp.concatenate([ref[...] for ref in part], axis=1) for part in parts]
        block = jnp.concatenate(whole, axis=0)
        place = at_row(where[0], *shifts[j])
        columns = pl.ds(pl.multiple_of(place * rows, rows), rows)
        term = block_product([ops[0, part, :, columns] for part in range(4)], block)
        total = term if total is None else total + term
    if last:
        half = total.shape[1] // 2
        near, far = total[:, half:], total[:, :half]
        if parity:
            even = where[1] % 2 == 0
            near, far = jnp.where(even, far, near), jnp.where(even, near, far)
        near_out[...] = (near + extra[:, :half].astype(jnp.float32)).astype(jnp.bfloat16)
        far_out[...] = (far + extra[:, half:].astype(jnp.float32)).astype(jnp.bfloat16)
    else:
        total_out[...] = total


def stage(operators, where, blocks, parity=False, before=None, extra=None):
    rows = operators.shape[2]
    shifts = [shift for shift, _ in blocks]
    layout = [[len(part) for part in parts] for _, parts in blocks]
    flat = [array for _, parts in blocks for part in parts for array in part]
    width = sum(array.shape[1] for array in blocks[0][1][0])
    operands = [where, operators] + flat
    if before is not None:
        operands.append(before)
    if extra is not None:
        operands.append(extra)
        out_shape = [jax.ShapeDtypeStruct((rows, width // 2), jnp.bfloat16)] * 2
        out_specs = [VMEM, VMEM]
    else:
        out_shape = jax.ShapeDtypeStruct((rows, width), jnp.float32)
        out_specs = VMEM
    n = len(blocks)
    return pl.pallas_call(
        functools.partial(stage_kernel, shifts, layout, parity, before is None, extra is not None),
        out_shape=out_shape,
        in_specs=[SMEM] + [VMEM] * (len(operands) - 1),
        out_specs=out_specs,
        compiler_params=pltpu.CompilerParams(vmem_limit_bytes=24 * 2**20),
        cost_estimate=pl.CostEstimate(
            flops=2 * n * 4 * rows * rows * width,
            bytes_accessed=n * (4 * rows * rows + rows * width) * 2,
            transcendentals=0,
        ),
    )(*operands)


def sources_kernel(where, sources, source_layer, out):
    half = sources.shape[1] // 2
    mask = source_layer[...] == where[1]
    mask = jnp.concatenate([mask, mask], axis=1)
    down = jnp.where(mask, sources[:, :half].astype(jnp.float32), 0.0)
    up = jnp.where(mask, sources[:, half:].astype(jnp.float32), 0.0)
    even = where[1] % 2 == 0
    out[:, :half] = jnp.where(even, down, up).astype(jnp.bfloat16)
    out[:, half:] = jnp.where(even, up, down).astype(jnp.bfloat16)


def layer_sources(where, sources, source_layer):
    return pl.pallas_call(
        sources_kernel,
        out_shape=jax.ShapeDtypeStruct(sources.shape, jnp.bfloat16),
        in_specs=[SMEM, VMEM, VMEM],
        out_specs=VMEM,
        compiler_params=pltpu.CompilerParams(vmem_limit_bytes=6 * 2**20),
    )(where, sources, source_layer)


def per_device(layers, rows, waves, operators, sources, source_layer):
    third = operators.shape[2] // 3
    where = jnp.stack([lax.axis_index("row"), lax.axis_index("layer")]).astype(jnp.int32)

    def move(array, dx, dy):
        return permute(array, layers, rows, stay, dx, dy)

    outs = None
    for tick in range(TICKS):
        if outs is None:
            own = [waves[0]]
        else:
            own = [jnp.concatenate([near_in, far_in], axis=1)]
        below, across, above = move(own[0], 0, -1), move(own[0], 1, 0), move(own[0], 0, 1)
        total = stage(operators, where, [((0, 0), [own])])
        if tick == 0:
            source_term = layer_sources(where, sources, source_layer.reshape(1, -1))
            below, across, total, source_term = lax.optimization_barrier((below, across, total, source_term))
        far_y = move(below, 0, -1)
        across_below = move(below, 1, 0)
        across_above = move(across, 0, 1)
        part0 = move(far_y[:third], 1, 0)
        part1 = move(across_above[third : 2 * third], 0, 1)
        part2 = move(across_below[2 * third :], 0, -1)
        total = stage(
            operators, where, [((0, 1), [[below]]), ((1, 0), [[across]]), ((0, -1), [[above]])], before=total
        )
        total = stage(
            operators,
            where,
            [((0, 2), [[far_y]]), ((1, 1), [[across_below]]), ((1, -1), [[across_above]])],
            before=total,
        )
        outs = stage(
            operators,
            where,
            [((1, 2), [[part0], [part1], [part2]])],
            parity=tick == 0,
            before=total,
            extra=source_term,
        )
        near_in = permute(outs[0], layers, rows, near_layer, 0, 0)
        far_in = permute(outs[1], layers, rows, far_layer, 0, 0)
    even = where[1] % 2 == 0
    down, up = jnp.where(even, far_in, near_in), jnp.where(even, near_in, far_in)
    return jnp.concatenate([down, up], axis=1)[None]


def solution(mesh):
    return jax.shard_map(
        functools.partial(per_device, mesh.shape["layer"], mesh.shape["row"]),
        mesh=mesh,
        in_specs=(P("layer", "row", None), P("layer", None, "row", None), P("row", None), P()),
        out_specs=P("layer", "row", None),
        check_vma=False,
    )
```

time: 146 us -> 130 us (0.89)
  starting transfers between devices: 80 us -> 49.5 us
  waiting for transfers between devices: 27.2 us -> 48.4 us
  Pallas kernels: 36.1 us -> 23.9 us
  local copies, waits for them, and re-layouts: 1.1 us -> 6.46 us
    ppermute x39 -> x33, starting transfers between devices: 80 us -> 49.5 us  [permute(): return lax.ppermute(array, AXES, pairs)]
    ppermute x39 -> x33, waiting for transfers between devices: 27.2 us -> 48.4 us  [permute(): return lax.ppermute(array, AXES, pairs)]
    pallas_call x9 -> x12, Pallas kernels: 34.7 us -> 23.3 us  [stage(): pl.pallas_call(functools.partial(stage_kernel, shifts, layout, parity, be...]
    unnamed x6 -> x10, local copies, waits for them, and re-layouts: 1.01 us -> 6.35 us
  transfers between devices with their start and end apart: 39 -> 33, of which waited for: 10 -> 16; matrix products, arithmetic and copies ran while one was open for 0% -> 0% of each run, Pallas kernels for 19% -> 15%
where the time goes in v3:
time: 130 us
  starting transfers between devices  49.5 us (38%)
  waiting for transfers between devices  48.4 us (37%)
  Pallas kernels  23.9 us (18%)
  local copies, waits for them, and re-layouts  6.46 us (5%)
    ppermute x33, starting transfers between devices, permute(): return lax.ppermute(array, AXES, pairs)  49.5 us
    ppermute x33, waiting for transfers between devices, permute(): return lax.ppermute(array, AXES, pairs)  48.4 us
    pallas_call x12, Pallas kernels, stage(): pl.pallas_call(functools.partial(stage_kernel, shifts, layout, parity, be...  23.3 us
    unnamed x10, local copies, waits for them, and re-layouts  6.35 us
  transfers between devices with their start and end apart: 33, of which 16 were waited for; matrix products, arithmetic and copies ran while one was open for 0% of the time, Pallas kernels for 15%

profile of v3, /device:TPU:6, one launch (start us, length us, event | category | flops | bytes accessed | tf_op | source)
XLA Modules:
  0.0 129.5 jit_solution(3746756748294354860)
XLA Ops:
  0.0 3.0 %collective-permute-start = (bf16[384,512]{1,0:T(8,128)(2,1)}, bf16[384,512]{1,0:T(8,128)(2,1)S(1)}, u32[]{:S(2)}, u32[]{:S(2)}) collective-permute-start(bf16[384,512]{1,0:T(8,128)(2,1)} %bitcast.6), channel_id=1, source_target_pairs={{0,3},{1,0},{2,1},{3,2},{4,7},{5,4},{6,5},{7,6},{8,11},{9,8},{10,9... | collective-permute-start | bytes 1179656 | tf_op jit(solution)/shard_map/ppermute | solution.py:39
  6.2 3.7 %copy-done = bf16[1,4,384,3072]{3,2,1,0:T(8,128)(2,1)S(1)} copy-done((bf16[1,4,384,3072]{3,2,1,0:T(8,128)(2,1)S(1)}, bf16[1,4,384,3072]{3,2,1,0:T(8,128)(2,1)}, u32[]{:S(2)}) %copy-start) | copy-done | bytes 9437208
  12.2 1.6 %collective-permute-done.1.refs_1_ = bf16[384,512]{1,0:T(8,128)(2,1)S(1)} collective-permute-done((bf16[384,512]{1,0:T(8,128)(2,1)}, bf16[384,512]{1,0:T(8,128)(2,1)S(1)}, u32[]{:S(2)}, u32[]{:S(2)}) %collective-permute-start.1) | collective-permute-done | bytes 393248 | tf_op jit(solution)/shard_map/ppermute | solution.py:39
  13.8 1.8 %collective-permute-start.2 = (bf16[384,512]{1,0:T(8,128)(2,1)S(1)}, bf16[384,512]{1,0:T(8,128)(2,1)S(1)}, u32[]{:S(2)}, u32[]{:S(2)}) collective-permute-start(bf16[384,512]{1,0:T(8,128)(2,1)S(1)} %collective-permute-done.refs_0_), channel_id=1, source_target_pairs={{0,3},{1,0},{2,1},{3,2},{4,7},{5,4},{6,5},{7,6},{8,11},{9,8},{10,9... | collective-permute-start | bytes 1179656 | tf_op jit(solution)/shard_map/ppermute | solution.py:39
  16.8 2.6 %shard_map.48.refs_3_ = f32[384,512]{1,0:T(8,128)S(1)} custom-call(s32[2]{0:T(128)S(1)} %pad_add_fusion.where, bf16[1,4,384,3072]{3,2,1,0:T(8,128)(2,1)S(1)} %copy-done, bf16[384,512]{1,0:T(8,128)(2,1)S(1)} %collective-permute-done.refs_0_, bf16[384,512]{1,0:T(8,128)(2,1)S(1)} %collective-permute-done.1.refs_1_, ...), custom_call_target="tpu_custom_call" | custom-call | flops 1811939328 | bytes 4718592 | tf_op jit(solution)/shard_map/pallas_call | solution.py:110
  19.3 4.1 %collective-permute-done.2.refs_0_ = bf16[384,512]{1,0:T(8,128)(2,1)S(1)} collective-permute-done((bf16[384,512]{1,0:T(8,128)(2,1)S(1)}, bf16[384,512]{1,0:T(8,128)(2,1)S(1)}, u32[]{:S(2)}, u32[]{:S(2)}) %collective-permute-start.2) | collective-permute-done | bytes 393248 | tf_op jit(solution)/shard_map/ppermute | solution.py:39
  24.4 2.3 %collective-permute-done.6.refs_1_ = bf16[384,512]{1,0:T(8,128)(2,1)S(1)} collective-permute-done((bf16[384,512]{1,0:T(8,128)(2,1)S(1)}, bf16[384,512]{1,0:T(8,128)(2,1)S(1)}, u32[]{:S(2)}, u32[]{:S(2)}) %collective-permute-start.6) | collective-permute-done | bytes 393248 | tf_op jit(solution)/shard_map/ppermute | solution.py:39
  26.7 1.5 %collective-permute-start.7 = (bf16[128,512]{1,0:T(8,128)(2,1)S(1)}, bf16[128,512]{1,0:T(8,128)(2,1)S(1)}, u32[]{:S(2)}, u32[]{:S(2)}) collective-permute-start(bf16[128,512]{1,0:T(8,128)(2,1)S(1)} %slice.38), channel_id=1, source_target_pairs={{0,3},{1,0},{2,1},{3,2},{4,7},{5,4},{6,5},{7,6},{8,11},{9,8},{10,9... | collective-permute-start | bytes 393224 | tf_op jit(solution)/shard_map/ppermute | solution.py:39
  28.9 2.6 %shard_map.49.refs_3_ = f32[384,512]{1,0:T(8,128)S(1)} custom-call(s32[2]{0:T(128)S(1)} %pad_add_fusion.where, bf16[1,4,384,3072]{3,2,1,0:T(8,128)(2,1)S(1)} %copy-done, bf16[384,512]{1,0:T(8,128)(2,1)S(1)} %collective-permute-done.2.refs_0_, bf16[384,512]{1,0:T(8,128)(2,1)S(1)} %collective-permute-done.6.refs_1_, ...), custom_call_target="tpu_custom_call" | custom-call | flops 1811939328 | bytes 4718592 | tf_op jit(solution)/shard_map/pallas_call | solution.py:110
  31.7 2.7 %collective-permute-done.5.refs_1_ = bf16[128,512]{1,0:T(8,128)(2,1)S(1)} collective-permute-done((bf16[128,512]{1,0:T(8,128)(2,1)S(1)}, bf16[128,512]{1,0:T(8,128)(2,1)S(1)}, u32[]{:S(2)}, u32[]{:S(2)}) %collective-permute-start.5) | collective-permute-done | bytes 131104 | tf_op jit(solution)/shard_map/ppermute | solution.py:39
  34.5 1.3 %shard_map.50 = (bf16[384,256]{1,0:T(8,128)(2,1)S(1)}, bf16[384,256]{1,0:T(8,128)(2,1)S(1)}) custom-call(s32[2]{0:T(128)S(1)} %pad_add_fusion.where, bf16[1,4,384,3072]{3,2,1,0:T(8,128)(2,1)S(1)} %copy-done, bf16[128,512]{1,0:T(8,128)(2,1)S(1)} %collective-permute-done.3.refs_0_, bf16[128,512]{1,0:T(8,128)(2,1)S(1)} %collective-permute-done.5.refs_1_, ...), custom_call_target="tpu_custom_call" | custom-call | flops 603979776 | bytes 1572864 | tf_op jit(solution)/shard_map/pallas_call | solution.py:110
  35.9 8.7 %collective-permute-start.10 = (bf16[384,256]{1,0:T(8,128)(2,1)S(1)}, bf16[384,256]{1,0:T(8,128)(2,1)S(1)}, u32[]{:S(2)}, u32[]{:S(2)}) collective-permute-start(bf16[384,256]{1,0:T(8,128)(2,1)S(1)} %get-tuple-element.20), channel_id=1, source_target_pairs={{8,16},{9,17},{10,18},{11,19},{12,20},{13,21},{14,22},{15,23},{16,... | collective-permute-start | bytes 589832 | tf_op jit(solution)/shard_map/ppermute | solution.py:39
  44.6 3.4 %collective-permute-done.10 = bf16[384,256]{1,0:T(8,128)(2,1)S(1)} collective-permute-done((bf16[384,256]{1,0:T(8,128)(2,1)S(1)}, bf16[384,256]{1,0:T(8,128)(2,1)S(1)}, u32[]{:S(2)}, u32[]{:S(2)}) %collective-permute-start.10) | collective-permute-done | bytes 196640 | tf_op jit(solution)/shard_map/ppermute | solution.py:39
  48.4 1.7 %collective-permute-start.19 = (bf16[384,512]{1,0:T(8,128)(2,1)S(1)}, bf16[384,512]{1,0:T(8,128)(2,1)S(1)}, u32[]{:S(2)}, u32[]{:S(2)}) collective-permute-start(bf16[384,512]{1,0:T(8,128)(2,1)S(1)} %constant_dynamic-update-slice_fusion.refs_0_), channel_id=1, source_target_pairs={{0,1},{1,2},{2,3},{3,0},{4,5},{5,6},{6,7},{7,4},{8,9},{9,10},{10,1... | collective-permute-start | bytes 1179656 | tf_op jit(solution)/shard_map/ppermute | solution.py:39
  50.2 9.0 %collective-permute-done.11.refs_0_ = bf16[384,512]{1,0:T(8,128)(2,1)S(1)} collective-permute-done((bf16[384,512]{1,0:T(8,128)(2,1)S(1)}, bf16[384,512]{1,0:T(8,128)(2,1)S(1)}, u32[]{:S(2)}, u32[]{:S(2)}) %collective-permute-start.11) | collective-permute-done | bytes 393248 | tf_op jit(solution)/shard_map/ppermute | solution.py:39
  59.2 2.0 %collective-permute-start.15 = (bf16[384,512]{1,0:T(8,128)(2,1)S(1)}, bf16[384,512]{1,0:T(8,128)(2,1)S(1)}, u32[]{:S(2)}, u32[]{:S(2)}) collective-permute-start(bf16[384,512]{1,0:T(8,128)(2,1)S(1)} %collective-permute-done.14.refs_1_), channel_id=1, source_target_pairs={{0,1},{1,2},{2,3},{3,0},{4,5},{5,6},{6,7},{7,4},{8,9},{9,10},{10,1... | collective-permute-start | bytes 1179656 | tf_op jit(solution)/shard_map/ppermute | solution.py:39
  62.5 2.6 %shard_map.52.refs_3_ = f32[384,512]{1,0:T(8,128)S(1)} custom-call(s32[2]{0:T(128)S(1)} %pad_add_fusion.where, bf16[1,4,384,3072]{3,2,1,0:T(8,128)(2,1)S(1)} %copy-done, bf16[384,512]{1,0:T(8,128)(2,1)S(1)} %collective-permute-done.11.refs_0_, bf16[384,512]{1,0:T(8,128)(2,1)S(1)} %collective-permute-done.14.refs_1_, ...), custom_call_target="tpu_custom_call" | custom-call | flops 1811939328 | bytes 4718592 | tf_op jit(solution)/shard_map/pallas_call | solution.py:110
  65.1 3.2 %collective-permute-done.12.refs_0_ = bf16[384,512]{1,0:T(8,128)(2,1)S(1)} collective-permute-done((bf16[384,512]{1,0:T(8,128)(2,1)S(1)}, bf16[384,512]{1,0:T(8,128)(2,1)S(1)}, u32[]{:S(2)}, u32[]{:S(2)}) %collective-permute-start.12) | collective-permute-done | bytes 393248 | tf_op jit(solution)/shard_map/ppermute | solution.py:39
  70.4 2.6 %collective-permute-start.18 = (bf16[128,512]{1,0:T(8,128)(2,1)S(1)}, bf16[128,512]{1,0:T(8,128)(2,1)S(1)}, u32[]{:S(2)}, u32[]{:S(2)}) collective-permute-start(bf16[128,512]{1,0:T(8,128)(2,1)S(1)} %slice.41), channel_id=1, source_target_pairs={{0,3},{1,0},{2,1},{3,2},{4,7},{5,4},{6,5},{7,6},{8,11},{9,8},{10,9... | collective-permute-start | bytes 393224 | tf_op jit(solution)/shard_map/ppermute | solution.py:39
  73.0 2.6 %shard_map.53.refs_3_ = f32[384,512]{1,0:T(8,128)S(1)} custom-call(s32[2]{0:T(128)S(1)} %pad_add_fusion.where, bf16[1,4,384,3072]{3,2,1,0:T(8,128)(2,1)S(1)} %copy-done, bf16[384,512]{1,0:T(8,128)(2,1)S(1)} %collective-permute-done.12.refs_0_, bf16[384,512]{1,0:T(8,128)(2,1)S(1)} %collective-permute-done.17.refs_1_, ...), custom_call_target="tpu_custom_call" | custom-call | flops 1811939328 | bytes 4718592 | tf_op jit(solution)/shard_map/pallas_call | solution.py:110
  75.8 1.3 %shard_map.54 = (bf16[384,256]{1,0:T(8,128)(2,1)S(1)}, bf16[384,256]{1,0:T(8,128)(2,1)S(1)}) custom-call(s32[2]{0:T(128)S(1)} %pad_add_fusion.where, bf16[1,4,384,3072]{3,2,1,0:T(8,128)(2,1)S(1)} %copy-done, bf16[128,512]{1,0:T(8,128)(2,1)S(1)} %collective-permute-done.13.refs_0_, bf16[128,512]{1,0:T(8,128)(2,1)S(1)} %collective-permute-done.16.refs_1_, ...), custom_call_target="tpu_custom_call" | custom-call | flops 603979776 | bytes 1572864 | tf_op jit(solution)/shard_map/pallas_call | solution.py:110
  77.3 3.5 %collective-permute-start.21 = (bf16[384,256]{1,0:T(8,128)(2,1)S(1)}, bf16[384,256]{1,0:T(8,128)(2,1)S(1)}, u32[]{:S(2)}, u32[]{:S(2)}) collective-permute-start(bf16[384,256]{1,0:T(8,128)(2,1)S(1)} %get-tuple-element.22), channel_id=1, source_target_pairs={{8,16},{9,17},{10,18},{11,19},{12,20},{13,21},{14,22},{15,23},{16,... | collective-permute-start | bytes 589832 | tf_op jit(solution)/shard_map/ppermute | solution.py:39
  80.9 7.1 %collective-permute-done.21 = bf16[384,256]{1,0:T(8,128)(2,1)S(1)} collective-permute-done((bf16[384,256]{1,0:T(8,128)(2,1)S(1)}, bf16[384,256]{1,0:T(8,128)(2,1)S(1)}, u32[]{:S(2)}, u32[]{:S(2)}) %collective-permute-start.21) | collective-permute-done | bytes 196640 | tf_op jit(solution)/shard_map/ppermute | solution.py:39
  88.0 3.4 %collective-permute-start.22 = (bf16[384,512]{1,0:T(8,128)(2,1)S(1)}, bf16[384,512]{1,0:T(8,128)(2,1)S(1)}, u32[]{:S(2)}, u32[]{:S(2)}) collective-permute-start(bf16[384,512]{1,0:T(8,128)(2,1)S(1)} %constant_dynamic-update-slice_fusion.2.refs_0_), channel_id=1, source_target_pairs={{0,3},{1,0},{2,1},{3,2},{4,7},{5,4},{6,5},{7,6},{8,11},{9,8},{10,9... | collective-permute-start | bytes 1179656 | tf_op jit(solution)/shard_map/ppermute | solution.py:39
  92.3 4.9 %collective-permute-done.22.refs_0_ = bf16[384,512]{1,0:T(8,128)(2,1)S(1)} collective-permute-done((bf16[384,512]{1,0:T(8,128)(2,1)S(1)}, bf16[384,512]{1,0:T(8,128)(2,1)S(1)}, u32[]{:S(2)}, u32[]{:S(2)}) %collective-permute-start.22) | collective-permute-done | bytes 393248 | tf_op jit(solution)/shard_map/ppermute | solution.py:39
  97.2 3.7 %collective-permute-start.23 = (bf16[384,512]{1,0:T(8,128)(2,1)S(1)}, bf16[384,512]{1,0:T(8,128)(2,1)S(1)}, u32[]{:S(2)}, u32[]{:S(2)}) collective-permute-start(bf16[384,512]{1,0:T(8,128)(2,1)S(1)} %collective-permute-done.22.refs_0_), channel_id=1, source_target_pairs={{0,3},{1,0},{2,1},{3,2},{4,7},{5,4},{6,5},{7,6},{8,11},{9,8},{10,9... | collective-permute-start | bytes 1179656 | tf_op jit(solution)/shard_map/ppermute | solution.py:39
  103.2 2.6 %shard_map.56.refs_3_ = f32[384,512]{1,0:T(8,128)S(1)} custom-call(s32[2]{0:T(128)S(1)} %pad_add_fusion.where, bf16[1,4,384,3072]{3,2,1,0:T(8,128)(2,1)S(1)} %copy-done, bf16[384,512]{1,0:T(8,128)(2,1)S(1)} %collective-permute-done.22.refs_0_, bf16[384,512]{1,0:T(8,128)(2,1)S(1)} %collective-permute-done.25.refs_1_, ...), custom_call_target="tpu_custom_call" | custom-call | flops 1811939328 | bytes 4718592 | tf_op jit(solution)/shard_map/pallas_call | solution.py:110
  107.2 3.3 %collective-permute-done.26.refs_2_ = bf16[384,512]{1,0:T(8,128)(2,1)S(1)} collective-permute-done((bf16[384,512]{1,0:T(8,128)(2,1)S(1)}, bf16[384,512]{1,0:T(8,128)(2,1)S(1)}, u32[]{:S(2)}, u32[]{:S(2)}) %collective-permute-start.26) | collective-permute-done | bytes 393248 | tf_op jit(solution)/shard_map/ppermute | solution.py:39
  110.7 3.3 %collective-permute-start.29 = (bf16[128,512]{1,0:T(8,128)(2,1)S(1)}, bf16[128,512]{1,0:T(8,128)(2,1)S(1)}, u32[]{:S(2)}, u32[]{:S(2)}) collective-permute-start(bf16[128,512]{1,0:T(8,128)(2,1)S(1)} %slice.44), channel_id=1, source_target_pairs={{0,3},{1,0},{2,1},{3,2},{4,7},{5,4},{6,5},{7,6},{8,11},{9,8},{10,9... | collective-permute-start | bytes 393224 | tf_op jit(solution)/shard_map/ppermute | solution.py:39
  113.9 2.6 %shard_map.57.refs_3_ = f32[384,512]{1,0:T(8,128)S(1)} custom-call(s32[2]{0:T(128)S(1)} %pad_add_fusion.where, bf16[1,4,384,3072]{3,2,1,0:T(8,128)(2,1)S(1)} %copy-done, bf16[384,512]{1,0:T(8,128)(2,1)S(1)} %collective-permute-done.23.refs_0_, bf16[384,512]{1,0:T(8,128)(2,1)S(1)} %collective-permute-done.28.refs_1_, ...), custom_call_target="tpu_custom_call" | custom-call | flops 1811939328 | bytes 4718592 | tf_op jit(solution)/shard_map/pallas_call | solution.py:110
  118.1 6.2 %collective-permute-start.31 = (bf16[384,256]{1,0:T(8,128)(2,1)S(1)}, bf16[384,256]{1,0:T(8,128)(2,1)S(1)}, u32[]{:S(2)}, u32[]{:S(2)}) collective-permute-start(bf16[384,256]{1,0:T(8,128)(2,1)S(1)} %get-tuple-element.23), channel_id=1, source_target_pairs={{8,16},{9,17},{10,18},{11,19},{12,20},{13,21},{14,22},{15,23},{16,... | collective-permute-start | bytes 589832 | tf_op jit(solution)/shard_map/ppermute | solution.py:39
  124.4 4.3 %collective-permute-done.31 = bf16[384,256]{1,0:T(8,128)(2,1)S(1)} collective-permute-done((bf16[384,256]{1,0:T(8,128)(2,1)S(1)}, bf16[384,256]{1,0:T(8,128)(2,1)S(1)}, u32[]{:S(2)}, u32[]{:S(2)}) %collective-permute-start.31) | collective-permute-done | bytes 196640 | tf_op jit(solution)/shard_map/ppermute | solution.py:39
  (71 shorter events, 20.1 us)
Async XLA Ops:
  0.0 12.2 %collective-permute-start = (bf16[384,512]{1,0:T(8,128)(2,1)}, bf16[384,512]{1,0:T(8,128)(2,1)S(1)}, u32[]{:S(2)}, u32[]{:S(2)}) collective-permute-start(bf16[384,512]{1,0:T(8,128)(2,1)} %bitcast.6), channel_id=1, source_target_pairs={{0,3},{1,0},{2,1},{3,2},{4,7},{5,4},{6,5},{7,6},{8,11},{9,8},{10,9... | collective-permute-start | bytes 1179656 | tf_op jit(solution)/shard_map/ppermute | solution.py:39
  3.0 10.8 %collective-permute-start.1 = (bf16[384,512]{1,0:T(8,128)(2,1)}, bf16[384,512]{1,0:T(8,128)(2,1)S(1)}, u32[]{:S(2)}, u32[]{:S(2)}) collective-permute-start(bf16[384,512]{1,0:T(8,128)(2,1)} %bitcast.7), channel_id=1, source_target_pairs={{0,4},{1,5},{2,6},{3,7},{4,0},{5,1},{6,2},{7,3},{8,12},{9,13},{10,... | collective-permute-start | bytes 1179656 | tf_op jit(solution)/shard_map/ppermute | solution.py:39
  3.8 12.9 %collective-permute-start.8 = (bf16[384,512]{1,0:T(8,128)(2,1)}, bf16[384,512]{1,0:T(8,128)(2,1)S(1)}, u32[]{:S(2)}, u32[]{:S(2)}) collective-permute-start(bf16[384,512]{1,0:T(8,128)(2,1)} %bitcast.8), channel_id=1, source_target_pairs={{0,1},{1,2},{2,3},{3,0},{4,5},{5,6},{6,7},{7,4},{8,9},{9,10},{10,1... | collective-permute-start | bytes 1179656 | tf_op jit(solution)/shard_map/ppermute | solution.py:39
  13.8 9.7 %collective-permute-start.2 = (bf16[384,512]{1,0:T(8,128)(2,1)S(1)}, bf16[384,512]{1,0:T(8,128)(2,1)S(1)}, u32[]{:S(2)}, u32[]{:S(2)}) collective-permute-start(bf16[384,512]{1,0:T(8,128)(2,1)S(1)} %collective-permute-done.refs_0_), channel_id=1, source_target_pairs={{0,3},{1,0},{2,1},{3,2},{4,7},{5,4},{6,5},{7,6},{8,11},{9,8},{10,9... | collective-permute-start | bytes 1179656 | tf_op jit(solution)/shard_map/ppermute | solution.py:39
  15.6 11.1 %collective-permute-start.6 = (bf16[384,512]{1,0:T(8,128)(2,1)S(1)}, bf16[384,512]{1,0:T(8,128)(2,1)S(1)}, u32[]{:S(2)}, u32[]{:S(2)}) collective-permute-start(bf16[384,512]{1,0:T(8,128)(2,1)S(1)} %collective-permute-done.refs_0_), channel_id=1, source_target_pairs={{0,4},{1,5},{2,6},{3,7},{4,0},{5,1},{6,2},{7,3},{8,12},{9,13},{10,... | collective-permute-start | bytes 1179656 | tf_op jit(solution)/shard_map/ppermute | solution.py:39
  16.8 11.4 %collective-permute-start.4 = (bf16[384,512]{1,0:T(8,128)(2,1)S(1)}, bf16[384,512]{1,0:T(8,128)(2,1)S(1)}, u32[]{:S(2)}, u32[]{:S(2)}) collective-permute-start(bf16[384,512]{1,0:T(8,128)(2,1)S(1)} %collective-permute-done.1.refs_1_), channel_id=1, source_target_pairs={{0,1},{1,2},{2,3},{3,0},{4,5},{5,6},{6,7},{7,4},{8,9},{9,10},{10,1... | collective-permute-start | bytes 1179656 | tf_op jit(solution)/shard_map/ppermute | solution.py:39
  23.5 8.0 %collective-permute-start.3 = (bf16[128,512]{1,0:T(8,128)(2,1)S(1)}, bf16[128,512]{1,0:T(8,128)(2,1)S(1)}, u32[]{:S(2)}, u32[]{:S(2)}) collective-permute-start(bf16[128,512]{1,0:T(8,128)(2,1)S(1)} %slice.36), channel_id=1, source_target_pairs={{0,4},{1,5},{2,6},{3,7},{4,0},{5,1},{6,2},{7,3},{8,12},{9,13},{10,... | collective-permute-start | bytes 393224 | tf_op jit(solution)/shard_map/ppermute | solution.py:39
  26.7 5.0 %collective-permute-start.7 = (bf16[128,512]{1,0:T(8,128)(2,1)S(1)}, bf16[128,512]{1,0:T(8,128)(2,1)S(1)}, u32[]{:S(2)}, u32[]{:S(2)}) collective-permute-start(bf16[128,512]{1,0:T(8,128)(2,1)S(1)} %slice.38), channel_id=1, source_target_pairs={{0,3},{1,0},{2,1},{3,2},{4,7},{5,4},{6,5},{7,6},{8,11},{9,8},{10,9... | collective-permute-start | bytes 393224 | tf_op jit(solution)/shard_map/ppermute | solution.py:39
  28.2 6.3 %collective-permute-start.5 = (bf16[128,512]{1,0:T(8,128)(2,1)S(1)}, bf16[128,512]{1,0:T(8,128)(2,1)S(1)}, u32[]{:S(2)}, u32[]{:S(2)}) collective-permute-start(bf16[128,512]{1,0:T(8,128)(2,1)S(1)} %slice.37), channel_id=1, source_target_pairs={{0,1},{1,2},{2,3},{3,0},{4,5},{5,6},{6,7},{7,4},{8,9},{9,10},{10,1... | collective-permute-start | bytes 393224 | tf_op jit(solution)/shard_map/ppermute | solution.py:39
  35.8 8.8 %collective-permute-start.9 = (bf16[384,256]{1,0:T(8,128)(2,1)S(1)}, bf16[384,256]{1,0:T(8,128)(2,1)S(1)}, u32[]{:S(2)}, u32[]{:S(2)}) collective-permute-start(bf16[384,256]{1,0:T(8,128)(2,1)S(1)} %get-tuple-element.19), channel_id=1, source_target_pairs={{0,8},{1,9},{2,10},{3,11},{4,12},{5,13},{6,14},{7,15},{8,0},{9,1},... | collective-permute-start | bytes 589832 | tf_op jit(solution)/shard_map/ppermute | solution.py:39
  35.9 12.2 %collective-permute-start.10 = (bf16[384,256]{1,0:T(8,128)(2,1)S(1)}, bf16[384,256]{1,0:T(8,128)(2,1)S(1)}, u32[]{:S(2)}, u32[]{:S(2)}) collective-permute-start(bf16[384,256]{1,0:T(8,128)(2,1)S(1)} %get-tuple-element.20), channel_id=1, source_target_pairs={{8,16},{9,17},{10,18},{11,19},{12,20},{13,21},{14,22},{15,23},{16,... | collective-permute-start | bytes 589832 | tf_op jit(solution)/shard_map/ppermute | solution.py:39
  48.1 11.1 %collective-permute-start.11 = (bf16[384,512]{1,0:T(8,128)(2,1)S(1)}, bf16[384,512]{1,0:T(8,128)(2,1)S(1)}, u32[]{:S(2)}, u32[]{:S(2)}) collective-permute-start(bf16[384,512]{1,0:T(8,128)(2,1)S(1)} %constant_dynamic-update-slice_fusion.refs_0_), channel_id=1, source_target_pairs={{0,3},{1,0},{2,1},{3,2},{4,7},{5,4},{6,5},{7,6},{8,11},{9,8},{10,9... | collective-permute-start | bytes 1179656 | tf_op jit(solution)/shard_map/ppermute | solution.py:39
  48.2 11.0 %collective-permute-start.14 = (bf16[384,512]{1,0:T(8,128)(2,1)S(1)}, bf16[384,512]{1,0:T(8,128)(2,1)S(1)}, u32[]{:S(2)}, u32[]{:S(2)}) collective-permute-start(bf16[384,512]{1,0:T(8,128)(2,1)S(1)} %constant_dynamic-update-slice_fusion.refs_0_), channel_id=1, source_target_pairs={{0,4},{1,5},{2,6},{3,7},{4,0},{5,1},{6,2},{7,3},{8,12},{9,13},{10,... | collective-permute-start | bytes 1179656 | tf_op jit(solution)/shard_map/ppermute | solution.py:39
  48.4 14.1 %collective-permute-start.19 = (bf16[384,512]{1,0:T(8,128)(2,1)S(1)}, bf16[384,512]{1,0:T(8,128)(2,1)S(1)}, u32[]{:S(2)}, u32[]{:S(2)}) collective-permute-start(bf16[384,512]{1,0:T(8,128)(2,1)S(1)} %constant_dynamic-update-slice_fusion.refs_0_), channel_id=1, source_target_pairs={{0,1},{1,2},{2,3},{3,0},{4,5},{5,6},{6,7},{7,4},{8,9},{9,10},{10,1... | collective-permute-start | bytes 1179656 | tf_op jit(solution)/shard_map/ppermute | solution.py:39
  59.2 9.2 %collective-permute-start.12 = (bf16[384,512]{1,0:T(8,128)(2,1)S(1)}, bf16[384,512]{1,0:T(8,128)(2,1)S(1)}, u32[]{:S(2)}, u32[]{:S(2)}) collective-permute-start(bf16[384,512]{1,0:T(8,128)(2,1)S(1)} %collective-permute-done.11.refs_0_), channel_id=1, source_target_pairs={{0,3},{1,0},{2,1},{3,2},{4,7},{5,4},{6,5},{7,6},{8,11},{9,8},{10,9... | collective-permute-start | bytes 1179656 | tf_op jit(solution)/shard_map/ppermute | solution.py:39
  59.2 10.4 %collective-permute-start.15 = (bf16[384,512]{1,0:T(8,128)(2,1)S(1)}, bf16[384,512]{1,0:T(8,128)(2,1)S(1)}, u32[]{:S(2)}, u32[]{:S(2)}) collective-permute-start(bf16[384,512]{1,0:T(8,128)(2,1)S(1)} %collective-permute-done.14.refs_1_), channel_id=1, source_target_pairs={{0,1},{1,2},{2,3},{3,0},{4,5},{5,6},{6,7},{7,4},{8,9},{9,10},{10,1... | collective-permute-start | bytes 1179656 | tf_op jit(solution)/shard_map/ppermute | solution.py:39
  61.2 9.2 %collective-permute-start.17 = (bf16[384,512]{1,0:T(8,128)(2,1)S(1)}, bf16[384,512]{1,0:T(8,128)(2,1)S(1)}, u32[]{:S(2)}, u32[]{:S(2)}) collective-permute-start(bf16[384,512]{1,0:T(8,128)(2,1)S(1)} %collective-permute-done.11.refs_0_), channel_id=1, source_target_pairs={{0,4},{1,5},{2,6},{3,7},{4,0},{5,1},{6,2},{7,3},{8,12},{9,13},{10,... | collective-permute-start | bytes 1179656 | tf_op jit(solution)/shard_map/ppermute | solution.py:39
  68.4 7.2 %collective-permute-start.13 = (bf16[128,512]{1,0:T(8,128)(2,1)S(1)}, bf16[128,512]{1,0:T(8,128)(2,1)S(1)}, u32[]{:S(2)}, u32[]{:S(2)}) collective-permute-start(bf16[128,512]{1,0:T(8,128)(2,1)S(1)} %slice.39), channel_id=1, source_target_pairs={{0,4},{1,5},{2,6},{3,7},{4,0},{5,1},{6,2},{7,3},{8,12},{9,13},{10,... | collective-permute-start | bytes 393224 | tf_op jit(solution)/shard_map/ppermute | solution.py:39
  69.6 6.3 %collective-permute-start.16 = (bf16[128,512]{1,0:T(8,128)(2,1)S(1)}, bf16[128,512]{1,0:T(8,128)(2,1)S(1)}, u32[]{:S(2)}, u32[]{:S(2)}) collective-permute-start(bf16[128,512]{1,0:T(8,128)(2,1)S(1)} %slice.40), channel_id=1, source_target_pairs={{0,1},{1,2},{2,3},{3,0},{4,5},{5,6},{6,7},{7,4},{8,9},{9,10},{10,1... | collective-permute-start | bytes 393224 | tf_op jit(solution)/shard_map/ppermute | solution.py:39
  70.4 5.4 %collective-permute-start.18 = (bf16[128,512]{1,0:T(8,128)(2,1)S(1)}, bf16[128,512]{1,0:T(8,128)(2,1)S(1)}, u32[]{:S(2)}, u32[]{:S(2)}) collective-permute-start(bf16[128,512]{1,0:T(8,128)(2,1)S(1)} %slice.41), channel_id=1, source_target_pairs={{0,3},{1,0},{2,1},{3,2},{4,7},{5,4},{6,5},{7,6},{8,11},{9,8},{10,9... | collective-permute-start | bytes 393224 | tf_op jit(solution)/shard_map/ppermute | solution.py:39
  77.3 10.7 %collective-permute-start.21 = (bf16[384,256]{1,0:T(8,128)(2,1)S(1)}, bf16[384,256]{1,0:T(8,128)(2,1)S(1)}, u32[]{:S(2)}, u32[]{:S(2)}) collective-permute-start(bf16[384,256]{1,0:T(8,128)(2,1)S(1)} %get-tuple-element.22), channel_id=1, source_target_pairs={{8,16},{9,17},{10,18},{11,19},{12,20},{13,21},{14,22},{15,23},{16,... | collective-permute-start | bytes 589832 | tf_op jit(solution)/shard_map/ppermute | solution.py:39
  88.0 9.2 %collective-permute-start.22 = (bf16[384,512]{1,0:T(8,128)(2,1)S(1)}, bf16[384,512]{1,0:T(8,128)(2,1)S(1)}, u32[]{:S(2)}, u32[]{:S(2)}) collective-permute-start(bf16[384,512]{1,0:T(8,128)(2,1)S(1)} %constant_dynamic-update-slice_fusion.2.refs_0_), channel_id=1, source_target_pairs={{0,3},{1,0},{2,1},{3,2},{4,7},{5,4},{6,5},{7,6},{8,11},{9,8},{10,9... | collective-permute-start | bytes 1179656 | tf_op jit(solution)/shard_map/ppermute | solution.py:39
  91.4 9.5 %collective-permute-start.25 = (bf16[384,512]{1,0:T(8,128)(2,1)S(1)}, bf16[384,512]{1,0:T(8,128)(2,1)S(1)}, u32[]{:S(2)}, u32[]{:S(2)}) collective-permute-start(bf16[384,512]{1,0:T(8,128)(2,1)S(1)} %constant_dynamic-update-slice_fusion.2.refs_0_), channel_id=1, source_target_pairs={{0,4},{1,5},{2,6},{3,7},{4,0},{5,1},{6,2},{7,3},{8,12},{9,13},{10,... | collective-permute-start | bytes 1179656 | tf_op jit(solution)/shard_map/ppermute | solution.py:39
  92.3 10.9 %collective-permute-start.30 = (bf16[384,512]{1,0:T(8,128)(2,1)S(1)}, bf16[384,512]{1,0:T(8,128)(2,1)S(1)}, u32[]{:S(2)}, u32[]{:S(2)}) collective-permute-start(bf16[384,512]{1,0:T(8,128)(2,1)S(1)} %constant_dynamic-update-slice_fusion.2.refs_0_), channel_id=1, source_target_pairs={{0,1},{1,2},{2,3},{3,0},{4,5},{5,6},{6,7},{7,4},{8,9},{9,10},{10,1... | collective-permute-start | bytes 1179656 | tf_op jit(solution)/shard_map/ppermute | solution.py:39
  97.2 9.0 %collective-permute-start.23 = (bf16[384,512]{1,0:T(8,128)(2,1)S(1)}, bf16[384,512]{1,0:T(8,128)(2,1)S(1)}, u32[]{:S(2)}, u32[]{:S(2)}) collective-permute-start(bf16[384,512]{1,0:T(8,128)(2,1)S(1)} %collective-permute-done.22.refs_0_), channel_id=1, source_target_pairs={{0,3},{1,0},{2,1},{3,2},{4,7},{5,4},{6,5},{7,6},{8,11},{9,8},{10,9... | collective-permute-start | bytes 1179656 | tf_op jit(solution)/shard_map/ppermute | solution.py:39
  100.9 9.6 %collective-permute-start.26 = (bf16[384,512]{1,0:T(8,128)(2,1)S(1)}, bf16[384,512]{1,0:T(8,128)(2,1)S(1)}, u32[]{:S(2)}, u32[]{:S(2)}) collective-permute-start(bf16[384,512]{1,0:T(8,128)(2,1)S(1)} %collective-permute-done.25.refs_1_), channel_id=1, source_target_pairs={{0,1},{1,2},{2,3},{3,0},{4,5},{5,6},{6,7},{7,4},{8,9},{9,10},{10,1... | collective-permute-start | bytes 1179656 | tf_op jit(solution)/shard_map/ppermute | solution.py:39
  100.9 9.7 %collective-permute-start.28 = (bf16[384,512]{1,0:T(8,128)(2,1)S(1)}, bf16[384,512]{1,0:T(8,128)(2,1)S(1)}, u32[]{:S(2)}, u32[]{:S(2)}) collective-permute-start(bf16[384,512]{1,0:T(8,128)(2,1)S(1)} %collective-permute-done.22.refs_0_), channel_id=1, source_target_pairs={{0,4},{1,5},{2,6},{3,7},{4,0},{5,1},{6,2},{7,3},{8,12},{9,13},{10,... | collective-permute-start | bytes 1179656 | tf_op jit(solution)/shard_map/ppermute | solution.py:39
  106.2 10.3 %collective-permute-start.24 = (bf16[128,512]{1,0:T(8,128)(2,1)S(1)}, bf16[128,512]{1,0:T(8,128)(2,1)S(1)}, u32[]{:S(2)}, u32[]{:S(2)}) collective-permute-start(bf16[128,512]{1,0:T(8,128)(2,1)S(1)} %slice.42), channel_id=1, source_target_pairs={{0,4},{1,5},{2,6},{3,7},{4,0},{5,1},{6,2},{7,3},{8,12},{9,13},{10,... | collective-permute-start | bytes 393224 | tf_op jit(solution)/shard_map/ppermute | solution.py:39
  110.5 6.3 %collective-permute-start.27 = (bf16[128,512]{1,0:T(8,128)(2,1)S(1)}, bf16[128,512]{1,0:T(8,128)(2,1)S(1)}, u32[]{:S(2)}, u32[]{:S(2)}) collective-permute-start(bf16[128,512]{1,0:T(8,128)(2,1)S(1)} %slice.43), channel_id=1, source_target_pairs={{0,1},{1,2},{2,3},{3,0},{4,5},{5,6},{6,7},{7,4},{8,9},{9,10},{10,1... | collective-permute-start | bytes 393224 | tf_op jit(solution)/shard_map/ppermute | solution.py:39
  110.7 6.1 %collective-permute-start.29 = (bf16[128,512]{1,0:T(8,128)(2,1)S(1)}, bf16[128,512]{1,0:T(8,128)(2,1)S(1)}, u32[]{:S(2)}, u32[]{:S(2)}) collective-permute-start(bf16[128,512]{1,0:T(8,128)(2,1)S(1)} %slice.44), channel_id=1, source_target_pairs={{0,3},{1,0},{2,1},{3,2},{4,7},{5,4},{6,5},{7,6},{8,11},{9,8},{10,9... | collective-permute-start | bytes 393224 | tf_op jit(solution)/shard_map/ppermute | solution.py:39
  118.1 10.6 %collective-permute-start.31 = (bf16[384,256]{1,0:T(8,128)(2,1)S(1)}, bf16[384,256]{1,0:T(8,128)(2,1)S(1)}, u32[]{:S(2)}, u32[]{:S(2)}) collective-permute-start(bf16[384,256]{1,0:T(8,128)(2,1)S(1)} %get-tuple-element.23), channel_id=1, source_target_pairs={{8,16},{9,17},{10,18},{11,19},{12,20},{13,21},{14,22},{15,23},{16,... | collective-permute-start | bytes 589832 | tf_op jit(solution)/shard_map/ppermute | solution.py:39
  124.3 4.4 %collective-permute-start.32 = (bf16[384,256]{1,0:T(8,128)(2,1)S(1)}, bf16[384,256]{1,0:T(8,128)(2,1)S(1)}, u32[]{:S(2)}, u32[]{:S(2)}) collective-permute-start(bf16[384,256]{1,0:T(8,128)(2,1)S(1)} %get-tuple-element.24), channel_id=1, source_target_pairs={{0,8},{1,9},{2,10},{3,11},{4,12},{5,13},{6,14},{7,15},{8,0},{9,1},... | collective-permute-start | bytes 589832 | tf_op jit(solution)/shard_map/ppermute | solution.py:39
  (5 other events, 10.0 us)

commit v4 on v3

--- a/solution.py
+++ b/solution.py
@@ -143,7 +143,7 @@
 
 
 def per_device(layers, rows, waves, operators, sources, source_layer):
-    third = operators.shape[2] // 3
+    half = operators.shape[2] // 2
     where = jnp.stack([lax.axis_index("row"), lax.axis_index("layer")]).astype(jnp.int32)
 
     def move(array, dx, dy):
@@ -160,25 +160,27 @@
         if tick == 0:
             source_term = layer_sources(where, sources, source_layer.reshape(1, -1))
             below, across, total, source_term = lax.optimization_barrier((below, across, total, source_term))
-        far_y = move(below, 0, -1)
+        far_y = [move(below[:half], 0, -1), move(below[half:], 0, -1)]
+        across_above = [move(across[:half], 0, 1), move(across[half:], 0, 1)]
         across_below = move(below, 1, 0)
-        across_above = move(across, 0, 1)
-        part0 = move(far_y[:third], 1, 0)
-        part1 = move(across_above[third : 2 * third], 0, 1)
-        part2 = move(across_below[2 * third :], 0, -1)
+        opposite = [move(far_y[0], 1, 0), move(across_above[1], 0, 1)]
         total = stage(
             operators, where, [((0, 1), [[below]]), ((1, 0), [[across]]), ((0, -1), [[above]])], before=total
         )
         total = stage(
             operators,
             where,
-            [((0, 2), [[far_y]]), ((1, 1), [[across_below]]), ((1, -1), [[across_above]])],
+            [
+                ((0, 2), [[part] for part in far_y]),
+                ((1, -1), [[part] for part in across_above]),
+                ((1, 1), [[across_below]]),
+            ],
             before=total,
         )
         outs = stage(
             operators,
             where,
-            [((1, 2), [[part0], [part1], [part2]])],
+            [((1, 2), [[part] for part in opposite])],
             parity=tick == 0,
             before=total,
             extra=source_term,

time: 130 us -> 128 us (0.985)
  waiting for transfers between devices: 48.4 us -> 45.4 us
    ppermute x33 -> x36, waiting for transfers between devices: 48.4 us -> 45.4 us  [permute(): return lax.ppermute(array, AXES, pairs)]
    ppermute x33 -> x36, starting transfers between devices: 49.5 us -> 50.6 us  [permute(): return lax.ppermute(array, AXES, pairs)]
  transfers between devices with their start and end apart: 33 -> 36, of which waited for: 16 -> 14; matrix products, arithmetic and copies ran while one was open for 0% -> 0% of each run, Pallas kernels for 15% -> 16%
where the time goes in v4:
time: 128 us
  starting transfers between devices  50.6 us (40%)
  waiting for transfers between devices  45.4 us (35%)
  Pallas kernels  23.9 us (19%)
  local copies, waits for them, and re-layouts  6.54 us (5%)
    ppermute x36, starting transfers between devices, permute(): return lax.ppermute(array, AXES, pairs)  50.6 us
    ppermute x36, waiting for transfers between devices, permute(): return lax.ppermute(array, AXES, pairs)  45.4 us
    pallas_call x12, Pallas kernels, stage(): pl.pallas_call(functools.partial(stage_kernel, shifts, layout, parity, be...  23.3 us
    unnamed x10, local copies, waits for them, and re-layouts  6.35 us
  transfers between devices with their start and end apart: 36, of which 14 were waited for; matrix products, arithmetic and copies ran while one was open for 0% of the time, Pallas kernels for 16%

profile of v4, /device:TPU:6, one launch (start us, length us, event | category | flops | bytes accessed | tf_op | source)
XLA Modules:
  0.0 127.7 jit_solution(6111597399523877047)
XLA Ops:
  0.0 3.0 %collective-permute-start = (bf16[384,512]{1,0:T(8,128)(2,1)}, bf16[384,512]{1,0:T(8,128)(2,1)S(1)}, u32[]{:S(2)}, u32[]{:S(2)}) collective-permute-start(bf16[384,512]{1,0:T(8,128)(2,1)} %bitcast.6), channel_id=1, source_target_pairs={{0,3},{1,0},{2,1},{3,2},{4,7},{5,4},{6,5},{7,6},{8,11},{9,8},{10,9... | collective-permute-start | bytes 1179656 | tf_op jit(solution)/shard_map/ppermute | solution.py:39
  6.2 3.7 %copy-done = bf16[1,4,384,3072]{3,2,1,0:T(8,128)(2,1)S(1)} copy-done((bf16[1,4,384,3072]{3,2,1,0:T(8,128)(2,1)S(1)}, bf16[1,4,384,3072]{3,2,1,0:T(8,128)(2,1)}, u32[]{:S(2)}) %copy-start) | copy-done | bytes 9437208
  14.7 2.1 %collective-permute-start.2 = (bf16[192,512]{1,0:T(8,128)(2,1)S(1)}, bf16[192,512]{1,0:T(8,128)(2,1)S(1)}, u32[]{:S(2)}, u32[]{:S(2)}) collective-permute-start(bf16[192,512]{1,0:T(8,128)(2,1)S(1)} %get-tuple-element.38), channel_id=1, source_target_pairs={{0,3},{1,0},{2,1},{3,2},{4,7},{5,4},{6,5},{7,6},{8,11},{9,8},{10,9... | collective-permute-start | bytes 589832 | tf_op jit(solution)/shard_map/ppermute | solution.py:39
  16.9 3.2 %collective-permute-start.6 = (bf16[192,512]{1,0:T(8,128)(2,1)S(1)}, bf16[192,512]{1,0:T(8,128)(2,1)S(1)}, u32[]{:S(2)}, u32[]{:S(2)}) collective-permute-start(bf16[192,512]{1,0:T(8,128)(2,1)S(1)} %get-tuple-element.37), channel_id=1, source_target_pairs={{0,3},{1,0},{2,1},{3,2},{4,7},{5,4},{6,5},{7,6},{8,11},{9,8},{10,9... | collective-permute-start | bytes 589832 | tf_op jit(solution)/shard_map/ppermute | solution.py:39
  20.2 2.1 %collective-permute-done.2.refs_0_ = bf16[192,512]{1,0:T(8,128)(2,1)S(1)} collective-permute-done((bf16[192,512]{1,0:T(8,128)(2,1)S(1)}, bf16[192,512]{1,0:T(8,128)(2,1)S(1)}, u32[]{:S(2)}, u32[]{:S(2)}) %collective-permute-start.2) | collective-permute-done | bytes 196640 | tf_op jit(solution)/shard_map/ppermute | solution.py:39
  23.2 2.5 %collective-permute-done.4.refs_3_ = bf16[192,512]{1,0:T(8,128)(2,1)S(1)} collective-permute-done((bf16[192,512]{1,0:T(8,128)(2,1)S(1)}, bf16[192,512]{1,0:T(8,128)(2,1)S(1)}, u32[]{:S(2)}, u32[]{:S(2)}) %collective-permute-start.4) | collective-permute-done | bytes 196640 | tf_op jit(solution)/shard_map/ppermute | solution.py:39
  25.8 2.6 %shard_map.48.refs_5_ = f32[384,512]{1,0:T(8,128)S(1)} custom-call(s32[2]{0:T(128)S(1)} %pad_add_fusion.where, bf16[1,4,384,3072]{3,2,1,0:T(8,128)(2,1)S(1)} %copy-done, bf16[384,512]{1,0:T(8,128)(2,1)S(1)} %collective-permute-done.refs_0_, bf16[384,512]{1,0:T(8,128)(2,1)S(1)} %collective-permute-done.1.refs_1_, ...), custom_call_target="tpu_custom_call" | custom-call | flops 1811939328 | bytes 4718592 | tf_op jit(solution)/shard_map/pallas_call | solution.py:110
  28.3 1.6 %collective-permute-done.7.refs_2_ = bf16[192,512]{1,0:T(8,128)(2,1)S(1)} collective-permute-done((bf16[192,512]{1,0:T(8,128)(2,1)S(1)}, bf16[192,512]{1,0:T(8,128)(2,1)S(1)}, u32[]{:S(2)}, u32[]{:S(2)}) %collective-permute-start.7) | collective-permute-done | bytes 196640 | tf_op jit(solution)/shard_map/ppermute | solution.py:39
  30.0 2.6 %shard_map.49.refs_2_ = f32[384,512]{1,0:T(8,128)S(1)} custom-call(s32[2]{0:T(128)S(1)} %pad_add_fusion.where, bf16[1,4,384,3072]{3,2,1,0:T(8,128)(2,1)S(1)} %copy-done, bf16[192,512]{1,0:T(8,128)(2,1)S(1)} %collective-permute-done.2.refs_0_, bf16[192,512]{1,0:T(8,128)(2,1)S(1)} %collective-permute-done.6.refs_1_, ...), custom_call_target="tpu_custom_call" | custom-call | flops 1811939328 | bytes 4718592 | tf_op jit(solution)/shard_map/pallas_call | solution.py:110
  34.1 8.7 %collective-permute-start.11 = (bf16[384,256]{1,0:T(8,128)(2,1)S(1)}, bf16[384,256]{1,0:T(8,128)(2,1)S(1)}, u32[]{:S(2)}, u32[]{:S(2)}) collective-permute-start(bf16[384,256]{1,0:T(8,128)(2,1)S(1)} %get-tuple-element.20), channel_id=1, source_target_pairs={{8,16},{9,17},{10,18},{11,19},{12,20},{13,21},{14,22},{15,23},{16,... | collective-permute-start | bytes 589832 | tf_op jit(solution)/shard_map/ppermute | solution.py:39
  42.8 3.4 %collective-permute-done.11 = bf16[384,256]{1,0:T(8,128)(2,1)S(1)} collective-permute-done((bf16[384,256]{1,0:T(8,128)(2,1)S(1)}, bf16[384,256]{1,0:T(8,128)(2,1)S(1)}, u32[]{:S(2)}, u32[]{:S(2)}) %collective-permute-start.11) | collective-permute-done | bytes 196640 | tf_op jit(solution)/shard_map/ppermute | solution.py:39
  46.2 1.8 %collective-permute-start.12 = (bf16[384,512]{1,0:T(8,128)(2,1)S(1)}, bf16[384,512]{1,0:T(8,128)(2,1)S(1)}, u32[]{:S(2)}, u32[]{:S(2)}) collective-permute-start(bf16[384,512]{1,0:T(8,128)(2,1)S(1)} %constant_dynamic-update-slice_fusion.refs_0_), channel_id=1, source_target_pairs={{0,3},{1,0},{2,1},{3,2},{4,7},{5,4},{6,5},{7,6},{8,11},{9,8},{10,9... | collective-permute-start | bytes 1179656 | tf_op jit(solution)/shard_map/ppermute | solution.py:39
  48.6 8.8 %collective-permute-done.12.refs_0_ = bf16[384,512]{1,0:T(8,128)(2,1)S(1)} collective-permute-done((bf16[384,512]{1,0:T(8,128)(2,1)S(1)}, bf16[384,512]{1,0:T(8,128)(2,1)S(1)}, u32[]{:S(2)}, u32[]{:S(2)}) %collective-permute-start.12) | collective-permute-done | bytes 393248 | tf_op jit(solution)/shard_map/ppermute | solution.py:39
  59.8 2.5 %collective-permute-start.18 = (bf16[192,512]{1,0:T(8,128)(2,1)S(1)}, bf16[192,512]{1,0:T(8,128)(2,1)S(1)}, u32[]{:S(2)}, u32[]{:S(2)}) collective-permute-start(bf16[192,512]{1,0:T(8,128)(2,1)S(1)} %get-tuple-element.33), channel_id=1, source_target_pairs={{0,3},{1,0},{2,1},{3,2},{4,7},{5,4},{6,5},{7,6},{8,11},{9,8},{10,9... | collective-permute-start | bytes 589832 | tf_op jit(solution)/shard_map/ppermute | solution.py:39
  63.7 2.1 %collective-permute-start.14 = (bf16[192,512]{1,0:T(8,128)(2,1)S(1)}, bf16[192,512]{1,0:T(8,128)(2,1)S(1)}, u32[]{:S(2)}, u32[]{:S(2)}) collective-permute-start(bf16[192,512]{1,0:T(8,128)(2,1)S(1)} %collective-permute-done.13.refs_0_), channel_id=1, source_target_pairs={{0,4},{1,5},{2,6},{3,7},{4,0},{5,1},{6,2},{7,3},{8,12},{9,13},{10,... | collective-permute-start | bytes 589832 | tf_op jit(solution)/shard_map/ppermute | solution.py:39
  67.0 2.6 %shard_map.52.refs_5_ = f32[384,512]{1,0:T(8,128)S(1)} custom-call(s32[2]{0:T(128)S(1)} %pad_add_fusion.where, bf16[1,4,384,3072]{3,2,1,0:T(8,128)(2,1)S(1)} %copy-done, bf16[384,512]{1,0:T(8,128)(2,1)S(1)} %collective-permute-done.12.refs_0_, bf16[384,512]{1,0:T(8,128)(2,1)S(1)} %collective-permute-done.15.refs_1_, ...), custom_call_target="tpu_custom_call" | custom-call | flops 1811939328 | bytes 4718592 | tf_op jit(solution)/shard_map/pallas_call | solution.py:110
  69.6 2.6 %shard_map.53.refs_2_ = f32[384,512]{1,0:T(8,128)S(1)} custom-call(s32[2]{0:T(128)S(1)} %pad_add_fusion.where, bf16[1,4,384,3072]{3,2,1,0:T(8,128)(2,1)S(1)} %copy-done, bf16[192,512]{1,0:T(8,128)(2,1)S(1)} %collective-permute-done.13.refs_0_, bf16[192,512]{1,0:T(8,128)(2,1)S(1)} %collective-permute-done.18.refs_1_, ...), custom_call_target="tpu_custom_call" | custom-call | flops 1811939328 | bytes 4718592 | tf_op jit(solution)/shard_map/pallas_call | solution.py:110
  72.2 1.7 %collective-permute-done.17.refs_1_ = bf16[192,512]{1,0:T(8,128)(2,1)S(1)} collective-permute-done((bf16[192,512]{1,0:T(8,128)(2,1)S(1)}, bf16[192,512]{1,0:T(8,128)(2,1)S(1)}, u32[]{:S(2)}, u32[]{:S(2)}) %collective-permute-start.17) | collective-permute-done | bytes 196640 | tf_op jit(solution)/shard_map/ppermute | solution.py:39
  75.3 5.2 %collective-permute-start.23 = (bf16[384,256]{1,0:T(8,128)(2,1)S(1)}, bf16[384,256]{1,0:T(8,128)(2,1)S(1)}, u32[]{:S(2)}, u32[]{:S(2)}) collective-permute-start(bf16[384,256]{1,0:T(8,128)(2,1)S(1)} %get-tuple-element.22), channel_id=1, source_target_pairs={{8,16},{9,17},{10,18},{11,19},{12,20},{13,21},{14,22},{15,23},{16,... | collective-permute-start | bytes 589832 | tf_op jit(solution)/shard_map/ppermute | solution.py:39
  80.6 5.5 %collective-permute-done.23 = bf16[384,256]{1,0:T(8,128)(2,1)S(1)} collective-permute-done((bf16[384,256]{1,0:T(8,128)(2,1)S(1)}, bf16[384,256]{1,0:T(8,128)(2,1)S(1)}, u32[]{:S(2)}, u32[]{:S(2)}) %collective-permute-start.23) | collective-permute-done | bytes 196640 | tf_op jit(solution)/shard_map/ppermute | solution.py:39
  86.1 1.6 %collective-permute-start.24 = (bf16[384,512]{1,0:T(8,128)(2,1)S(1)}, bf16[384,512]{1,0:T(8,128)(2,1)S(1)}, u32[]{:S(2)}, u32[]{:S(2)}) collective-permute-start(bf16[384,512]{1,0:T(8,128)(2,1)S(1)} %constant_dynamic-update-slice_fusion.2.refs_0_), channel_id=1, source_target_pairs={{0,3},{1,0},{2,1},{3,2},{4,7},{5,4},{6,5},{7,6},{8,11},{9,8},{10,9... | collective-permute-start | bytes 1179656 | tf_op jit(solution)/shard_map/ppermute | solution.py:39
  87.7 2.1 %collective-permute-start.27 = (bf16[384,512]{1,0:T(8,128)(2,1)S(1)}, bf16[384,512]{1,0:T(8,128)(2,1)S(1)}, u32[]{:S(2)}, u32[]{:S(2)}) collective-permute-start(bf16[384,512]{1,0:T(8,128)(2,1)S(1)} %constant_dynamic-update-slice_fusion.2.refs_0_), channel_id=1, source_target_pairs={{0,4},{1,5},{2,6},{3,7},{4,0},{5,1},{6,2},{7,3},{8,12},{9,13},{10,... | collective-permute-start | bytes 1179656 | tf_op jit(solution)/shard_map/ppermute | solution.py:39
  90.3 5.3 %collective-permute-done.24.refs_0_ = bf16[384,512]{1,0:T(8,128)(2,1)S(1)} collective-permute-done((bf16[384,512]{1,0:T(8,128)(2,1)S(1)}, bf16[384,512]{1,0:T(8,128)(2,1)S(1)}, u32[]{:S(2)}, u32[]{:S(2)}) %collective-permute-start.24) | collective-permute-done | bytes 393248 | tf_op jit(solution)/shard_map/ppermute | solution.py:39
  95.6 1.6 %collective-permute-start.25 = (bf16[192,512]{1,0:T(8,128)(2,1)S(1)}, bf16[192,512]{1,0:T(8,128)(2,1)S(1)}, u32[]{:S(2)}, u32[]{:S(2)}) collective-permute-start(bf16[192,512]{1,0:T(8,128)(2,1)S(1)} %get-tuple-element.30), channel_id=1, source_target_pairs={{0,3},{1,0},{2,1},{3,2},{4,7},{5,4},{6,5},{7,6},{8,11},{9,8},{10,9... | collective-permute-start | bytes 589832 | tf_op jit(solution)/shard_map/ppermute | solution.py:39
  97.2 2.1 %collective-permute-start.32 = (bf16[384,512]{1,0:T(8,128)(2,1)S(1)}, bf16[384,512]{1,0:T(8,128)(2,1)S(1)}, u32[]{:S(2)}, u32[]{:S(2)}) collective-permute-start(bf16[384,512]{1,0:T(8,128)(2,1)S(1)} %collective-permute-done.24.refs_0_), channel_id=1, source_target_pairs={{0,4},{1,5},{2,6},{3,7},{4,0},{5,1},{6,2},{7,3},{8,12},{9,13},{10,... | collective-permute-start | bytes 1179656 | tf_op jit(solution)/shard_map/ppermute | solution.py:39
  99.9 2.7 %collective-permute-start.30 = (bf16[192,512]{1,0:T(8,128)(2,1)S(1)}, bf16[192,512]{1,0:T(8,128)(2,1)S(1)}, u32[]{:S(2)}, u32[]{:S(2)}) collective-permute-start(bf16[192,512]{1,0:T(8,128)(2,1)S(1)} %get-tuple-element.29), channel_id=1, source_target_pairs={{0,3},{1,0},{2,1},{3,2},{4,7},{5,4},{6,5},{7,6},{8,11},{9,8},{10,9... | collective-permute-start | bytes 589832 | tf_op jit(solution)/shard_map/ppermute | solution.py:39
  104.1 4.0 %collective-permute-done.28.refs_3_ = bf16[192,512]{1,0:T(8,128)(2,1)S(1)} collective-permute-done((bf16[192,512]{1,0:T(8,128)(2,1)S(1)}, bf16[192,512]{1,0:T(8,128)(2,1)S(1)}, u32[]{:S(2)}, u32[]{:S(2)}) %collective-permute-start.28) | collective-permute-done | bytes 196640 | tf_op jit(solution)/shard_map/ppermute | solution.py:39
  108.1 2.6 %shard_map.56.refs_5_ = f32[384,512]{1,0:T(8,128)S(1)} custom-call(s32[2]{0:T(128)S(1)} %pad_add_fusion.where, bf16[1,4,384,3072]{3,2,1,0:T(8,128)(2,1)S(1)} %copy-done, bf16[384,512]{1,0:T(8,128)(2,1)S(1)} %collective-permute-done.24.refs_0_, bf16[384,512]{1,0:T(8,128)(2,1)S(1)} %collective-permute-done.27.refs_1_, ...), custom_call_target="tpu_custom_call" | custom-call | flops 1811939328 | bytes 4718592 | tf_op jit(solution)/shard_map/pallas_call | solution.py:110
  110.6 2.6 %shard_map.57.refs_2_ = f32[384,512]{1,0:T(8,128)S(1)} custom-call(s32[2]{0:T(128)S(1)} %pad_add_fusion.where, bf16[1,4,384,3072]{3,2,1,0:T(8,128)(2,1)S(1)} %copy-done, bf16[192,512]{1,0:T(8,128)(2,1)S(1)} %collective-permute-done.25.refs_0_, bf16[192,512]{1,0:T(8,128)(2,1)S(1)} %collective-permute-done.30.refs_1_, ...), custom_call_target="tpu_custom_call" | custom-call | flops 1811939328 | bytes 4718592 | tf_op jit(solution)/shard_map/pallas_call | solution.py:110
  113.2 1.7 %collective-permute-done.29.refs_1_ = bf16[192,512]{1,0:T(8,128)(2,1)S(1)} collective-permute-done((bf16[192,512]{1,0:T(8,128)(2,1)S(1)}, bf16[192,512]{1,0:T(8,128)(2,1)S(1)}, u32[]{:S(2)}, u32[]{:S(2)}) %collective-permute-start.29) | collective-permute-done | bytes 196640 | tf_op jit(solution)/shard_map/ppermute | solution.py:39
  116.3 4.7 %collective-permute-start.34 = (bf16[384,256]{1,0:T(8,128)(2,1)S(1)}, bf16[384,256]{1,0:T(8,128)(2,1)S(1)}, u32[]{:S(2)}, u32[]{:S(2)}) collective-permute-start(bf16[384,256]{1,0:T(8,128)(2,1)S(1)} %get-tuple-element.23), channel_id=1, source_target_pairs={{8,16},{9,17},{10,18},{11,19},{12,20},{13,21},{14,22},{15,23},{16,... | collective-permute-start | bytes 589832 | tf_op jit(solution)/shard_map/ppermute | solution.py:39
  121.1 5.8 %collective-permute-done.34 = bf16[384,256]{1,0:T(8,128)(2,1)S(1)} collective-permute-done((bf16[384,256]{1,0:T(8,128)(2,1)S(1)}, bf16[384,256]{1,0:T(8,128)(2,1)S(1)}, u32[]{:S(2)}, u32[]{:S(2)}) %collective-permute-start.34) | collective-permute-done | bytes 196640 | tf_op jit(solution)/shard_map/ppermute | solution.py:39
  (74 shorter events, 22.5 us)
Async XLA Ops:
  0.0 12.2 %collective-permute-start = (bf16[384,512]{1,0:T(8,128)(2,1)}, bf16[384,512]{1,0:T(8,128)(2,1)S(1)}, u32[]{:S(2)}, u32[]{:S(2)}) collective-permute-start(bf16[384,512]{1,0:T(8,128)(2,1)} %bitcast.6), channel_id=1, source_target_pairs={{0,3},{1,0},{2,1},{3,2},{4,7},{5,4},{6,5},{7,6},{8,11},{9,8},{10,9... | collective-permute-start | bytes 1179656 | tf_op jit(solution)/shard_map/ppermute | solution.py:39
  3.0 10.8 %collective-permute-start.1 = (bf16[384,512]{1,0:T(8,128)(2,1)}, bf16[384,512]{1,0:T(8,128)(2,1)S(1)}, u32[]{:S(2)}, u32[]{:S(2)}) collective-permute-start(bf16[384,512]{1,0:T(8,128)(2,1)} %bitcast.7), channel_id=1, source_target_pairs={{0,4},{1,5},{2,6},{3,7},{4,0},{5,1},{6,2},{7,3},{8,12},{9,13},{10,... | collective-permute-start | bytes 1179656 | tf_op jit(solution)/shard_map/ppermute | solution.py:39
  3.8 16.3 %collective-permute-start.9 = (bf16[384,512]{1,0:T(8,128)(2,1)}, bf16[384,512]{1,0:T(8,128)(2,1)S(1)}, u32[]{:S(2)}, u32[]{:S(2)}) collective-permute-start(bf16[384,512]{1,0:T(8,128)(2,1)} %bitcast.8), channel_id=1, source_target_pairs={{0,1},{1,2},{2,3},{3,0},{4,5},{5,6},{6,7},{7,4},{8,9},{9,10},{10,1... | collective-permute-start | bytes 1179656 | tf_op jit(solution)/shard_map/ppermute | solution.py:39
  13.8 16.1 %collective-permute-start.8 = (bf16[384,512]{1,0:T(8,128)(2,1)S(1)}, bf16[384,512]{1,0:T(8,128)(2,1)S(1)}, u32[]{:S(2)}, u32[]{:S(2)}) collective-permute-start(bf16[384,512]{1,0:T(8,128)(2,1)S(1)} %collective-permute-done.refs_0_), channel_id=1, source_target_pairs={{0,4},{1,5},{2,6},{3,7},{4,0},{5,1},{6,2},{7,3},{8,12},{9,13},{10,... | collective-permute-start | bytes 1179656 | tf_op jit(solution)/shard_map/ppermute | solution.py:39
  14.7 7.5 %collective-permute-start.2 = (bf16[192,512]{1,0:T(8,128)(2,1)S(1)}, bf16[192,512]{1,0:T(8,128)(2,1)S(1)}, u32[]{:S(2)}, u32[]{:S(2)}) collective-permute-start(bf16[192,512]{1,0:T(8,128)(2,1)S(1)} %get-tuple-element.38), channel_id=1, source_target_pairs={{0,3},{1,0},{2,1},{3,2},{4,7},{5,4},{6,5},{7,6},{8,11},{9,8},{10,9... | collective-permute-start | bytes 589832 | tf_op jit(solution)/shard_map/ppermute | solution.py:39
  16.8 8.9 %collective-permute-start.4 = (bf16[192,512]{1,0:T(8,128)(2,1)S(1)}, bf16[192,512]{1,0:T(8,128)(2,1)S(1)}, u32[]{:S(2)}, u32[]{:S(2)}) collective-permute-start(bf16[192,512]{1,0:T(8,128)(2,1)S(1)} %get-tuple-element.36), channel_id=1, source_target_pairs={{0,1},{1,2},{2,3},{3,0},{4,5},{5,6},{6,7},{7,4},{8,9},{9,10},{10,1... | collective-permute-start | bytes 589832 | tf_op jit(solution)/shard_map/ppermute | solution.py:39
  16.9 11.4 %collective-permute-start.6 = (bf16[192,512]{1,0:T(8,128)(2,1)S(1)}, bf16[192,512]{1,0:T(8,128)(2,1)S(1)}, u32[]{:S(2)}, u32[]{:S(2)}) collective-permute-start(bf16[192,512]{1,0:T(8,128)(2,1)S(1)} %get-tuple-element.37), channel_id=1, source_target_pairs={{0,3},{1,0},{2,1},{3,2},{4,7},{5,4},{6,5},{7,6},{8,11},{9,8},{10,9... | collective-permute-start | bytes 589832 | tf_op jit(solution)/shard_map/ppermute | solution.py:39
  20.2 9.8 %collective-permute-start.7 = (bf16[192,512]{1,0:T(8,128)(2,1)S(1)}, bf16[192,512]{1,0:T(8,128)(2,1)S(1)}, u32[]{:S(2)}, u32[]{:S(2)}) collective-permute-start(bf16[192,512]{1,0:T(8,128)(2,1)S(1)} %get-tuple-element.35), channel_id=1, source_target_pairs={{0,1},{1,2},{2,3},{3,0},{4,5},{5,6},{6,7},{7,4},{8,9},{9,10},{10,1... | collective-permute-start | bytes 589832 | tf_op jit(solution)/shard_map/ppermute | solution.py:39
  22.2 10.3 %collective-permute-start.3 = (bf16[192,512]{1,0:T(8,128)(2,1)S(1)}, bf16[192,512]{1,0:T(8,128)(2,1)S(1)}, u32[]{:S(2)}, u32[]{:S(2)}) collective-permute-start(bf16[192,512]{1,0:T(8,128)(2,1)S(1)} %collective-permute-done.2.refs_0_), channel_id=1, source_target_pairs={{0,4},{1,5},{2,6},{3,7},{4,0},{5,1},{6,2},{7,3},{8,12},{9,13},{10,... | collective-permute-start | bytes 589832 | tf_op jit(solution)/shard_map/ppermute | solution.py:39
  25.8 6.9 %collective-permute-start.5 = (bf16[192,512]{1,0:T(8,128)(2,1)S(1)}, bf16[192,512]{1,0:T(8,128)(2,1)S(1)}, u32[]{:S(2)}, u32[]{:S(2)}) collective-permute-start(bf16[192,512]{1,0:T(8,128)(2,1)S(1)} %collective-permute-done.4.refs_3_), channel_id=1, source_target_pairs={{0,1},{1,2},{2,3},{3,0},{4,5},{5,6},{6,7},{7,4},{8,9},{9,10},{10,1... | collective-permute-start | bytes 589832 | tf_op jit(solution)/shard_map/ppermute | solution.py:39
  34.0 8.8 %collective-permute-start.10 = (bf16[384,256]{1,0:T(8,128)(2,1)S(1)}, bf16[384,256]{1,0:T(8,128)(2,1)S(1)}, u32[]{:S(2)}, u32[]{:S(2)}) collective-permute-start(bf16[384,256]{1,0:T(8,128)(2,1)S(1)} %get-tuple-element.19), channel_id=1, source_target_pairs={{0,8},{1,9},{2,10},{3,11},{4,12},{5,13},{6,14},{7,15},{8,0},{9,1},... | collective-permute-start | bytes 589832 | tf_op jit(solution)/shard_map/ppermute | solution.py:39
  34.1 12.1 %collective-permute-start.11 = (bf16[384,256]{1,0:T(8,128)(2,1)S(1)}, bf16[384,256]{1,0:T(8,128)(2,1)S(1)}, u32[]{:S(2)}, u32[]{:S(2)}) collective-permute-start(bf16[384,256]{1,0:T(8,128)(2,1)S(1)} %get-tuple-element.20), channel_id=1, source_target_pairs={{8,16},{9,17},{10,18},{11,19},{12,20},{13,21},{14,22},{15,23},{16,... | collective-permute-start | bytes 589832 | tf_op jit(solution)/shard_map/ppermute | solution.py:39
  46.2 11.1 %collective-permute-start.12 = (bf16[384,512]{1,0:T(8,128)(2,1)S(1)}, bf16[384,512]{1,0:T(8,128)(2,1)S(1)}, u32[]{:S(2)}, u32[]{:S(2)}) collective-permute-start(bf16[384,512]{1,0:T(8,128)(2,1)S(1)} %constant_dynamic-update-slice_fusion.refs_0_), channel_id=1, source_target_pairs={{0,3},{1,0},{2,1},{3,2},{4,7},{5,4},{6,5},{7,6},{8,11},{9,8},{10,9... | collective-permute-start | bytes 1179656 | tf_op jit(solution)/shard_map/ppermute | solution.py:39
  48.0 10.9 %collective-permute-start.15 = (bf16[384,512]{1,0:T(8,128)(2,1)S(1)}, bf16[384,512]{1,0:T(8,128)(2,1)S(1)}, u32[]{:S(2)}, u32[]{:S(2)}) collective-permute-start(bf16[384,512]{1,0:T(8,128)(2,1)S(1)} %constant_dynamic-update-slice_fusion.refs_0_), channel_id=1, source_target_pairs={{0,4},{1,5},{2,6},{3,7},{4,0},{5,1},{6,2},{7,3},{8,12},{9,13},{10,... | collective-permute-start | bytes 1179656 | tf_op jit(solution)/shard_map/ppermute | solution.py:39
  48.1 14.2 %collective-permute-start.21 = (bf16[384,512]{1,0:T(8,128)(2,1)S(1)}, bf16[384,512]{1,0:T(8,128)(2,1)S(1)}, u32[]{:S(2)}, u32[]{:S(2)}) collective-permute-start(bf16[384,512]{1,0:T(8,128)(2,1)S(1)} %constant_dynamic-update-slice_fusion.refs_0_), channel_id=1, source_target_pairs={{0,1},{1,2},{2,3},{3,0},{4,5},{5,6},{6,7},{7,4},{8,9},{9,10},{10,1... | collective-permute-start | bytes 1179656 | tf_op jit(solution)/shard_map/ppermute | solution.py:39
  59.0 10.6 %collective-permute-start.20 = (bf16[384,512]{1,0:T(8,128)(2,1)S(1)}, bf16[384,512]{1,0:T(8,128)(2,1)S(1)}, u32[]{:S(2)}, u32[]{:S(2)}) collective-permute-start(bf16[384,512]{1,0:T(8,128)(2,1)S(1)} %collective-permute-done.12.refs_0_), channel_id=1, source_target_pairs={{0,4},{1,5},{2,6},{3,7},{4,0},{5,1},{6,2},{7,3},{8,12},{9,13},{10,... | collective-permute-start | bytes 1179656 | tf_op jit(solution)/shard_map/ppermute | solution.py:39
  59.0 8.0 %collective-permute-start.16 = (bf16[192,512]{1,0:T(8,128)(2,1)S(1)}, bf16[192,512]{1,0:T(8,128)(2,1)S(1)}, u32[]{:S(2)}, u32[]{:S(2)}) collective-permute-start(bf16[192,512]{1,0:T(8,128)(2,1)S(1)} %get-tuple-element.32), channel_id=1, source_target_pairs={{0,1},{1,2},{2,3},{3,0},{4,5},{5,6},{6,7},{7,4},{8,9},{9,10},{10,1... | collective-permute-start | bytes 589832 | tf_op jit(solution)/shard_map/ppermute | solution.py:39
  59.8 9.8 %collective-permute-start.18 = (bf16[192,512]{1,0:T(8,128)(2,1)S(1)}, bf16[192,512]{1,0:T(8,128)(2,1)S(1)}, u32[]{:S(2)}, u32[]{:S(2)}) collective-permute-start(bf16[192,512]{1,0:T(8,128)(2,1)S(1)} %get-tuple-element.33), channel_id=1, source_target_pairs={{0,3},{1,0},{2,1},{3,2},{4,7},{5,4},{6,5},{7,6},{8,11},{9,8},{10,9... | collective-permute-start | bytes 589832 | tf_op jit(solution)/shard_map/ppermute | solution.py:39
  62.3 7.3 %collective-permute-start.19 = (bf16[192,512]{1,0:T(8,128)(2,1)S(1)}, bf16[192,512]{1,0:T(8,128)(2,1)S(1)}, u32[]{:S(2)}, u32[]{:S(2)}) collective-permute-start(bf16[192,512]{1,0:T(8,128)(2,1)S(1)} %get-tuple-element.31), channel_id=1, source_target_pairs={{0,1},{1,2},{2,3},{3,0},{4,5},{5,6},{6,7},{7,4},{8,9},{9,10},{10,1... | collective-permute-start | bytes 589832 | tf_op jit(solution)/shard_map/ppermute | solution.py:39
  63.7 8.5 %collective-permute-start.14 = (bf16[192,512]{1,0:T(8,128)(2,1)S(1)}, bf16[192,512]{1,0:T(8,128)(2,1)S(1)}, u32[]{:S(2)}, u32[]{:S(2)}) collective-permute-start(bf16[192,512]{1,0:T(8,128)(2,1)S(1)} %collective-permute-done.13.refs_0_), channel_id=1, source_target_pairs={{0,4},{1,5},{2,6},{3,7},{4,0},{5,1},{6,2},{7,3},{8,12},{9,13},{10,... | collective-permute-start | bytes 589832 | tf_op jit(solution)/shard_map/ppermute | solution.py:39
  67.0 6.9 %collective-permute-start.17 = (bf16[192,512]{1,0:T(8,128)(2,1)S(1)}, bf16[192,512]{1,0:T(8,128)(2,1)S(1)}, u32[]{:S(2)}, u32[]{:S(2)}) collective-permute-start(bf16[192,512]{1,0:T(8,128)(2,1)S(1)} %collective-permute-done.16.refs_3_), channel_id=1, source_target_pairs={{0,1},{1,2},{2,3},{3,0},{4,5},{5,6},{6,7},{7,4},{8,9},{9,10},{10,1... | collective-permute-start | bytes 589832 | tf_op jit(solution)/shard_map/ppermute | solution.py:39
  75.3 10.7 %collective-permute-start.23 = (bf16[384,256]{1,0:T(8,128)(2,1)S(1)}, bf16[384,256]{1,0:T(8,128)(2,1)S(1)}, u32[]{:S(2)}, u32[]{:S(2)}) collective-permute-start(bf16[384,256]{1,0:T(8,128)(2,1)S(1)} %get-tuple-element.22), channel_id=1, source_target_pairs={{8,16},{9,17},{10,18},{11,19},{12,20},{13,21},{14,22},{15,23},{16,... | collective-permute-start | bytes 589832 | tf_op jit(solution)/shard_map/ppermute | solution.py:39
  86.1 9.5 %collective-permute-start.24 = (bf16[384,512]{1,0:T(8,128)(2,1)S(1)}, bf16[384,512]{1,0:T(8,128)(2,1)S(1)}, u32[]{:S(2)}, u32[]{:S(2)}) collective-permute-start(bf16[384,512]{1,0:T(8,128)(2,1)S(1)} %constant_dynamic-update-slice_fusion.2.refs_0_), channel_id=1, source_target_pairs={{0,3},{1,0},{2,1},{3,2},{4,7},{5,4},{6,5},{7,6},{8,11},{9,8},{10,9... | collective-permute-start | bytes 1179656 | tf_op jit(solution)/shard_map/ppermute | solution.py:39
  87.7 11.6 %collective-permute-start.27 = (bf16[384,512]{1,0:T(8,128)(2,1)S(1)}, bf16[384,512]{1,0:T(8,128)(2,1)S(1)}, u32[]{:S(2)}, u32[]{:S(2)}) collective-permute-start(bf16[384,512]{1,0:T(8,128)(2,1)S(1)} %constant_dynamic-update-slice_fusion.2.refs_0_), channel_id=1, source_target_pairs={{0,4},{1,5},{2,6},{3,7},{4,0},{5,1},{6,2},{7,3},{8,12},{9,13},{10,... | collective-permute-start | bytes 1179656 | tf_op jit(solution)/shard_map/ppermute | solution.py:39
  89.8 12.9 %collective-permute-start.33 = (bf16[384,512]{1,0:T(8,128)(2,1)S(1)}, bf16[384,512]{1,0:T(8,128)(2,1)S(1)}, u32[]{:S(2)}, u32[]{:S(2)}) collective-permute-start(bf16[384,512]{1,0:T(8,128)(2,1)S(1)} %constant_dynamic-update-slice_fusion.2.refs_0_), channel_id=1, source_target_pairs={{0,1},{1,2},{2,3},{3,0},{4,5},{5,6},{6,7},{7,4},{8,9},{9,10},{10,1... | collective-permute-start | bytes 1179656 | tf_op jit(solution)/shard_map/ppermute | solution.py:39
  95.6 8.4 %collective-permute-start.25 = (bf16[192,512]{1,0:T(8,128)(2,1)S(1)}, bf16[192,512]{1,0:T(8,128)(2,1)S(1)}, u32[]{:S(2)}, u32[]{:S(2)}) collective-permute-start(bf16[192,512]{1,0:T(8,128)(2,1)S(1)} %get-tuple-element.30), channel_id=1, source_target_pairs={{0,3},{1,0},{2,1},{3,2},{4,7},{5,4},{6,5},{7,6},{8,11},{9,8},{10,9... | collective-permute-start | bytes 589832 | tf_op jit(solution)/shard_map/ppermute | solution.py:39
  97.2 13.4 %collective-permute-start.32 = (bf16[384,512]{1,0:T(8,128)(2,1)S(1)}, bf16[384,512]{1,0:T(8,128)(2,1)S(1)}, u32[]{:S(2)}, u32[]{:S(2)}) collective-permute-start(bf16[384,512]{1,0:T(8,128)(2,1)S(1)} %collective-permute-done.24.refs_0_), channel_id=1, source_target_pairs={{0,4},{1,5},{2,6},{3,7},{4,0},{5,1},{6,2},{7,3},{8,12},{9,13},{10,... | collective-permute-start | bytes 1179656 | tf_op jit(solution)/shard_map/ppermute | solution.py:39
  99.3 8.7 %collective-permute-start.28 = (bf16[192,512]{1,0:T(8,128)(2,1)S(1)}, bf16[192,512]{1,0:T(8,128)(2,1)S(1)}, u32[]{:S(2)}, u32[]{:S(2)}) collective-permute-start(bf16[192,512]{1,0:T(8,128)(2,1)S(1)} %get-tuple-element.28), channel_id=1, source_target_pairs={{0,1},{1,2},{2,3},{3,0},{4,5},{5,6},{6,7},{7,4},{8,9},{9,10},{10,1... | collective-permute-start | bytes 589832 | tf_op jit(solution)/shard_map/ppermute | solution.py:39
  99.9 10.7 %collective-permute-start.30 = (bf16[192,512]{1,0:T(8,128)(2,1)S(1)}, bf16[192,512]{1,0:T(8,128)(2,1)S(1)}, u32[]{:S(2)}, u32[]{:S(2)}) collective-permute-start(bf16[192,512]{1,0:T(8,128)(2,1)S(1)} %get-tuple-element.29), channel_id=1, source_target_pairs={{0,3},{1,0},{2,1},{3,2},{4,7},{5,4},{6,5},{7,6},{8,11},{9,8},{10,9... | collective-permute-start | bytes 589832 | tf_op jit(solution)/shard_map/ppermute | solution.py:39
  102.6 8.0 %collective-permute-start.31 = (bf16[192,512]{1,0:T(8,128)(2,1)S(1)}, bf16[192,512]{1,0:T(8,128)(2,1)S(1)}, u32[]{:S(2)}, u32[]{:S(2)}) collective-permute-start(bf16[192,512]{1,0:T(8,128)(2,1)S(1)} %get-tuple-element.27), channel_id=1, source_target_pairs={{0,1},{1,2},{2,3},{3,0},{4,5},{5,6},{6,7},{7,4},{8,9},{9,10},{10,1... | collective-permute-start | bytes 589832 | tf_op jit(solution)/shard_map/ppermute | solution.py:39
  104.0 9.2 %collective-permute-start.26 = (bf16[192,512]{1,0:T(8,128)(2,1)S(1)}, bf16[192,512]{1,0:T(8,128)(2,1)S(1)}, u32[]{:S(2)}, u32[]{:S(2)}) collective-permute-start(bf16[192,512]{1,0:T(8,128)(2,1)S(1)} %collective-permute-done.25.refs_0_), channel_id=1, source_target_pairs={{0,4},{1,5},{2,6},{3,7},{4,0},{5,1},{6,2},{7,3},{8,12},{9,13},{10,... | collective-permute-start | bytes 589832 | tf_op jit(solution)/shard_map/ppermute | solution.py:39
  116.3 10.6 %collective-permute-start.34 = (bf16[384,256]{1,0:T(8,128)(2,1)S(1)}, bf16[384,256]{1,0:T(8,128)(2,1)S(1)}, u32[]{:S(2)}, u32[]{:S(2)}) collective-permute-start(bf16[384,256]{1,0:T(8,128)(2,1)S(1)} %get-tuple-element.23), channel_id=1, source_target_pairs={{8,16},{9,17},{10,18},{11,19},{12,20},{13,21},{14,22},{15,23},{16,... | collective-permute-start | bytes 589832 | tf_op jit(solution)/shard_map/ppermute | solution.py:39
  (8 other events, 30.7 us)

commit v5 on v4

--- a/solution.py
+++ b/solution.py
@@ -159,7 +159,7 @@
         total = stage(operators, where, [((0, 0), [own])])
         if tick == 0:
             source_term = layer_sources(where, sources, source_layer.reshape(1, -1))
-            below, across, total, source_term = lax.optimization_barrier((below, across, total, source_term))
+        below, across, total, source_term = lax.optimization_barrier((below, across, total, source_term))
         far_y = [move(below[:half], 0, -1), move(below[half:], 0, -1)]
         across_above = [move(across[:half], 0, 1), move(across[half:], 0, 1)]
         across_below = move(below, 1, 0)

time: 128 us -> 128 us (level)
  transfers between devices with their start and end apart: 36 -> 36, of which waited for: 14 -> 17; matrix products, arithmetic and copies ran while one was open for 0% -> 0% of each run, Pallas kernels for 16% -> 16%
where the time goes in v5:
time: 128 us
  starting transfers between devices  49.5 us (39%)
  waiting for transfers between devices  46.6 us (36%)
  Pallas kernels  23.9 us (19%)
  local copies, waits for them, and re-layouts  6.54 us (5%)
    ppermute x36, starting transfers between devices, permute(): return lax.ppermute(array, AXES, pairs)  49.5 us
    ppermute x36, waiting for transfers between devices, permute(): return lax.ppermute(array, AXES, pairs)  46.6 us
    pallas_call x12, Pallas kernels, stage(): pl.pallas_call(functools.partial(stage_kernel, shifts, layout, parity, be...  23.3 us
    unnamed x10, local copies, waits for them, and re-layouts  6.35 us
  transfers between devices with their start and end apart: 36, of which 17 were waited for; matrix products, arithmetic and copies ran while one was open for 0% of the time, Pallas kernels for 16%

profile of v5, /device:TPU:6, one launch (start us, length us, event | category | flops | bytes accessed | tf_op | source)
XLA Modules:
  0.0 127.7 jit_solution(14815540408137594230)
XLA Ops:
  0.0 3.0 %collective-permute-start = (bf16[384,512]{1,0:T(8,128)(2,1)}, bf16[384,512]{1,0:T(8,128)(2,1)S(1)}, u32[]{:S(2)}, u32[]{:S(2)}) collective-permute-start(bf16[384,512]{1,0:T(8,128)(2,1)} %bitcast.6), channel_id=1, source_target_pairs={{0,3},{1,0},{2,1},{3,2},{4,7},{5,4},{6,5},{7,6},{8,11},{9,8},{10,9... | collective-permute-start | bytes 1179656 | tf_op jit(solution)/shard_map/ppermute | solution.py:39
  6.2 3.7 %copy-done = bf16[1,4,384,3072]{3,2,1,0:T(8,128)(2,1)S(1)} copy-done((bf16[1,4,384,3072]{3,2,1,0:T(8,128)(2,1)S(1)}, bf16[1,4,384,3072]{3,2,1,0:T(8,128)(2,1)}, u32[]{:S(2)}) %copy-start) | copy-done | bytes 9437208
  14.7 2.1 %collective-permute-start.2 = (bf16[192,512]{1,0:T(8,128)(2,1)S(1)}, bf16[192,512]{1,0:T(8,128)(2,1)S(1)}, u32[]{:S(2)}, u32[]{:S(2)}) collective-permute-start(bf16[192,512]{1,0:T(8,128)(2,1)S(1)} %get-tuple-element.54), channel_id=1, source_target_pairs={{0,3},{1,0},{2,1},{3,2},{4,7},{5,4},{6,5},{7,6},{8,11},{9,8},{10,9... | collective-permute-start | bytes 589832 | tf_op jit(solution)/shard_map/ppermute | solution.py:39
  16.9 3.2 %collective-permute-start.6 = (bf16[192,512]{1,0:T(8,128)(2,1)S(1)}, bf16[192,512]{1,0:T(8,128)(2,1)S(1)}, u32[]{:S(2)}, u32[]{:S(2)}) collective-permute-start(bf16[192,512]{1,0:T(8,128)(2,1)S(1)} %get-tuple-element.53), channel_id=1, source_target_pairs={{0,3},{1,0},{2,1},{3,2},{4,7},{5,4},{6,5},{7,6},{8,11},{9,8},{10,9... | collective-permute-start | bytes 589832 | tf_op jit(solution)/shard_map/ppermute | solution.py:39
  20.2 2.1 %collective-permute-done.2.refs_0_ = bf16[192,512]{1,0:T(8,128)(2,1)S(1)} collective-permute-done((bf16[192,512]{1,0:T(8,128)(2,1)S(1)}, bf16[192,512]{1,0:T(8,128)(2,1)S(1)}, u32[]{:S(2)}, u32[]{:S(2)}) %collective-permute-start.2) | collective-permute-done | bytes 196640 | tf_op jit(solution)/shard_map/ppermute | solution.py:39
  23.2 2.5 %collective-permute-done.4.refs_3_ = bf16[192,512]{1,0:T(8,128)(2,1)S(1)} collective-permute-done((bf16[192,512]{1,0:T(8,128)(2,1)S(1)}, bf16[192,512]{1,0:T(8,128)(2,1)S(1)}, u32[]{:S(2)}, u32[]{:S(2)}) %collective-permute-start.4) | collective-permute-done | bytes 196640 | tf_op jit(solution)/shard_map/ppermute | solution.py:39
  25.8 2.6 %shard_map.48.refs_5_ = f32[384,512]{1,0:T(8,128)S(1)} custom-call(s32[2]{0:T(128)S(1)} %pad_add_fusion.where, bf16[1,4,384,3072]{3,2,1,0:T(8,128)(2,1)S(1)} %copy-done, bf16[384,512]{1,0:T(8,128)(2,1)S(1)} %collective-permute-done.refs_0_, bf16[384,512]{1,0:T(8,128)(2,1)S(1)} %collective-permute-done.1.refs_1_, ...), custom_call_target="tpu_custom_call" | custom-call | flops 1811939328 | bytes 4718592 | tf_op jit(solution)/shard_map/pallas_call | solution.py:110
  28.3 1.6 %collective-permute-done.7.refs_2_ = bf16[192,512]{1,0:T(8,128)(2,1)S(1)} collective-permute-done((bf16[192,512]{1,0:T(8,128)(2,1)S(1)}, bf16[192,512]{1,0:T(8,128)(2,1)S(1)}, u32[]{:S(2)}, u32[]{:S(2)}) %collective-permute-start.7) | collective-permute-done | bytes 196640 | tf_op jit(solution)/shard_map/ppermute | solution.py:39
  30.0 2.6 %shard_map.49.refs_2_ = f32[384,512]{1,0:T(8,128)S(1)} custom-call(s32[2]{0:T(128)S(1)} %pad_add_fusion.where, bf16[1,4,384,3072]{3,2,1,0:T(8,128)(2,1)S(1)} %copy-done, bf16[192,512]{1,0:T(8,128)(2,1)S(1)} %collective-permute-done.2.refs_0_, bf16[192,512]{1,0:T(8,128)(2,1)S(1)} %collective-permute-done.6.refs_1_, ...), custom_call_target="tpu_custom_call" | custom-call | flops 1811939328 | bytes 4718592 | tf_op jit(solution)/shard_map/pallas_call | solution.py:110
  34.1 8.7 %collective-permute-start.11 = (bf16[384,256]{1,0:T(8,128)(2,1)S(1)}, bf16[384,256]{1,0:T(8,128)(2,1)S(1)}, u32[]{:S(2)}, u32[]{:S(2)}) collective-permute-start(bf16[384,256]{1,0:T(8,128)(2,1)S(1)} %get-tuple-element.28), channel_id=1, source_target_pairs={{8,16},{9,17},{10,18},{11,19},{12,20},{13,21},{14,22},{15,23},{16,... | collective-permute-start | bytes 589832 | tf_op jit(solution)/shard_map/ppermute | solution.py:39
  42.8 3.4 %collective-permute-done.11 = bf16[384,256]{1,0:T(8,128)(2,1)S(1)} collective-permute-done((bf16[384,256]{1,0:T(8,128)(2,1)S(1)}, bf16[384,256]{1,0:T(8,128)(2,1)S(1)}, u32[]{:S(2)}, u32[]{:S(2)}) %collective-permute-start.11) | collective-permute-done | bytes 196640 | tf_op jit(solution)/shard_map/ppermute | solution.py:39
  46.2 1.8 %collective-permute-start.12 = (bf16[384,512]{1,0:T(8,128)(2,1)S(1)}, bf16[384,512]{1,0:T(8,128)(2,1)S(1)}, u32[]{:S(2)}, u32[]{:S(2)}) collective-permute-start(bf16[384,512]{1,0:T(8,128)(2,1)S(1)} %constant_dynamic-update-slice_fusion.refs_0_), channel_id=1, source_target_pairs={{0,3},{1,0},{2,1},{3,2},{4,7},{5,4},{6,5},{7,6},{8,11},{9,8},{10,9... | collective-permute-start | bytes 1179656 | tf_op jit(solution)/shard_map/ppermute | solution.py:39
  49.9 5.3 %collective-permute-done.12.refs_0_ = bf16[384,512]{1,0:T(8,128)(2,1)S(1)} collective-permute-done((bf16[384,512]{1,0:T(8,128)(2,1)S(1)}, bf16[384,512]{1,0:T(8,128)(2,1)S(1)}, u32[]{:S(2)}, u32[]{:S(2)}) %collective-permute-start.12) | collective-permute-done | bytes 393248 | tf_op jit(solution)/shard_map/ppermute | solution.py:39
  55.2 4.0 %collective-permute-done.13.refs_1_ = bf16[384,512]{1,0:T(8,128)(2,1)S(1)} collective-permute-done((bf16[384,512]{1,0:T(8,128)(2,1)S(1)}, bf16[384,512]{1,0:T(8,128)(2,1)S(1)}, u32[]{:S(2)}, u32[]{:S(2)}) %collective-permute-start.13) | collective-permute-done | bytes 393248 | tf_op jit(solution)/shard_map/ppermute | solution.py:39
  59.5 2.1 %collective-permute-start.16 = (bf16[192,512]{1,0:T(8,128)(2,1)S(1)}, bf16[192,512]{1,0:T(8,128)(2,1)S(1)}, u32[]{:S(2)}, u32[]{:S(2)}) collective-permute-start(bf16[192,512]{1,0:T(8,128)(2,1)S(1)} %get-tuple-element.48), channel_id=1, source_target_pairs={{0,1},{1,2},{2,3},{3,0},{4,5},{5,6},{6,7},{7,4},{8,9},{9,10},{10,1... | collective-permute-start | bytes 589832 | tf_op jit(solution)/shard_map/ppermute | solution.py:39
  65.1 1.9 %collective-permute-start.15 = (bf16[192,512]{1,0:T(8,128)(2,1)S(1)}, bf16[192,512]{1,0:T(8,128)(2,1)S(1)}, u32[]{:S(2)}, u32[]{:S(2)}) collective-permute-start(bf16[192,512]{1,0:T(8,128)(2,1)S(1)} %collective-permute-done.14.refs_0_), channel_id=1, source_target_pairs={{0,4},{1,5},{2,6},{3,7},{4,0},{5,1},{6,2},{7,3},{8,12},{9,13},{10,... | collective-permute-start | bytes 589832 | tf_op jit(solution)/shard_map/ppermute | solution.py:39
  67.2 2.6 %shard_map.52.refs_5_ = f32[384,512]{1,0:T(8,128)S(1)} custom-call(s32[2]{0:T(128)S(1)} %pad_add_fusion.where, bf16[1,4,384,3072]{3,2,1,0:T(8,128)(2,1)S(1)} %copy-done, bf16[384,512]{1,0:T(8,128)(2,1)S(1)} %collective-permute-done.12.refs_0_, bf16[384,512]{1,0:T(8,128)(2,1)S(1)} %collective-permute-done.13.refs_1_, ...), custom_call_target="tpu_custom_call" | custom-call | flops 1811939328 | bytes 4718592 | tf_op jit(solution)/shard_map/pallas_call | solution.py:110
  69.8 2.6 %shard_map.53.refs_2_ = f32[384,512]{1,0:T(8,128)S(1)} custom-call(s32[2]{0:T(128)S(1)} %pad_add_fusion.where, bf16[1,4,384,3072]{3,2,1,0:T(8,128)(2,1)S(1)} %copy-done, bf16[192,512]{1,0:T(8,128)(2,1)S(1)} %collective-permute-done.14.refs_0_, bf16[192,512]{1,0:T(8,128)(2,1)S(1)} %collective-permute-done.18.refs_1_, ...), custom_call_target="tpu_custom_call" | custom-call | flops 1811939328 | bytes 4718592 | tf_op jit(solution)/shard_map/pallas_call | solution.py:110
  75.4 5.2 %collective-permute-start.23 = (bf16[384,256]{1,0:T(8,128)(2,1)S(1)}, bf16[384,256]{1,0:T(8,128)(2,1)S(1)}, u32[]{:S(2)}, u32[]{:S(2)}) collective-permute-start(bf16[384,256]{1,0:T(8,128)(2,1)S(1)} %get-tuple-element.34), channel_id=1, source_target_pairs={{8,16},{9,17},{10,18},{11,19},{12,20},{13,21},{14,22},{15,23},{16,... | collective-permute-start | bytes 589832 | tf_op jit(solution)/shard_map/ppermute | solution.py:39
  80.6 5.5 %collective-permute-done.23 = bf16[384,256]{1,0:T(8,128)(2,1)S(1)} collective-permute-done((bf16[384,256]{1,0:T(8,128)(2,1)S(1)}, bf16[384,256]{1,0:T(8,128)(2,1)S(1)}, u32[]{:S(2)}, u32[]{:S(2)}) %collective-permute-start.23) | collective-permute-done | bytes 196640 | tf_op jit(solution)/shard_map/ppermute | solution.py:39
  86.1 1.6 %collective-permute-start.24 = (bf16[384,512]{1,0:T(8,128)(2,1)S(1)}, bf16[384,512]{1,0:T(8,128)(2,1)S(1)}, u32[]{:S(2)}, u32[]{:S(2)}) collective-permute-start(bf16[384,512]{1,0:T(8,128)(2,1)S(1)} %constant_dynamic-update-slice_fusion.2.refs_0_), channel_id=1, source_target_pairs={{0,3},{1,0},{2,1},{3,2},{4,7},{5,4},{6,5},{7,6},{8,11},{9,8},{10,9... | collective-permute-start | bytes 1179656 | tf_op jit(solution)/shard_map/ppermute | solution.py:39
  87.7 2.1 %collective-permute-start.25 = (bf16[384,512]{1,0:T(8,128)(2,1)S(1)}, bf16[384,512]{1,0:T(8,128)(2,1)S(1)}, u32[]{:S(2)}, u32[]{:S(2)}) collective-permute-start(bf16[384,512]{1,0:T(8,128)(2,1)S(1)} %constant_dynamic-update-slice_fusion.2.refs_0_), channel_id=1, source_target_pairs={{0,4},{1,5},{2,6},{3,7},{4,0},{5,1},{6,2},{7,3},{8,12},{9,13},{10,... | collective-permute-start | bytes 1179656 | tf_op jit(solution)/shard_map/ppermute | solution.py:39
  91.6 2.3 %collective-permute-done.24.refs_0_ = bf16[384,512]{1,0:T(8,128)(2,1)S(1)} collective-permute-done((bf16[384,512]{1,0:T(8,128)(2,1)S(1)}, bf16[384,512]{1,0:T(8,128)(2,1)S(1)}, u32[]{:S(2)}, u32[]{:S(2)}) %collective-permute-start.24) | collective-permute-done | bytes 393248 | tf_op jit(solution)/shard_map/ppermute | solution.py:39
  94.0 2.9 %collective-permute-done.25.refs_1_ = bf16[384,512]{1,0:T(8,128)(2,1)S(1)} collective-permute-done((bf16[384,512]{1,0:T(8,128)(2,1)S(1)}, bf16[384,512]{1,0:T(8,128)(2,1)S(1)}, u32[]{:S(2)}, u32[]{:S(2)}) %collective-permute-start.25) | collective-permute-done | bytes 393248 | tf_op jit(solution)/shard_map/ppermute | solution.py:39
  96.9 2.4 %collective-permute-start.32 = (bf16[384,512]{1,0:T(8,128)(2,1)S(1)}, bf16[384,512]{1,0:T(8,128)(2,1)S(1)}, u32[]{:S(2)}, u32[]{:S(2)}) collective-permute-start(bf16[384,512]{1,0:T(8,128)(2,1)S(1)} %collective-permute-done.24.refs_0_), channel_id=1, source_target_pairs={{0,4},{1,5},{2,6},{3,7},{4,0},{5,1},{6,2},{7,3},{8,12},{9,13},{10,... | collective-permute-start | bytes 1179656 | tf_op jit(solution)/shard_map/ppermute | solution.py:39
  99.3 2.1 %collective-permute-start.28 = (bf16[192,512]{1,0:T(8,128)(2,1)S(1)}, bf16[192,512]{1,0:T(8,128)(2,1)S(1)}, u32[]{:S(2)}, u32[]{:S(2)}) collective-permute-start(bf16[192,512]{1,0:T(8,128)(2,1)S(1)} %get-tuple-element.44), channel_id=1, source_target_pairs={{0,1},{1,2},{2,3},{3,0},{4,5},{5,6},{6,7},{7,4},{8,9},{9,10},{10,1... | collective-permute-start | bytes 589832 | tf_op jit(solution)/shard_map/ppermute | solution.py:39
  105.0 3.1 %collective-permute-done.28.refs_3_ = bf16[192,512]{1,0:T(8,128)(2,1)S(1)} collective-permute-done((bf16[192,512]{1,0:T(8,128)(2,1)S(1)}, bf16[192,512]{1,0:T(8,128)(2,1)S(1)}, u32[]{:S(2)}, u32[]{:S(2)}) %collective-permute-start.28) | collective-permute-done | bytes 196640 | tf_op jit(solution)/shard_map/ppermute | solution.py:39
  108.1 2.6 %shard_map.56.refs_5_ = f32[384,512]{1,0:T(8,128)S(1)} custom-call(s32[2]{0:T(128)S(1)} %pad_add_fusion.where, bf16[1,4,384,3072]{3,2,1,0:T(8,128)(2,1)S(1)} %copy-done, bf16[384,512]{1,0:T(8,128)(2,1)S(1)} %collective-permute-done.24.refs_0_, bf16[384,512]{1,0:T(8,128)(2,1)S(1)} %collective-permute-done.25.refs_1_, ...), custom_call_target="tpu_custom_call" | custom-call | flops 1811939328 | bytes 4718592 | tf_op jit(solution)/shard_map/pallas_call | solution.py:110
  110.7 2.6 %shard_map.57.refs_2_ = f32[384,512]{1,0:T(8,128)S(1)} custom-call(s32[2]{0:T(128)S(1)} %pad_add_fusion.where, bf16[1,4,384,3072]{3,2,1,0:T(8,128)(2,1)S(1)} %copy-done, bf16[192,512]{1,0:T(8,128)(2,1)S(1)} %collective-permute-done.26.refs_0_, bf16[192,512]{1,0:T(8,128)(2,1)S(1)} %collective-permute-done.30.refs_1_, ...), custom_call_target="tpu_custom_call" | custom-call | flops 1811939328 | bytes 4718592 | tf_op jit(solution)/shard_map/pallas_call | solution.py:110
  113.3 1.7 %collective-permute-done.29.refs_1_ = bf16[192,512]{1,0:T(8,128)(2,1)S(1)} collective-permute-done((bf16[192,512]{1,0:T(8,128)(2,1)S(1)}, bf16[192,512]{1,0:T(8,128)(2,1)S(1)}, u32[]{:S(2)}, u32[]{:S(2)}) %collective-permute-start.29) | collective-permute-done | bytes 196640 | tf_op jit(solution)/shard_map/ppermute | solution.py:39
  116.3 4.6 %collective-permute-start.34 = (bf16[384,256]{1,0:T(8,128)(2,1)S(1)}, bf16[384,256]{1,0:T(8,128)(2,1)S(1)}, u32[]{:S(2)}, u32[]{:S(2)}) collective-permute-start(bf16[384,256]{1,0:T(8,128)(2,1)S(1)} %get-tuple-element.39), channel_id=1, source_target_pairs={{8,16},{9,17},{10,18},{11,19},{12,20},{13,21},{14,22},{15,23},{16,... | collective-permute-start | bytes 589832 | tf_op jit(solution)/shard_map/ppermute | solution.py:39
  121.1 5.8 %collective-permute-done.34 = bf16[384,256]{1,0:T(8,128)(2,1)S(1)} collective-permute-done((bf16[384,256]{1,0:T(8,128)(2,1)S(1)}, bf16[384,256]{1,0:T(8,128)(2,1)S(1)}, u32[]{:S(2)}, u32[]{:S(2)}) %collective-permute-start.34) | collective-permute-done | bytes 196640 | tf_op jit(solution)/shard_map/ppermute | solution.py:39
  (74 shorter events, 27.2 us)
Async XLA Ops:
  0.0 12.2 %collective-permute-start = (bf16[384,512]{1,0:T(8,128)(2,1)}, bf16[384,512]{1,0:T(8,128)(2,1)S(1)}, u32[]{:S(2)}, u32[]{:S(2)}) collective-permute-start(bf16[384,512]{1,0:T(8,128)(2,1)} %bitcast.6), channel_id=1, source_target_pairs={{0,3},{1,0},{2,1},{3,2},{4,7},{5,4},{6,5},{7,6},{8,11},{9,8},{10,9... | collective-permute-start | bytes 1179656 | tf_op jit(solution)/shard_map/ppermute | solution.py:39
  3.0 10.8 %collective-permute-start.1 = (bf16[384,512]{1,0:T(8,128)(2,1)}, bf16[384,512]{1,0:T(8,128)(2,1)S(1)}, u32[]{:S(2)}, u32[]{:S(2)}) collective-permute-start(bf16[384,512]{1,0:T(8,128)(2,1)} %bitcast.7), channel_id=1, source_target_pairs={{0,4},{1,5},{2,6},{3,7},{4,0},{5,1},{6,2},{7,3},{8,12},{9,13},{10,... | collective-permute-start | bytes 1179656 | tf_op jit(solution)/shard_map/ppermute | solution.py:39
  3.8 16.3 %collective-permute-start.9 = (bf16[384,512]{1,0:T(8,128)(2,1)}, bf16[384,512]{1,0:T(8,128)(2,1)S(1)}, u32[]{:S(2)}, u32[]{:S(2)}) collective-permute-start(bf16[384,512]{1,0:T(8,128)(2,1)} %bitcast.8), channel_id=1, source_target_pairs={{0,1},{1,2},{2,3},{3,0},{4,5},{5,6},{6,7},{7,4},{8,9},{9,10},{10,1... | collective-permute-start | bytes 1179656 | tf_op jit(solution)/shard_map/ppermute | solution.py:39
  13.8 16.1 %collective-permute-start.8 = (bf16[384,512]{1,0:T(8,128)(2,1)S(1)}, bf16[384,512]{1,0:T(8,128)(2,1)S(1)}, u32[]{:S(2)}, u32[]{:S(2)}) collective-permute-start(bf16[384,512]{1,0:T(8,128)(2,1)S(1)} %collective-permute-done.refs_0_), channel_id=1, source_target_pairs={{0,4},{1,5},{2,6},{3,7},{4,0},{5,1},{6,2},{7,3},{8,12},{9,13},{10,... | collective-permute-start | bytes 1179656 | tf_op jit(solution)/shard_map/ppermute | solution.py:39
  14.7 7.5 %collective-permute-start.2 = (bf16[192,512]{1,0:T(8,128)(2,1)S(1)}, bf16[192,512]{1,0:T(8,128)(2,1)S(1)}, u32[]{:S(2)}, u32[]{:S(2)}) collective-permute-start(bf16[192,512]{1,0:T(8,128)(2,1)S(1)} %get-tuple-element.54), channel_id=1, source_target_pairs={{0,3},{1,0},{2,1},{3,2},{4,7},{5,4},{6,5},{7,6},{8,11},{9,8},{10,9... | collective-permute-start | bytes 589832 | tf_op jit(solution)/shard_map/ppermute | solution.py:39
  16.8 8.9 %collective-permute-start.4 = (bf16[192,512]{1,0:T(8,128)(2,1)S(1)}, bf16[192,512]{1,0:T(8,128)(2,1)S(1)}, u32[]{:S(2)}, u32[]{:S(2)}) collective-permute-start(bf16[192,512]{1,0:T(8,128)(2,1)S(1)} %get-tuple-element.52), channel_id=1, source_target_pairs={{0,1},{1,2},{2,3},{3,0},{4,5},{5,6},{6,7},{7,4},{8,9},{9,10},{10,1... | collective-permute-start | bytes 589832 | tf_op jit(solution)/shard_map/ppermute | solution.py:39
  16.9 11.4 %collective-permute-start.6 = (bf16[192,512]{1,0:T(8,128)(2,1)S(1)}, bf16[192,512]{1,0:T(8,128)(2,1)S(1)}, u32[]{:S(2)}, u32[]{:S(2)}) collective-permute-start(bf16[192,512]{1,0:T(8,128)(2,1)S(1)} %get-tuple-element.53), channel_id=1, source_target_pairs={{0,3},{1,0},{2,1},{3,2},{4,7},{5,4},{6,5},{7,6},{8,11},{9,8},{10,9... | collective-permute-start | bytes 589832 | tf_op jit(solution)/shard_map/ppermute | solution.py:39
  20.2 9.8 %collective-permute-start.7 = (bf16[192,512]{1,0:T(8,128)(2,1)S(1)}, bf16[192,512]{1,0:T(8,128)(2,1)S(1)}, u32[]{:S(2)}, u32[]{:S(2)}) collective-permute-start(bf16[192,512]{1,0:T(8,128)(2,1)S(1)} %get-tuple-element.51), channel_id=1, source_target_pairs={{0,1},{1,2},{2,3},{3,0},{4,5},{5,6},{6,7},{7,4},{8,9},{9,10},{10,1... | collective-permute-start | bytes 589832 | tf_op jit(solution)/shard_map/ppermute | solution.py:39
  22.2 10.3 %collective-permute-start.3 = (bf16[192,512]{1,0:T(8,128)(2,1)S(1)}, bf16[192,512]{1,0:T(8,128)(2,1)S(1)}, u32[]{:S(2)}, u32[]{:S(2)}) collective-permute-start(bf16[192,512]{1,0:T(8,128)(2,1)S(1)} %collective-permute-done.2.refs_0_), channel_id=1, source_target_pairs={{0,4},{1,5},{2,6},{3,7},{4,0},{5,1},{6,2},{7,3},{8,12},{9,13},{10,... | collective-permute-start | bytes 589832 | tf_op jit(solution)/shard_map/ppermute | solution.py:39
  25.8 6.9 %collective-permute-start.5 = (bf16[192,512]{1,0:T(8,128)(2,1)S(1)}, bf16[192,512]{1,0:T(8,128)(2,1)S(1)}, u32[]{:S(2)}, u32[]{:S(2)}) collective-permute-start(bf16[192,512]{1,0:T(8,128)(2,1)S(1)} %collective-permute-done.4.refs_3_), channel_id=1, source_target_pairs={{0,1},{1,2},{2,3},{3,0},{4,5},{5,6},{6,7},{7,4},{8,9},{9,10},{10,1... | collective-permute-start | bytes 589832 | tf_op jit(solution)/shard_map/ppermute | solution.py:39
  34.0 8.8 %collective-permute-start.10 = (bf16[384,256]{1,0:T(8,128)(2,1)S(1)}, bf16[384,256]{1,0:T(8,128)(2,1)S(1)}, u32[]{:S(2)}, u32[]{:S(2)}) collective-permute-start(bf16[384,256]{1,0:T(8,128)(2,1)S(1)} %get-tuple-element.27), channel_id=1, source_target_pairs={{0,8},{1,9},{2,10},{3,11},{4,12},{5,13},{6,14},{7,15},{8,0},{9,1},... | collective-permute-start | bytes 589832 | tf_op jit(solution)/shard_map/ppermute | solution.py:39
  34.1 12.1 %collective-permute-start.11 = (bf16[384,256]{1,0:T(8,128)(2,1)S(1)}, bf16[384,256]{1,0:T(8,128)(2,1)S(1)}, u32[]{:S(2)}, u32[]{:S(2)}) collective-permute-start(bf16[384,256]{1,0:T(8,128)(2,1)S(1)} %get-tuple-element.28), channel_id=1, source_target_pairs={{8,16},{9,17},{10,18},{11,19},{12,20},{13,21},{14,22},{15,23},{16,... | collective-permute-start | bytes 589832 | tf_op jit(solution)/shard_map/ppermute | solution.py:39
  46.2 9.0 %collective-permute-start.12 = (bf16[384,512]{1,0:T(8,128)(2,1)S(1)}, bf16[384,512]{1,0:T(8,128)(2,1)S(1)}, u32[]{:S(2)}, u32[]{:S(2)}) collective-permute-start(bf16[384,512]{1,0:T(8,128)(2,1)S(1)} %constant_dynamic-update-slice_fusion.refs_0_), channel_id=1, source_target_pairs={{0,3},{1,0},{2,1},{3,2},{4,7},{5,4},{6,5},{7,6},{8,11},{9,8},{10,9... | collective-permute-start | bytes 1179656 | tf_op jit(solution)/shard_map/ppermute | solution.py:39
  48.0 11.2 %collective-permute-start.13 = (bf16[384,512]{1,0:T(8,128)(2,1)S(1)}, bf16[384,512]{1,0:T(8,128)(2,1)S(1)}, u32[]{:S(2)}, u32[]{:S(2)}) collective-permute-start(bf16[384,512]{1,0:T(8,128)(2,1)S(1)} %constant_dynamic-update-slice_fusion.refs_0_), channel_id=1, source_target_pairs={{0,4},{1,5},{2,6},{3,7},{4,0},{5,1},{6,2},{7,3},{8,12},{9,13},{10,... | collective-permute-start | bytes 1179656 | tf_op jit(solution)/shard_map/ppermute | solution.py:39
  48.1 14.7 %collective-permute-start.21 = (bf16[384,512]{1,0:T(8,128)(2,1)S(1)}, bf16[384,512]{1,0:T(8,128)(2,1)S(1)}, u32[]{:S(2)}, u32[]{:S(2)}) collective-permute-start(bf16[384,512]{1,0:T(8,128)(2,1)S(1)} %constant_dynamic-update-slice_fusion.refs_0_), channel_id=1, source_target_pairs={{0,1},{1,2},{2,3},{3,0},{4,5},{5,6},{6,7},{7,4},{8,9},{9,10},{10,1... | collective-permute-start | bytes 1179656 | tf_op jit(solution)/shard_map/ppermute | solution.py:39
  59.3 10.6 %collective-permute-start.20 = (bf16[384,512]{1,0:T(8,128)(2,1)S(1)}, bf16[384,512]{1,0:T(8,128)(2,1)S(1)}, u32[]{:S(2)}, u32[]{:S(2)}) collective-permute-start(bf16[384,512]{1,0:T(8,128)(2,1)S(1)} %collective-permute-done.12.refs_0_), channel_id=1, source_target_pairs={{0,4},{1,5},{2,6},{3,7},{4,0},{5,1},{6,2},{7,3},{8,12},{9,13},{10,... | collective-permute-start | bytes 1179656 | tf_op jit(solution)/shard_map/ppermute | solution.py:39
  59.5 7.6 %collective-permute-start.16 = (bf16[192,512]{1,0:T(8,128)(2,1)S(1)}, bf16[192,512]{1,0:T(8,128)(2,1)S(1)}, u32[]{:S(2)}, u32[]{:S(2)}) collective-permute-start(bf16[192,512]{1,0:T(8,128)(2,1)S(1)} %get-tuple-element.48), channel_id=1, source_target_pairs={{0,1},{1,2},{2,3},{3,0},{4,5},{5,6},{6,7},{7,4},{8,9},{9,10},{10,1... | collective-permute-start | bytes 589832 | tf_op jit(solution)/shard_map/ppermute | solution.py:39
  61.6 8.2 %collective-permute-start.18 = (bf16[192,512]{1,0:T(8,128)(2,1)S(1)}, bf16[192,512]{1,0:T(8,128)(2,1)S(1)}, u32[]{:S(2)}, u32[]{:S(2)}) collective-permute-start(bf16[192,512]{1,0:T(8,128)(2,1)S(1)} %get-tuple-element.49), channel_id=1, source_target_pairs={{0,3},{1,0},{2,1},{3,2},{4,7},{5,4},{6,5},{7,6},{8,11},{9,8},{10,9... | collective-permute-start | bytes 589832 | tf_op jit(solution)/shard_map/ppermute | solution.py:39
  62.8 7.0 %collective-permute-start.19 = (bf16[192,512]{1,0:T(8,128)(2,1)S(1)}, bf16[192,512]{1,0:T(8,128)(2,1)S(1)}, u32[]{:S(2)}, u32[]{:S(2)}) collective-permute-start(bf16[192,512]{1,0:T(8,128)(2,1)S(1)} %get-tuple-element.47), channel_id=1, source_target_pairs={{0,1},{1,2},{2,3},{3,0},{4,5},{5,6},{6,7},{7,4},{8,9},{9,10},{10,1... | collective-permute-start | bytes 589832 | tf_op jit(solution)/shard_map/ppermute | solution.py:39
  65.1 7.3 %collective-permute-start.15 = (bf16[192,512]{1,0:T(8,128)(2,1)S(1)}, bf16[192,512]{1,0:T(8,128)(2,1)S(1)}, u32[]{:S(2)}, u32[]{:S(2)}) collective-permute-start(bf16[192,512]{1,0:T(8,128)(2,1)S(1)} %collective-permute-done.14.refs_0_), channel_id=1, source_target_pairs={{0,4},{1,5},{2,6},{3,7},{4,0},{5,1},{6,2},{7,3},{8,12},{9,13},{10,... | collective-permute-start | bytes 589832 | tf_op jit(solution)/shard_map/ppermute | solution.py:39
  67.1 6.9 %collective-permute-start.17 = (bf16[192,512]{1,0:T(8,128)(2,1)S(1)}, bf16[192,512]{1,0:T(8,128)(2,1)S(1)}, u32[]{:S(2)}, u32[]{:S(2)}) collective-permute-start(bf16[192,512]{1,0:T(8,128)(2,1)S(1)} %collective-permute-done.16.refs_3_), channel_id=1, source_target_pairs={{0,1},{1,2},{2,3},{3,0},{4,5},{5,6},{6,7},{7,4},{8,9},{9,10},{10,1... | collective-permute-start | bytes 589832 | tf_op jit(solution)/shard_map/ppermute | solution.py:39
  75.4 10.7 %collective-permute-start.23 = (bf16[384,256]{1,0:T(8,128)(2,1)S(1)}, bf16[384,256]{1,0:T(8,128)(2,1)S(1)}, u32[]{:S(2)}, u32[]{:S(2)}) collective-permute-start(bf16[384,256]{1,0:T(8,128)(2,1)S(1)} %get-tuple-element.34), channel_id=1, source_target_pairs={{8,16},{9,17},{10,18},{11,19},{12,20},{13,21},{14,22},{15,23},{16,... | collective-permute-start | bytes 589832 | tf_op jit(solution)/shard_map/ppermute | solution.py:39
  86.1 7.9 %collective-permute-start.24 = (bf16[384,512]{1,0:T(8,128)(2,1)S(1)}, bf16[384,512]{1,0:T(8,128)(2,1)S(1)}, u32[]{:S(2)}, u32[]{:S(2)}) collective-permute-start(bf16[384,512]{1,0:T(8,128)(2,1)S(1)} %constant_dynamic-update-slice_fusion.2.refs_0_), channel_id=1, source_target_pairs={{0,3},{1,0},{2,1},{3,2},{4,7},{5,4},{6,5},{7,6},{8,11},{9,8},{10,9... | collective-permute-start | bytes 1179656 | tf_op jit(solution)/shard_map/ppermute | solution.py:39
  87.7 9.1 %collective-permute-start.25 = (bf16[384,512]{1,0:T(8,128)(2,1)S(1)}, bf16[384,512]{1,0:T(8,128)(2,1)S(1)}, u32[]{:S(2)}, u32[]{:S(2)}) collective-permute-start(bf16[384,512]{1,0:T(8,128)(2,1)S(1)} %constant_dynamic-update-slice_fusion.2.refs_0_), channel_id=1, source_target_pairs={{0,4},{1,5},{2,6},{3,7},{4,0},{5,1},{6,2},{7,3},{8,12},{9,13},{10,... | collective-permute-start | bytes 1179656 | tf_op jit(solution)/shard_map/ppermute | solution.py:39
  89.8 12.8 %collective-permute-start.33 = (bf16[384,512]{1,0:T(8,128)(2,1)S(1)}, bf16[384,512]{1,0:T(8,128)(2,1)S(1)}, u32[]{:S(2)}, u32[]{:S(2)}) collective-permute-start(bf16[384,512]{1,0:T(8,128)(2,1)S(1)} %constant_dynamic-update-slice_fusion.2.refs_0_), channel_id=1, source_target_pairs={{0,1},{1,2},{2,3},{3,0},{4,5},{5,6},{6,7},{7,4},{8,9},{9,10},{10,1... | collective-permute-start | bytes 1179656 | tf_op jit(solution)/shard_map/ppermute | solution.py:39
  96.9 13.8 %collective-permute-start.32 = (bf16[384,512]{1,0:T(8,128)(2,1)S(1)}, bf16[384,512]{1,0:T(8,128)(2,1)S(1)}, u32[]{:S(2)}, u32[]{:S(2)}) collective-permute-start(bf16[384,512]{1,0:T(8,128)(2,1)S(1)} %collective-permute-done.24.refs_0_), channel_id=1, source_target_pairs={{0,4},{1,5},{2,6},{3,7},{4,0},{5,1},{6,2},{7,3},{8,12},{9,13},{10,... | collective-permute-start | bytes 1179656 | tf_op jit(solution)/shard_map/ppermute | solution.py:39
  99.3 8.8 %collective-permute-start.28 = (bf16[192,512]{1,0:T(8,128)(2,1)S(1)}, bf16[192,512]{1,0:T(8,128)(2,1)S(1)}, u32[]{:S(2)}, u32[]{:S(2)}) collective-permute-start(bf16[192,512]{1,0:T(8,128)(2,1)S(1)} %get-tuple-element.44), channel_id=1, source_target_pairs={{0,1},{1,2},{2,3},{3,0},{4,5},{5,6},{6,7},{7,4},{8,9},{9,10},{10,1... | collective-permute-start | bytes 589832 | tf_op jit(solution)/shard_map/ppermute | solution.py:39
  101.4 9.3 %collective-permute-start.30 = (bf16[192,512]{1,0:T(8,128)(2,1)S(1)}, bf16[192,512]{1,0:T(8,128)(2,1)S(1)}, u32[]{:S(2)}, u32[]{:S(2)}) collective-permute-start(bf16[192,512]{1,0:T(8,128)(2,1)S(1)} %get-tuple-element.45), channel_id=1, source_target_pairs={{0,3},{1,0},{2,1},{3,2},{4,7},{5,4},{6,5},{7,6},{8,11},{9,8},{10,9... | collective-permute-start | bytes 589832 | tf_op jit(solution)/shard_map/ppermute | solution.py:39
  102.6 8.1 %collective-permute-start.31 = (bf16[192,512]{1,0:T(8,128)(2,1)S(1)}, bf16[192,512]{1,0:T(8,128)(2,1)S(1)}, u32[]{:S(2)}, u32[]{:S(2)}) collective-permute-start(bf16[192,512]{1,0:T(8,128)(2,1)S(1)} %get-tuple-element.43), channel_id=1, source_target_pairs={{0,1},{1,2},{2,3},{3,0},{4,5},{5,6},{6,7},{7,4},{8,9},{9,10},{10,1... | collective-permute-start | bytes 589832 | tf_op jit(solution)/shard_map/ppermute | solution.py:39
  104.9 8.3 %collective-permute-start.27 = (bf16[192,512]{1,0:T(8,128)(2,1)S(1)}, bf16[192,512]{1,0:T(8,128)(2,1)S(1)}, u32[]{:S(2)}, u32[]{:S(2)}) collective-permute-start(bf16[192,512]{1,0:T(8,128)(2,1)S(1)} %collective-permute-done.26.refs_0_), channel_id=1, source_target_pairs={{0,4},{1,5},{2,6},{3,7},{4,0},{5,1},{6,2},{7,3},{8,12},{9,13},{10,... | collective-permute-start | bytes 589832 | tf_op jit(solution)/shard_map/ppermute | solution.py:39
  108.1 6.9 %collective-permute-start.29 = (bf16[192,512]{1,0:T(8,128)(2,1)S(1)}, bf16[192,512]{1,0:T(8,128)(2,1)S(1)}, u32[]{:S(2)}, u32[]{:S(2)}) collective-permute-start(bf16[192,512]{1,0:T(8,128)(2,1)S(1)} %collective-permute-done.28.refs_3_), channel_id=1, source_target_pairs={{0,1},{1,2},{2,3},{3,0},{4,5},{5,6},{6,7},{7,4},{8,9},{9,10},{10,1... | collective-permute-start | bytes 589832 | tf_op jit(solution)/shard_map/ppermute | solution.py:39
  116.3 10.6 %collective-permute-start.34 = (bf16[384,256]{1,0:T(8,128)(2,1)S(1)}, bf16[384,256]{1,0:T(8,128)(2,1)S(1)}, u32[]{:S(2)}, u32[]{:S(2)}) collective-permute-start(bf16[384,256]{1,0:T(8,128)(2,1)S(1)} %get-tuple-element.39), channel_id=1, source_target_pairs={{8,16},{9,17},{10,18},{11,19},{12,20},{13,21},{14,22},{15,23},{16,... | collective-permute-start | bytes 589832 | tf_op jit(solution)/shard_map/ppermute | solution.py:39
  (8 other events, 29.0 us)
